TPU v7x, 32 devices: a whole 2x2x4 slice. The times are simulated.
32 devices in a mesh: dp: 8 (over z, x), chan: 4 (over y, core).
Axes of the slice: x: 2, y: 2, z: 4, core: 2. Of those that a mesh axis runs over, the one named last changes fastest.
Arguments:
- audio_clips: float32 [8, 8, 2304], P('dp'), may hold values from -6 to 6
- mel_frames: bfloat16 [8, 80, 72], P('dp'), may hold values from -6 to 6
- crop_offsets: int32 [8], P('dp'), may hold values from 0 to 8
- inv_weight: float32 [8, 8], replicated, may hold values from -0.11 to 1.2, as said below
- initial_projection_weight: float32 [512, 4], P('chan'), may hold values from -3 to 3
- start_bias: float32 [512], P('chan'), may hold values from -3 to 3
- cond_weight: bfloat16 [8, 2, 512, 80], P(None, None, 'chan'), may hold values from -0.625 to 0.625
- in_weight: bfloat16 [8, 2, 512, 1536], P(None, None, 'chan'), may hold values from -0.15625 to 0.15625
- in_bias: float32 [8, 2, 512], P(None, None, 'chan'), may hold values from -3 to 3
- res_weight: bfloat16 [7, 512, 512], P(None, None, 'chan'), may hold values from -0.25 to 0.25
- res_bias: float32 [7, 512], P(None, 'chan'), may hold values from -2 to 2
- skip_projection_weight: bfloat16 [8, 512, 512], P(None, None, 'chan'), may hold values from -0.25 to 0.25
- skip_output_bias: float32 [512], P('chan'), may hold values from -3 to 3
- final_projection_weight: float32 [8, 512], P(None, 'chan'), may hold values from -0.09375 to 0.09375
- end_bias: float32 [8], replicated, may hold values from -1.5 to 1.5
Outputs:
- latent: float32 [8, 8, 2048], P('dp')
- log_det: float32 [8], P('dp')
- crop_loss: float32 [8], P('dp')
- audio_grad: float32 [8, 8, 2048], P('dp')
- mel_grad: float32 [8, 80, 64], P('dp')
- inv_grad: float32 [8, 8], replicated
- initial_projection_gradient: float32 [512, 4], P('chan')
- start_bias_grad: float32 [512], P('chan')
- cond_grad: float32 [8, 2, 512, 80], P(None, None, 'chan')
- in_grad: float32 [8, 2, 512, 1536], P(None, None, 'chan')
- in_bias_grad: float32 [8, 2, 512], P(None, None, 'chan')
- res_grad: float32 [7, 512, 512], P(None, None, 'chan')
- res_bias_grad: float32 [7, 512], P(None, 'chan')
- skip_grad: float32 [8, 512, 512], P(None, None, 'chan')
- skip_bias_grad: float32 [512], P('chan')
- end_grad: float32 [8, 512], P(None, 'chan')
- end_bias_grad: float32 [8], replicated
Inputs may be any that keep to these rules, and one draw needn't show every extreme that they name: `inv_weight`: each row's diagonal entry is positive and exceeds the sum of the magnitudes of the row's other entries.
All inputs are finite; a program needn't handle non-finite values.
Results may differ from a plain program's by a relative error of at most 0.025.
Values may be sent and summed in bfloat16 or wider, within the bound.
A program may use at most 256 MiB of HBM per device.

v0:
```python
import jax
import jax.numpy as jnp
from jax import lax
from jax.sharding import PartitionSpec as P

CH = 8
MEL = 80
LAYERS = 8
HOP = 32
FRAMES = 2048


UPPER_LIMIT = lax.Precision.HIGHEST


def offset_frames(values, amount):
    if amount == 0:
        return values
    frame_count = values.shape[-1]
    filler = jnp.zeros(values.shape[:-1] + (abs(amount),), values.dtype)
    if amount > 0:
        return jnp.concatenate([values[..., amount:], filler], axis=-1)
    return jnp.concatenate([filler, values[..., : frame_count + amount]], axis=-1)


def upsample(values):
    spread = jnp.broadcast_to(values[..., None], values.shape + (HOP,))
    return spread.reshape(values.shape[:-1] + (values.shape[-1] * HOP,))


def invert_small(matrix):
    size_of = matrix.shape[0]
    augmented = jnp.concatenate([matrix, jnp.eye(size_of, dtype=jnp.float32)], axis=1)
    log_total = jnp.float32(0.0)
    for column in range(size_of):
        pivot = augmented[column, column]
        log_total = log_total + jnp.log(pivot)
        pivot_row = augmented[column] / pivot
        factor = augmented[:, column]
        augmented = augmented - factor[:, None] * pivot_row[None, :]
        augmented = augmented.at[column].set(pivot_row)
    return (augmented[:, size_of:], log_total)


def conv_rows(filter_weight_values, dilation, running, row_block_count):
    for filter_position in range(3):
        running = running + jnp.einsum(
            "jw,wpd->jpd",
            filter_weight_values[:, filter_position],
            offset_frames(row_block_count, (filter_position - 1) * dilation),
            preferred_element_type=jnp.float32,
        )
    return running


def res_skip_terms(residual_row_values, skip_row_values, gate_activation):
    return jnp.stack(
        [
            jnp.einsum(
                "jw,wpd->jpd",
                residual_row_values,
                gate_activation,
                preferred_element_type=jnp.float32,
            ),
            jnp.einsum(
                "jw,wpd->jpd", skip_row_values, gate_activation, preferred_element_type=jnp.float32
            ),
        ],
        axis=1,
    )


def single_terms(weight_row_values, gate_activation):
    return jnp.einsum(
        "jw,wpd->jpd", weight_row_values, gate_activation, preferred_element_type=jnp.float32
    )


def res_back(residual_row_values, gate_activation, carry, row_block_count):
    gated_back, grad_rows = carry
    gated_back = gated_back + jnp.einsum(
        "pr,pes->res", residual_row_values, row_block_count, preferred_element_type=jnp.float32
    )
    gradient_portion = jnp.einsum(
        "ers,lrs->el", row_block_count, gate_activation, preferred_element_type=jnp.float32
    )
    grad_rows = gradient_portion
    return (gated_back, grad_rows)


def weight_columns(flattened_gradient, dilation, row_block_count):
    pieces = [
        jnp.einsum(
            "ers,lrs->el",
            flattened_gradient,
            offset_frames(row_block_count, (filter_position - 1) * dilation),
            preferred_element_type=jnp.float32,
        )
        for filter_position in range(3)
    ]
    return jnp.stack(pieces, axis=1)


def input_rows(filter_weight_values, flattened_gradient, dilation, row_count):
    running = jnp.zeros((row_count,) + flattened_gradient.shape[1:], jnp.float32)
    for filter_position in range(3):
        term = jnp.einsum(
            "pr,pes->res",
            filter_weight_values[:, filter_position],
            flattened_gradient,
            preferred_element_type=jnp.float32,
        )
        running = running + offset_frames(term, -(filter_position - 1) * dilation)
    return running


def local(
    audio_clips,
    mel_frames,
    crop_offsets,
    inv_weight,
    initial_projection_weight,
    start_bias,
    cond_weight,
    in_weight,
    in_bias,
    res_weight,
    res_bias,
    skip_projection_weight,
    skip_output_bias,
    final_projection_weight,
    end_bias,
):
    crop_count = audio_clips.shape[0]
    shard_rows = initial_projection_weight.shape[0]
    full_width = res_weight.shape[1]
    half_group = CH // 2
    mel_count = FRAMES // HOP

    def crop_one(clip, mel_clip, offset):
        return (
            lax.dynamic_slice_in_dim(clip, offset * HOP, FRAMES, 1),
            lax.dynamic_slice_in_dim(mel_clip, offset, mel_count, 1),
        )

    crop_audio, crop_mel = jax.vmap(crop_one)(audio_clips, mel_frames, crop_offsets)
    mixed_input = jnp.einsum("ij,bjf->ibf", inv_weight, crop_audio, precision=UPPER_LIMIT)
    leading_half_channels = mixed_input[:half_group]
    second_half = mixed_input[half_group:]
    hidden = (
        jnp.einsum(
            "ry,yoe->roe", initial_projection_weight, leading_half_channels, precision=UPPER_LIMIT
        )
        + start_bias[:, None, None]
    )
    kept_hidden = []
    kept_preact = []
    skip_output_total = jnp.zeros((shard_rows, crop_count, FRAMES), jnp.float32)
    for layer_position in range(LAYERS):
        dilation = 2**layer_position
        rounded = hidden.astype(jnp.bfloat16)
        filter_weight_values = in_weight[layer_position].reshape(2 * shard_rows, 3, full_width)
        preact = conv_rows(
            filter_weight_values,
            dilation,
            jnp.zeros((2 * shard_rows, crop_count, FRAMES), jnp.float32),
            lax.all_gather(rounded, "chan", axis=0, tiled=True),
        )
        cond_small = jnp.einsum(
            "gcm,bmr->gcbr",
            cond_weight[layer_position],
            crop_mel,
            preferred_element_type=jnp.float32,
        )
        preact = (
            preact.reshape(2, shard_rows, crop_count, FRAMES)
            + in_bias[layer_position][:, :, None, None]
            + upsample(cond_small)
        )
        kept_hidden.append(rounded)
        kept_preact.append(preact)
        gate_activation = (jnp.tanh(preact[0]) * jax.nn.sigmoid(preact[1])).astype(jnp.bfloat16)
        if layer_position < LAYERS - 1:
            summed = lax.psum_scatter(
                res_skip_terms(
                    res_weight[layer_position],
                    skip_projection_weight[layer_position],
                    gate_activation,
                ),
                "chan",
                scatter_dimension=0,
                tiled=True,
            )
            hidden = hidden + summed[:, 0] + res_bias[layer_position][:, None, None]
            skip_output_total = skip_output_total + summed[:, 1]
        else:
            skip_output_total = skip_output_total + lax.psum_scatter(
                single_terms(skip_projection_weight[layer_position], gate_activation).astype(
                    jnp.bfloat16
                ),
                "chan",
                scatter_dimension=0,
                tiled=True,
            ).astype(jnp.float32)
    local_out = jnp.einsum(
        "ku,utx->ktx",
        final_projection_weight,
        skip_output_total + skip_output_bias[:, None, None],
        precision=UPPER_LIMIT,
    )
    output = (
        lax.psum(local_out.astype(jnp.bfloat16), "chan").astype(jnp.float32)
        + end_bias[:, None, None]
    )
    log_scale = output[:half_group]
    shift_term = output[half_group:]
    scale_term = jnp.exp(log_scale)
    second_out = scale_term * second_half + shift_term
    latent = jnp.concatenate([leading_half_channels, second_out], axis=0)
    inverse, log_abs = invert_small(inv_weight)
    log_det = jnp.sum(log_scale, axis=(0, 2)) + FRAMES * log_abs
    crop_loss = (0.5 * jnp.sum(latent * latent, axis=(0, 2)) - log_det) / (CH * FRAMES)
    scale_grad = second_out * scale_term * second_half - 1.0
    output_gradient = jnp.concatenate([scale_grad, second_out], axis=0)
    end_bias_grad = jnp.sum(output_gradient, axis=(1, 2))
    skip_backward_term = jnp.einsum(
        "kh,kyp->hyp", final_projection_weight, output_gradient, precision=UPPER_LIMIT
    )
    skip_bias_grad = jnp.sum(skip_backward_term, axis=(1, 2))
    end_grad = jnp.einsum(
        "egs,ngs->en",
        output_gradient,
        skip_output_total + skip_output_bias[:, None, None],
        precision=UPPER_LIMIT,
    )
    skip_lower_portion = lax.all_gather(
        skip_backward_term.astype(jnp.bfloat16), "chan", axis=0, tiled=True
    )
    mel_part = jnp.zeros((crop_count, MEL, mel_count), jnp.float32)
    cond_grads = []
    in_grads = []
    in_bias_grads = []
    res_grads = []
    res_bias_grads = []
    skip_grads = []
    hidden_state_gradient = None
    for layer_position in range(LAYERS - 1, -1, -1):
        dilation = 2**layer_position
        preact = kept_preact[layer_position]
        tanh_part = jnp.tanh(preact[0])
        sig_part = jax.nn.sigmoid(preact[1])
        gate_activation = (tanh_part * sig_part).astype(jnp.bfloat16)
        skip_grads.append(
            jnp.einsum(
                "ers,lrs->el",
                skip_lower_portion,
                gate_activation,
                preferred_element_type=jnp.float32,
            )
        )
        gated_back = jnp.einsum(
            "pr,pes->res",
            skip_projection_weight[layer_position],
            skip_lower_portion,
            preferred_element_type=jnp.float32,
        )
        if layer_position < LAYERS - 1:
            grad_low = hidden_state_gradient.astype(jnp.bfloat16)
            res_bias_grads.append(jnp.sum(grad_low, axis=(1, 2), dtype=jnp.float32))
            gated_back, residual_row_values = res_back(
                res_weight[layer_position],
                gate_activation,
                (gated_back, jnp.zeros((full_width, shard_rows), jnp.float32)),
                lax.all_gather(grad_low, "chan", axis=0, tiled=True),
            )
            res_grads.append(residual_row_values)
        tanh_grad = gated_back * sig_part * (1.0 - tanh_part * tanh_part)
        sig_grad = gated_back * tanh_part * sig_part * (1.0 - sig_part)
        preact_low = jnp.stack([tanh_grad, sig_grad]).astype(jnp.bfloat16)
        in_bias_grads.append(jnp.sum(preact_low, axis=(2, 3), dtype=jnp.float32))
        folded = jnp.sum(
            preact_low.reshape(2, shard_rows, crop_count, mel_count, HOP),
            axis=-1,
            dtype=jnp.float32,
        )
        cond_grads.append(
            jnp.einsum("gcbr,bmr->gcm", folded, crop_mel.astype(jnp.float32), precision=UPPER_LIMIT)
        )
        mel_part = mel_part + jnp.einsum(
            "gcm,gcbr->bmr",
            cond_weight[layer_position].astype(jnp.float32),
            folded,
            precision=UPPER_LIMIT,
        )
        flattened_gradient = preact_low.reshape(2 * shard_rows, crop_count, FRAMES)
        weight_grad = weight_columns(
            flattened_gradient,
            dilation,
            lax.all_gather(kept_hidden[layer_position], "chan", axis=0, tiled=True),
        )
        in_grads.append(weight_grad.reshape(2, shard_rows, 3 * full_width))
        filter_weight_values = in_weight[layer_position].reshape(2 * shard_rows, 3, full_width)
        input_part = lax.psum_scatter(
            input_rows(
                filter_weight_values,
                flattened_gradient,
                dilation,
                shard_rows * lax.axis_size("chan"),
            ).astype(jnp.bfloat16),
            "chan",
            scatter_dimension=0,
            tiled=True,
        ).astype(jnp.float32)
        hidden_state_gradient = (
            input_part if hidden_state_gradient is None else hidden_state_gradient + input_part
        )
    start_bias_grad = jnp.sum(hidden_state_gradient, axis=(1, 2))
    initial_projection_gradient = jnp.einsum(
        "lyo,eyo->le", hidden_state_gradient, leading_half_channels, precision=UPPER_LIMIT
    )
    leading_portion = jnp.einsum(
        "ks,khm->shm", initial_projection_weight, hidden_state_gradient, precision=UPPER_LIMIT
    )
    first_back, mel_grad = (
        lax.psum(leading_portion.astype(jnp.bfloat16), "chan").astype(jnp.float32),
        lax.psum(mel_part.astype(jnp.bfloat16), "chan").astype(jnp.float32),
    )
    mixed_grad = jnp.concatenate(
        [leading_half_channels + first_back, second_out * scale_term], axis=0
    )
    audio_grad = jnp.einsum("ij,ibf->bjf", inv_weight, mixed_grad, precision=UPPER_LIMIT)
    inv_grad = (
        jnp.einsum("ibf,bjf->ij", mixed_grad, crop_audio, precision=UPPER_LIMIT)
        - crop_count * FRAMES * inverse.T
    )
    (
        inv_grad,
        initial_projection_gradient,
        start_bias_grad,
        cond_grad,
        in_grad,
        in_bias_grad,
        res_grad,
        res_bias_grad,
        skip_grad,
        skip_bias_grad,
        end_grad,
        end_bias_grad,
    ) = lax.psum(
        (
            inv_grad,
            initial_projection_gradient,
            start_bias_grad,
            jnp.stack(cond_grads[::-1]),
            jnp.stack(in_grads[::-1]),
            jnp.stack(in_bias_grads[::-1]),
            jnp.stack(res_grads[::-1]),
            jnp.stack(res_bias_grads[::-1]),
            jnp.stack(skip_grads[::-1]),
            skip_bias_grad,
            end_grad,
            end_bias_grad,
        ),
        "dp",
    )
    return (
        jnp.moveaxis(latent, 0, 1),
        log_det,
        crop_loss,
        audio_grad,
        mel_grad,
        inv_grad,
        initial_projection_gradient,
        start_bias_grad,
        cond_grad,
        in_grad,
        in_bias_grad,
        res_grad,
        res_bias_grad,
        skip_grad,
        skip_bias_grad,
        end_grad,
        end_bias_grad,
    )


def solution(mesh):
    in_specs = (
        P("dp", None, None),
        P("dp", None, None),
        P("dp"),
        P(),
        P("chan", None),
        P("chan"),
        P(None, None, "chan", None),
        P(None, None, "chan", None),
        P(None, None, "chan"),
        P(None, None, "chan"),
        P(None, "chan"),
        P(None, None, "chan"),
        P("chan"),
        P(None, "chan"),
        P(),
    )
    out_specs = (
        P("dp", None, None),
        P("dp"),
        P("dp"),
        P("dp", None, None),
        P("dp", None, None),
        P(),
        P("chan", None),
        P("chan"),
        P(None, None, "chan", None),
        P(None, None, "chan", None),
        P(None, None, "chan"),
        P(None, None, "chan"),
        P(None, "chan"),
        P(None, None, "chan"),
        P("chan"),
        P(None, "chan"),
        P(),
    )
    return jax.shard_map(local, mesh=mesh, in_specs=in_specs, out_specs=out_specs, check_vma=False)
```

profile of v0, /device:TPU:0, one launch (start us, length us, event | category | flops | bytes accessed | tf_op | source)
XLA Modules:
  0.0 2153.9 jit_solution(15395347981967468615)
XLA Ops:
  21.5 16.5 all-gather.40.cloned.1.call-done
  58.2 71.2 %reduce-scatter.35.cloned.1.call-done = f32[128,2,1,2048]{0,3,2,1:T(8,128)} async-done(((f32[512,2,1,2048]{0,3,2,1:T(8,128)}), f32[128,2,1,2048]{0,3,2,1:T(8,128)}) %reduce-scatter.35.cloned.1.call-update) | async-done | bytes 2097168 | tf_op jit(solution)/shard_map/reduce_scatter | solution.py:184
  134.0 20.6 all-gather.42.cloned.1.call-done
  174.2 71.8 %reduce-scatter.37.cloned.1.call-done = f32[128,2,1,2048]{0,3,2,1:T(8,128)} async-done(((f32[512,2,1,2048]{0,3,2,1:T(8,128)}), f32[128,2,1,2048]{0,3,2,1:T(8,128)}) %reduce-scatter.37.cloned.1.call-update) | async-done | bytes 2097168 | tf_op jit(solution)/shard_map/reduce_scatter | solution.py:184
  252.0 19.8 all-gather.44.cloned.1.call-done
  291.3 71.8 %reduce-scatter.39.cloned.1.call-done = f32[128,2,1,2048]{0,3,2,1:T(8,128)} async-done(((f32[512,2,1,2048]{0,3,2,1:T(8,128)}), f32[128,2,1,2048]{0,3,2,1:T(8,128)}) %reduce-scatter.39.cloned.1.call-update) | async-done | bytes 2097168 | tf_op jit(solution)/shard_map/reduce_scatter | solution.py:184
  368.8 19.6 all-gather.46.cloned.1.call-done
  407.6 71.8 %reduce-scatter.41.cloned.1.call-done = f32[128,2,1,2048]{0,3,2,1:T(8,128)} async-done(((f32[512,2,1,2048]{0,3,2,1:T(8,128)}), f32[128,2,1,2048]{0,3,2,1:T(8,128)}) %reduce-scatter.41.cloned.1.call-update) | async-done | bytes 2097168 | tf_op jit(solution)/shard_map/reduce_scatter | solution.py:184
  486.0 19.1 all-gather.48.cloned.1.call-done
  524.4 71.8 %reduce-scatter.43.cloned.1.call-done = f32[128,2,1,2048]{0,3,2,1:T(8,128)} async-done(((f32[512,2,1,2048]{0,3,2,1:T(8,128)}), f32[128,2,1,2048]{0,3,2,1:T(8,128)}) %reduce-scatter.43.cloned.1.call-update) | async-done | bytes 2097168 | tf_op jit(solution)/shard_map/reduce_scatter | solution.py:184
  601.6 19.8 all-gather.50.cloned.1.call-done
  640.6 71.8 %reduce-scatter.45.cloned.1.call-done = f32[128,2,1,2048]{0,3,2,1:T(8,128)} async-done(((f32[512,2,1,2048]{0,3,2,1:T(8,128)}), f32[128,2,1,2048]{0,3,2,1:T(8,128)}) %reduce-scatter.45.cloned.1.call-update) | async-done | bytes 2097168 | tf_op jit(solution)/shard_map/reduce_scatter | solution.py:184
  719.1 19.0 all-gather.52.cloned.1.call-done
  757.1 71.8 %reduce-scatter.47.cloned.1.call-done = f32[128,2,1,2048]{0,3,2,1:T(8,128)} async-done(((f32[512,2,1,2048]{0,3,2,1:T(8,128)}), f32[128,2,1,2048]{0,3,2,1:T(8,128)}) %reduce-scatter.47.cloned.1.call-update) | async-done | bytes 2097168 | tf_op jit(solution)/shard_map/reduce_scatter | solution.py:184
  833.3 20.9 all-gather.54.cloned.1.call-done
  873.6 31.1 %reduce-scatter.49.cloned.1.call-done = bf16[128,2048]{1,0:T(8,128)(2,1)} async-done(((bf16[512,2048]{1,0:T(8,128)(2,1)}), bf16[128,2048]{1,0:T(8,128)(2,1)}) %reduce-scatter.49.cloned.1.call-update) | async-done | bytes 524304
  925.4 24.1 %all-gather.56.cloned.1.call-done = bf16[512,2048]{0,1:T(8,128)(2,1)} async-done(((bf16[128,2048]{0,1:T(8,128)(2,1)}), bf16[512,2048]{0,1:T(8,128)(2,1)}) %all-gather.56.cloned.1.call-update) | async-done | bytes 2097168 | tf_op jit(solution)/shard_map/all_gather | solution.py:236
  966.3 31.5 %reduce-scatter.51.cloned.1.call-done = bf16[128,2048]{1,0:T(8,128)(2,1)} async-done(((bf16[512,2048]{1,0:T(8,128)(2,1)}), bf16[128,2048]{1,0:T(8,128)(2,1)}) %reduce-scatter.51.cloned.1.call-update) | async-done | bytes 524304
  1001.8 21.2 all-gather.26.cloned.1.call-done
  1041.7 31.5 %reduce-scatter.53.cloned.1.call-done = bf16[128,2048]{1,0:T(8,128)(2,1)} async-done(((bf16[512,2048]{1,0:T(8,128)(2,1)}), bf16[128,2048]{1,0:T(8,128)(2,1)}) %reduce-scatter.53.cloned.1.call-update) | async-done | bytes 524304
  1078.9 20.4 all-gather.28.cloned.1.call-done
  1118.2 31.5 %reduce-scatter.55.cloned.1.call-done = bf16[128,2048]{1,0:T(8,128)(2,1)} async-done(((bf16[512,2048]{1,0:T(8,128)(2,1)}), bf16[128,2048]{1,0:T(8,128)(2,1)}) %reduce-scatter.55.cloned.1.call-update) | async-done | bytes 524304
  1157.8 20.0 all-gather.30.cloned.1.call-done
  1197.9 31.5 %reduce-scatter.57.cloned.1.call-done = bf16[128,2048]{1,0:T(8,128)(2,1)} async-done(((bf16[512,2048]{1,0:T(8,128)(2,1)}), bf16[128,2048]{1,0:T(8,128)(2,1)}) %reduce-scatter.57.cloned.1.call-update) | async-done | bytes 524304
  1237.2 20.3 all-gather.32.cloned.1.call-done
  1277.7 31.5 %reduce-scatter.59.cloned.1.call-done = bf16[128,2048]{1,0:T(8,128)(2,1)} async-done(((bf16[512,2048]{1,0:T(8,128)(2,1)}), bf16[128,2048]{1,0:T(8,128)(2,1)}) %reduce-scatter.59.cloned.1.call-update) | async-done | bytes 524304
  1317.8 20.2 all-gather.34.cloned.1.call-done
  1355.4 31.5 %reduce-scatter.61.cloned.1.call-done = bf16[128,2048]{1,0:T(8,128)(2,1)} async-done(((bf16[512,2048]{1,0:T(8,128)(2,1)}), bf16[128,2048]{1,0:T(8,128)(2,1)}) %reduce-scatter.61.cloned.1.call-update) | async-done | bytes 524304
  1651.4 11.7 all-reduce.34
  1664.8 39.5 %all-reduce.32 = (f32[8,8]{1,0:T(8,128)}, f32[128,4]{0,1:T(4,128)}, f32[128]{0:T(128)}, f32[8,2,128]{2,1,0:T(2,128)}, f32[7,128]{1,0:T(8,128)}, /*index=5*/f32[128]{0:T(128)}, f32[8,128]{1,0:T(8,128)}, f32[8]{0:T(128)}) all-reduce(f32[8,8]{1,0:T(8,128)S(1)} %convolution_subtract_fusion, ...), channel_id=1, replica_groups=mesh['dp'=8,'chan'=4] {'dp'}, use_global_device_ids=true, to_apply=%region_29.0 | all-reduce | flops 4808 | bytes 38464 | tf_op jit(solution)/shard_map/psum | solution.py:349
  1705.2 414.9 %all-reduce.37.cloned.1.call-done = (f32[8,2,128,80]{2,3,1,0:T(8,128)}, f32[8,2,128,1536]{2,1,3,0:T(2,128)}, f32[7,512,128]{2,1,0:T(8,128)}, f32[8,512,128]{2,1,0:T(8,128)}) async-done(((f32[8,2,128,80]{2,3,1,0:T(8,128)}, f32[8,2,128,1536]{2,1,3,0:T(2,128)}, f32[7,512,128]{2,1,0:T(8,128)}, f32[8,512,128]{2,1,0:T(8,128)}), (f32[8,2,128,80]{2,3,1,0:T(8,128)}, f32[8,2,128,1536]{2,1,3,0:T(2,128)}, ...) | async-done | bytes 17170448 | tf_op jit(solution)/shard_map/psum | solution.py:349
  2120.1 19.1 copy.156
  (918 shorter events, 637.0 us)
Async XLA Ops:
  12.4 117.0 %reduce-scatter.35.cloned.1.call-start = ((), (), s32[]{:S(2)}) async-start(), calls=%async_computation.16 | async-start | bytes 10485760 | tf_op jit(solution)/shard_map/reduce_scatter | solution.py:184
  57.5 97.1 %all-gather.42.cloned.1.call-start = ((), (), s32[]{:S(2)}) async-start(), calls=%async_computation.31 | async-start | bytes 2621440 | tf_op jit(solution)/shard_map/all_gather | solution.py:167
  131.7 114.4 %reduce-scatter.37.cloned.1.call-start = ((), (), s32[]{:S(2)}) async-start(), calls=%async_computation.17 | async-start | bytes 10485760 | tf_op jit(solution)/shard_map/reduce_scatter | solution.py:184
  174.2 97.6 %all-gather.44.cloned.1.call-start = ((), (), s32[]{:S(2)}) async-start(), calls=%async_computation.32 | async-start | bytes 2621440 | tf_op jit(solution)/shard_map/all_gather | solution.py:167
  248.8 114.3 %reduce-scatter.39.cloned.1.call-start = ((), (), s32[]{:S(2)}) async-start(), calls=%async_computation.18 | async-start | bytes 10485760 | tf_op jit(solution)/shard_map/reduce_scatter | solution.py:184
  291.3 97.1 %all-gather.46.cloned.1.call-start = ((), (), s32[]{:S(2)}) async-start(), calls=%async_computation.33 | async-start | bytes 2621440 | tf_op jit(solution)/shard_map/all_gather | solution.py:167
  365.4 114.0 %reduce-scatter.41.cloned.1.call-start = ((), (), s32[]{:S(2)}) async-start(), calls=%async_computation.19 | async-start | bytes 10485760 | tf_op jit(solution)/shard_map/reduce_scatter | solution.py:184
  407.5 97.5 %all-gather.48.cloned.1.call-start = ((), (), s32[]{:S(2)}) async-start(), calls=%async_computation.34 | async-start | bytes 2621440 | tf_op jit(solution)/shard_map/all_gather | solution.py:167
  482.0 114.2 %reduce-scatter.43.cloned.1.call-start = ((), (), s32[]{:S(2)}) async-start(), calls=%async_computation.20 | async-start | bytes 10485760 | tf_op jit(solution)/shard_map/reduce_scatter | solution.py:184
  524.3 97.1 %all-gather.50.cloned.1.call-start = ((), (), s32[]{:S(2)}) async-start(), calls=%async_computation.35 | async-start | bytes 2621440 | tf_op jit(solution)/shard_map/all_gather | solution.py:167
  598.4 114.0 %reduce-scatter.45.cloned.1.call-start = ((), (), s32[]{:S(2)}) async-start(), calls=%async_computation.21 | async-start | bytes 10485760 | tf_op jit(solution)/shard_map/reduce_scatter | solution.py:184
  640.5 97.5 %all-gather.52.cloned.1.call-start = ((), (), s32[]{:S(2)}) async-start(), calls=%async_computation.36 | async-start | bytes 2621440 | tf_op jit(solution)/shard_map/all_gather | solution.py:167
  715.0 113.9 %reduce-scatter.47.cloned.1.call-start = ((), (), s32[]{:S(2)}) async-start(), calls=%async_computation.22 | async-start | bytes 10485760 | tf_op jit(solution)/shard_map/reduce_scatter | solution.py:184
  757.1 97.1 %all-gather.54.cloned.1.call-start = ((), (), s32[]{:S(2)}) async-start(), calls=%async_computation.37 | async-start | bytes 2621440 | tf_op jit(solution)/shard_map/all_gather | solution.py:167
  831.2 73.5 %reduce-scatter.49.cloned.1.call-start = ((), (), s32[]{:S(2)}) async-start(), calls=%async_computation.39 | async-start | bytes 2621440
  873.1 76.4 %all-gather.56.cloned.1.call-start = ((), (), s32[]{:S(2)}) async-start(), calls=%async_computation.38 | async-start | bytes 2621440 | tf_op jit(solution)/shard_map/all_gather | solution.py:236
  925.4 72.5 %reduce-scatter.51.cloned.1.call-start = ((), (), s32[]{:S(2)}) async-start(), calls=%async_computation.40 | async-start | bytes 2621440
  966.3 56.7 %all-gather.26.cloned.1.call-start = ((), (), s32[]{:S(2)}) async-start(), calls=%async_computation.23 | async-start | bytes 2621440 | tf_op jit(solution)/shard_map/all_gather | solution.py:274
  999.9 73.4 %reduce-scatter.53.cloned.1.call-start = ((), (), s32[]{:S(2)}) async-start(), calls=%async_computation.41 | async-start | bytes 2621440
  1041.7 57.6 %all-gather.28.cloned.1.call-start = ((), (), s32[]{:S(2)}) async-start(), calls=%async_computation.24 | async-start | bytes 2621440 | tf_op jit(solution)/shard_map/all_gather | solution.py:274
  1076.3 73.5 %reduce-scatter.55.cloned.1.call-start = ((), (), s32[]{:S(2)}) async-start(), calls=%async_computation.42 | async-start | bytes 2621440
  1118.2 59.6 %all-gather.30.cloned.1.call-start = ((), (), s32[]{:S(2)}) async-start(), calls=%async_computation.25 | async-start | bytes 2621440 | tf_op jit(solution)/shard_map/all_gather | solution.py:274
  1154.8 74.6 %reduce-scatter.57.cloned.1.call-start = ((), (), s32[]{:S(2)}) async-start(), calls=%async_computation.43 | async-start | bytes 2621440
  1197.8 59.8 %all-gather.32.cloned.1.call-start = ((), (), s32[]{:S(2)}) async-start(), calls=%async_computation.26 | async-start | bytes 2621440 | tf_op jit(solution)/shard_map/all_gather | solution.py:274
  1234.6 74.6 %reduce-scatter.59.cloned.1.call-start = ((), (), s32[]{:S(2)}) async-start(), calls=%async_computation.44 | async-start | bytes 2621440
  1277.6 60.3 %all-gather.34.cloned.1.call-start = ((), (), s32[]{:S(2)}) async-start(), calls=%async_computation.27 | async-start | bytes 2621440 | tf_op jit(solution)/shard_map/all_gather | solution.py:274
  1315.0 71.9 %reduce-scatter.61.cloned.1.call-start = ((), (), s32[]{:S(2)}) async-start(), calls=%async_computation.45 | async-start | bytes 2621440
  1355.3 59.6 %all-gather.36.cloned.1.call-start = ((), (), s32[]{:S(2)}) async-start(), calls=%async_computation.28 | async-start | bytes 2621440 | tf_op jit(solution)/shard_map/all_gather | solution.py:274
  1391.9 76.7 %reduce-scatter.63.cloned.1.call-start = ((), (), s32[]{:S(2)}) async-start(), calls=%async_computation.46 | async-start | bytes 2621440
  1432.3 92.4 %all-gather.38.cloned.1.call-start = ((), (), s32[]{:S(2)}) async-start(), calls=%async_computation.29 | async-start | bytes 2621440 | tf_op jit(solution)/shard_map/all_gather | solution.py:274
  1471.5 176.2 %reduce-scatter.65.cloned.1.call-start = ((), (), s32[]{:S(2)}) async-start(), calls=%async_computation.47 | async-start | bytes 2621440
  1558.6 561.5 %all-reduce.37.cloned.1.call-start = ((), (), s32[]{:S(2)}) async-start(), calls=%async_computation.48 | async-start | bytes 34340864 | tf_op jit(solution)/shard_map/psum | solution.py:349
  (234 other events, 1858.1 us)
Sparse Core Ops, SparseCore 0:
  12.5 25.5 all-gather.39
  57.7 71.7 reduce-scatter.34
  131.8 22.8 all-gather.41
  174.3 71.6 reduce-scatter.36
  248.9 22.8 all-gather.43
  291.4 71.7 reduce-scatter.38
  365.5 22.8 all-gather.45
  407.7 71.6 reduce-scatter.40
  482.1 22.8 all-gather.47
  524.4 71.7 reduce-scatter.42
  640.7 71.6 reduce-scatter.44
  715.1 22.8 all-gather.51
  757.2 71.7 reduce-scatter.46
  831.3 22.8 all-gather.53
  873.2 31.4 reduce-scatter.48
  925.5 23.9 all-gather.55
  966.4 31.4 reduce-scatter.50
  1000.0 22.8 all-gather.25
  1041.8 31.4 reduce-scatter.52
  1076.4 22.8 all-gather.27
  1118.3 31.4 reduce-scatter.54
  1154.9 22.8 all-gather.29
  1197.9 31.4 reduce-scatter.56
  1234.7 22.8 all-gather.31
  1277.8 31.4 reduce-scatter.58
  1315.1 22.8 all-gather.33
  1355.5 31.3 reduce-scatter.60
  1392.0 22.8 all-gather.35
  1432.4 31.3 reduce-scatter.62
  1471.6 22.9 all-gather.37
  1558.7 31.5 reduce-scatter.64
  1595.6 524.4 all-reduce.36
  (1 shorter events, 22.8 us)
where the time goes:
time: 2170 us; the launch traced here: 2150 us
  waiting for transfers between devices  1420 us (65%)
  local copies, waits for them, and re-layouts  298 us (14%)
  matrix products  209 us (10%)
  other arithmetic  133 us (6%)
  blocking collectives  61.5 us (3%)
  between operations  28 us (1%)
    reduce_scatter x7, waiting for transfers between devices, local(): lax.psum_scatter(res_skip_terms(res_weight[layer_position], skip_projecti...  502 us
    psum x1, waiting for transfers between devices, local(): lax.psum((inv_grad, initial_projection_gradient, start_bias_grad, jnp.sta...  415 us
    unnamed x42, waiting for transfers between devices  221 us
    all_gather x8, waiting for transfers between devices, local(): lax.all_gather(rounded, 'chan', axis=0, tiled=True)  155 us
    unnamed x493, local copies, waits for them, and re-layouts  144 us
    all_gather x7, waiting for transfers between devices, local(): lax.all_gather(grad_low, 'chan', axis=0, tiled=True)  103 us
  transfers between devices with their start and end apart: 33, of which 30 were waited for; matrix products, arithmetic and copies ran while one was open for 10% of the time, Pallas kernels for 0%

commit v1 on v0

v1 whole, which is shorter than its diff:
```python
import jax
import jax.numpy as jnp
from jax import lax
from jax.sharding import PartitionSpec as P

CH = 8
HALF = 4
MEL = 80
LAYERS = 8
HOP = 32
FRAMES = 2048
CONV = 1536
EXT = 1664
PACK = 1920

HIGH = lax.Precision.HIGHEST
F32 = jnp.float32
BF16 = jnp.bfloat16


def dot(a, b):
    return jnp.dot(a, b, preferred_element_type=F32)


def invert_small(matrix):
    size_of = matrix.shape[0]
    augmented = jnp.concatenate([matrix, jnp.eye(size_of, dtype=F32)], axis=1)
    log_total = F32(0.0)
    for column in range(size_of):
        pivot = augmented[column, column]
        log_total = log_total + jnp.log(pivot)
        pivot_row = augmented[column] / pivot
        factor = augmented[:, column]
        augmented = augmented - factor[:, None] * pivot_row[None, :]
        augmented = augmented.at[column].set(pivot_row)
    return (augmented[:, size_of:], log_total)


def split(values):
    high = values.astype(BF16)
    return high, (values - high.astype(F32)).astype(BF16)


def local(
    audio_clips,
    mel_frames,
    crop_offsets,
    inv_weight,
    initial_projection_weight,
    start_bias,
    cond_weight,
    in_weight,
    in_bias,
    res_weight,
    res_bias,
    skip_projection_weight,
    skip_output_bias,
    final_projection_weight,
    end_bias,
):
    shards = lax.axis_size("chan")
    shard = lax.axis_index("chan")
    rows = initial_projection_weight.shape[0]
    width = rows * shards
    frames = FRAMES // shards
    mel_count = frames // HOP
    up = [(i, i + 1) for i in range(shards - 1)]
    down = [(i + 1, i) for i in range(shards - 1)]

    offset = crop_offsets[0]
    audio = lax.dynamic_slice(audio_clips[0], (0, offset * HOP + shard * frames), (CH, frames)).T
    mel = lax.dynamic_slice(mel_frames[0], (0, offset + shard * mel_count), (MEL, mel_count)).T
    mixed = jnp.dot(audio, inv_weight.T, precision=HIGH)
    first, second = mixed[:, :HALF], mixed[:, HALF:]

    small = jnp.concatenate(
        [
            initial_projection_weight.T,
            start_bias[None],
            res_bias,
            final_projection_weight,
            skip_output_bias[None],
        ],
        axis=0,
    )
    small = lax.all_gather(small, "chan", axis=1, tiled=True)
    start_weight = small[:4]
    start = small[4]
    residual_bias = small[5:12]
    final_weight = small[12:20]
    skip_bias = small[20]
    fold_local = jnp.einsum(
        "ko,loi->lki", final_weight, skip_projection_weight.astype(F32), precision=HIGH
    )
    fold = lax.all_gather(fold_local, "chan", axis=2, tiled=True)
    fold_high, fold_low = split(fold)
    const = jnp.dot(final_weight, skip_bias, precision=HIGH) + end_bias

    bias_high, bias_low = split(in_bias)
    packed = jnp.concatenate(
        [
            in_weight.reshape(LAYERS, 2 * rows, CONV),
            jnp.concatenate(
                [
                    cond_weight,
                    bias_high[..., None],
                    bias_low[..., None],
                    jnp.zeros((LAYERS, 2, rows, EXT - CONV - MEL - 2), BF16),
                ],
                axis=-1,
            ).reshape(LAYERS, 2 * rows, EXT - CONV),
            jnp.pad(
                res_weight.reshape(LAYERS - 1, 2, width // 2, rows)
                .swapaxes(1, 2)
                .reshape(LAYERS - 1, width // 2, 2 * rows),
                ((0, 1), (0, 0), (0, 0)),
            ),
        ],
        axis=2,
    )
    weights = lax.all_gather(packed, "chan", axis=0, tiled=False)

    mel_part = jnp.concatenate(
        [
            jnp.repeat(mel, HOP, axis=0),
            jnp.ones((frames, 2), BF16),
            jnp.zeros((frames, EXT - CONV - MEL - 2), BF16),
        ],
        axis=1,
    )
    hidden = jnp.dot(first, start_weight, precision=HIGH) + start
    kept = []
    out = jnp.zeros((frames, CH), F32)
    for layer in range(LAYERS):
        d = 2**layer
        low = hidden.astype(BF16)
        before = lax.ppermute(low[frames - d :], "chan", up)
        after = lax.ppermute(low[:d], "chan", down)
        ext = jnp.concatenate(
            [
                jnp.concatenate([before, low[: frames - d]], axis=0),
                low,
                jnp.concatenate([low[d:], after], axis=0),
                mel_part,
            ],
            axis=1,
        )
        gated, dt, ds = [], [], []
        for s in range(shards):
            pre = dot(ext, weights[s, layer, :, :EXT].T)
            t = jnp.tanh(pre[:, :rows])
            g = jax.nn.sigmoid(pre[:, rows:])
            gated.append((t * g).astype(BF16))
            dt.append((g * (1.0 - t * t)).astype(BF16))
            ds.append((t * g * (1.0 - g)).astype(BF16))
        full = jnp.concatenate(gated, axis=1)
        kept.append((ext, gated, dt, ds))
        out = out + dot(full, fold_high[layer].T) + dot(full, fold_low[layer].T)
        if layer < LAYERS - 1:
            residual = jnp.concatenate(
                [
                    weights[:, layer, :, EXT : EXT + rows],
                    weights[:, layer, :, EXT + rows :],
                ],
                axis=1,
            )
            residual = jnp.moveaxis(residual, 0, 1).reshape(width, width)
            hidden = hidden + dot(full, residual.T) + residual_bias[layer]
    out = out + const
    log_scale, shift = out[:, :HALF], out[:, HALF:]
    scale = jnp.exp(log_scale)
    second_out = scale * second + shift
    latent = jnp.concatenate([first, second_out], axis=1)
    inverse, log_abs = invert_small(inv_weight)
    sums = lax.psum(jnp.stack([jnp.sum(log_scale), jnp.sum(latent * latent)]), "chan")
    log_det = sums[0] + FRAMES * log_abs
    crop_loss = (0.5 * sums[1] - log_det) / (CH * FRAMES)
    out_grad = jnp.concatenate([second_out * scale * second - 1.0, second_out], axis=1)
    og_high, og_low = split(out_grad)
    og_ext = jnp.concatenate([og_high, og_low, og_high], axis=1)
    og_pad = jnp.concatenate(
        [jnp.zeros((frames, 88), BF16), og_high, og_low, jnp.zeros((frames, 24), BF16)], axis=1
    )

    hidden_grad = jnp.zeros((frames, width), F32)
    mel_grad = jnp.zeros((frames, EXT - CONV), F32)
    grads = []
    res_bias_grads = []
    for layer in range(LAYERS - 1, -1, -1):
        d = 2**layer
        ext, gated, dt, ds = kept[layer]
        low = hidden_grad.astype(BF16)
        res_bias_grads.append(jnp.sum(low.astype(F32), axis=0))
        fold_ext = jnp.concatenate([fold_high[layer], fold_high[layer], fold_low[layer]], axis=0)
        back = jnp.zeros((frames, EXT), F32)
        parts = []
        for s in range(shards):
            w = weights[s, layer]
            residual = jnp.concatenate([w[:, EXT : EXT + rows], w[:, EXT + rows :]], axis=0)
            gated_back = dot(og_ext, fold_ext[:, s * rows : (s + 1) * rows])
            if layer < LAYERS - 1:
                gated_back = gated_back + dot(low, residual)
            pg = jnp.concatenate(
                [gated_back * dt[s].astype(F32), gated_back * ds[s].astype(F32)], axis=1
            ).astype(BF16)
            back = back + dot(pg, w[:, :EXT])
            top = dot(pg.T, ext)
            side = dot(gated[s].T, jnp.concatenate([low, og_pad], axis=1))
            extra = side[:, width:]
            extra = extra[:, :96] + jnp.pad(extra[:, 96:104], ((0, 0), (88, 0)))
            extra = jnp.pad(extra, ((0, rows), (0, 32)))
            top = top + jnp.pad(extra, ((0, 0), (CONV, 0)))
            res = jnp.concatenate([side[:, : width // 2], side[:, width // 2 : width]], axis=0)
            parts.append(jnp.concatenate([top, res], axis=1).astype(BF16))
        grads.append(jnp.stack(parts))
        b0, b1, b2 = back[:, :width], back[:, width : 2 * width], back[:, 2 * width : 3 * width]
        mel_grad = mel_grad + back[:, CONV:]
        from_next = lax.ppermute(b0[:d].astype(BF16), "chan", down).astype(F32)
        from_prev = lax.ppermute(b2[frames - d :].astype(BF16), "chan", up).astype(F32)
        hidden_grad = (
            hidden_grad
            + b1
            + jnp.concatenate([b0[d:], from_next], axis=0)
            + jnp.concatenate([from_prev, b2[: frames - d]], axis=0)
        )
    total = lax.psum_scatter(
        jnp.stack(grads[::-1], axis=1), "chan", scatter_dimension=0, tiled=False
    )
    total = lax.psum(total, "dp").astype(F32)

    first_back = first + jnp.dot(hidden_grad, start_weight.T, precision=HIGH)
    mixed_grad = jnp.concatenate([first_back, second_out * scale], axis=1)
    audio_grad = jnp.dot(mixed_grad, inv_weight, precision=HIGH)
    rows_out = jnp.concatenate(
        [
            jnp.dot(first.T, hidden_grad, precision=HIGH),
            jnp.sum(hidden_grad, axis=0)[None],
            jnp.stack(res_bias_grads[:0:-1]),
        ],
        axis=0,
    )
    tiny = jnp.concatenate(
        [
            jnp.dot(mixed_grad.T, audio, precision=HIGH).reshape(-1),
            jnp.sum(out_grad, axis=0),
        ]
    )
    rows_out, tiny = lax.psum((rows_out, tiny), ("dp", "chan"))
    mine = lax.dynamic_slice_in_dim(rows_out, shard * rows, rows, 1)
    crops = lax.axis_size("dp") * audio_clips.shape[0]
    inv_grad = tiny[:64].reshape(8, 8) - crops * FRAMES * inverse.T
    end_bias_grad = tiny[64:]
    per_frame = jnp.concatenate([latent, audio_grad], axis=1)
    per_frame = lax.all_gather(per_frame, "chan", axis=0, tiled=True).T
    mel_out = mel_grad.reshape(mel_count, HOP, EXT - CONV).sum(axis=1)[:, :MEL]
    mel_out = lax.all_gather(mel_out, "chan", axis=0, tiled=True).T

    cond_part = total[:, :, CONV:EXT].reshape(LAYERS, 2, rows, EXT - CONV)
    e = jnp.swapaxes(cond_part[:, 0, :, 88:96], 1, 2)
    skip_grad = jnp.einsum("ko,lki->loi", final_weight, e, precision=HIGH)
    end_partial = jnp.einsum(
        "lki,loi->ko", e, skip_projection_weight.astype(F32), precision=HIGH
    )
    end_grad = (
        lax.psum_scatter(end_partial, "chan", scatter_dimension=1, tiled=True)
        + end_bias_grad[:, None] * skip_output_bias[None]
    )
    res_part = total[: LAYERS - 1, :, EXT:].reshape(LAYERS - 1, 2, rows, width // 2)
    res_grad = jnp.swapaxes(res_part, 2, 3).reshape(LAYERS - 1, width, rows)
    return (
        per_frame[:CH][None],
        log_det[None],
        crop_loss[None],
        per_frame[CH:][None],
        mel_out[None],
        inv_grad,
        mine[:4].T,
        mine[4],
        cond_part[..., :MEL],
        total[:, :, :CONV].reshape(LAYERS, 2, rows, CONV),
        cond_part[..., MEL],
        res_grad,
        mine[5:12],
        skip_grad,
        jnp.dot(end_bias_grad, final_projection_weight, precision=HIGH),
        end_grad,
        end_bias_grad,
    )


def solution(mesh):
    in_specs = (
        P("dp", None, None),
        P("dp", None, None),
        P("dp"),
        P(),
        P("chan", None),
        P("chan"),
        P(None, None, "chan", None),
        P(None, None, "chan", None),
        P(None, None, "chan"),
        P(None, None, "chan"),
        P(None, "chan"),
        P(None, None, "chan"),
        P("chan"),
        P(None, "chan"),
        P(),
    )
    out_specs = (
        P("dp", None, None),
        P("dp"),
        P("dp"),
        P("dp", None, None),
        P("dp", None, None),
        P(),
        P("chan", None),
        P("chan"),
        P(None, None, "chan", None),
        P(None, None, "chan", None),
        P(None, None, "chan"),
        P(None, None, "chan"),
        P(None, "chan"),
        P(None, None, "chan"),
        P("chan"),
        P(None, "chan"),
        P(),
    )
    return jax.shard_map(local, mesh=mesh, in_specs=in_specs, out_specs=out_specs, check_vma=False)
```

time: 2170 us -> 1530 us (0.71)
  waiting for transfers between devices: 1420 us -> 851 us
  local copies, waits for them, and re-layouts: 298 us -> 149 us
  starting transfers between devices: 4.57 us -> 83.6 us
  other arithmetic: 133 us -> 92.1 us
  matrix products: 209 us -> 234 us
    reduce_scatter x7 -> x1, waiting for transfers between devices: 502 us -> 0.01 us  [local(): lax.psum_scatter(end_partial, 'chan', scatter_dimension=1, tiled=True)]
    unnamed x42 -> x5, waiting for transfers between devices: 221 us -> 518 us
    psum x1, waiting for transfers between devices: 415 us -> 162 us  [local(): total = lax.psum(total, 'dp').astype(F32)]
    unnamed x493 -> x843, local copies, waits for them, and re-layouts: 144 us -> 12.3 us
    all_gather x16 -> x1, waiting for transfers between devices: 282 us -> 160 us  [local(): weights = lax.all_gather(packed, 'chan', axis=0, tiled=False)]
    ppermute x0 -> x32, starting transfers between devices: none -> 83.4 us  [the longest x8 32.1 us: local(): lax.ppermute(b2[frames - d:].astype(BF16), 'chan', up).astype(F32)]
    another operation x35 -> x0, local copies, waits for them, and re-layouts: 69.6 us -> none  [the longest x9 24.6 us: local(): jnp.stack(in_grads[::-1])]
    another operation x24 -> x2, other arithmetic: 50.6 us -> 4.99 us  [the longest x1 3.62 us: local(): jnp.stack(grads[::-1], axis=1)]
  transfers between devices with their start and end apart: 33 -> 36, of which waited for: 30 -> 9; matrix products, arithmetic and copies ran while one was open for 10% -> 11% of each run, Pallas kernels for 0% -> 0%
where the time goes in v1:
time: 1530 us; the launch traced here: 1520 us
  waiting for transfers between devices  851 us (56%)
  matrix products  234 us (15%)
  local copies, waits for them, and re-layouts  149 us (10%)
  other arithmetic  92.1 us (6%)
  starting transfers between devices  83.6 us (5%)
  blocking collectives  79 us (5%)
  between operations  31.8 us (2%)
    unnamed x5, waiting for transfers between devices  518 us
    dot_general x211, matrix products, dot(): return jnp.dot(a, b, preferred_element_type=F32)  220 us
    psum x1, waiting for transfers between devices, local(): total = lax.psum(total, 'dp').astype(F32)  162 us
    all_gather x1, waiting for transfers between devices, local(): weights = lax.all_gather(packed, 'chan', axis=0, tiled=False)  160 us
    psum x1, blocking collectives, local(): rows_out, tiny = lax.psum((rows_out, tiny), ('dp', 'chan'))  45.3 us
    ppermute x8, starting transfers between devices, local(): lax.ppermute(b2[frames - d:].astype(BF16), 'chan', up).astype(F32)  32.1 us
  transfers between devices with their start and end apart: 36, of which 9 were waited for; matrix products, arithmetic and copies ran while one was open for 11% of the time, Pallas kernels for 0%

profile of v1, /device:TPU:0, one launch (start us, length us, event | category | flops | bytes accessed | tf_op | source)
XLA Modules:
  0.0 1520.5 jit_solution(3668517914054395797)
XLA Ops:
  14.3 12.6 concatenate.1162
  28.0 6.2 all_gather.18
  43.2 8.0 all_gather.21
  59.9 160.3 %all-gather.3.cloned.1.call-done = bf16[32,256,1920]{2,1,0:T(8,128)(2,1)} async-done(((bf16[8,256,1920]{2,1,0:T(8,128)(2,1)}), bf16[32,256,1920]{2,1,0:T(8,128)(2,1)}) %all-gather.3.cloned.1.call-update) | async-done | bytes 31457296 | tf_op jit(solution)/shard_map/all_gather | solution.py:121
  231.2 3.7 slice_bitcast_fusion.97
  243.6 9.2 slice_bitcast_fusion
  252.9 12.0 slice_bitcast_fusion.2
  331.3 4.3 collective-permute-start.6
  351.8 3.8 collective-permute-start.8
  372.0 3.9 collective-permute-start.10
  392.2 4.1 collective-permute-start.12
  411.6 4.4 collective-permute-start.14
  471.5 5.2 collective-permute-start.17
  527.0 4.2 collective-permute-start.21
  553.8 4.5 collective-permute-start.23
  581.0 4.5 collective-permute-start.25
  608.4 4.5 collective-permute-start.27
  632.8 4.5 collective-permute-start.29
  661.7 3.7 fusion
  665.6 3.7 fusion.1
  669.4 3.6 fusion.2
  680.6 3.7 fusion.5
  684.4 3.7 fusion.6
  688.1 3.6 fusion.7
  702.2 517.7 %all-reduce.104.cloned.1.call-done = bf16[4,8,256,1920]{3,2,0,1:T(8,128)(2,1)} async-done(((bf16[4,8,256,1920]{3,2,0,1:T(8,128)(2,1)}), bf16[4,8,256,1920]{3,2,0,1:T(8,128)(2,1)}) %all-reduce.104.cloned.1.call-update) | async-done | bytes 31457296
  1219.9 7.8 dynamic-slice_bitcast_fusion
  1238.6 6.3 psum.28
  1255.5 7.3 all_gather.23
  1267.6 45.3 %all-reduce.98 = (f32[72]{0:T(128)S(1)}, f32[12,512]{1,0:T(8,128)S(1)}) all-reduce(f32[72]{0:T(128)S(1)} %pad_maximum_fusion.139, f32[12,512]{1,0:T(8,128)S(1)} %concatenate.1290), channel_id=1, replica_groups=mesh['dp'=8,'chan'=4] {'dp','chan'}, use_global_device_ids=true, to_apply=%region_5.6 | all-reduce | flops 6216 | bytes 49728 | tf_op jit(solution)/shard_map/psum | solution.py:248
  1314.0 5.8 all_gather.22
  1322.9 161.7 %all-reduce.102.cloned.1.call-done = bf16[8,256,1920]{2,1,0:T(8,128)(2,1)} async-done(((bf16[8,256,1920]{2,1,0:T(8,128)(2,1)}), bf16[8,256,1920]{2,1,0:T(8,128)(2,1)}) %all-reduce.102.cloned.1.call-update) | async-done | bytes 7864336 | tf_op jit(solution)/shard_map/psum | solution.py:229
  1500.1 9.4 slice.3085
  (1494 shorter events, 445.3 us)
Async XLA Ops:
  7.2 213.0 %all-gather.3.cloned.1.call-start = ((), (), s32[]{:S(2)}) async-start(), calls=%async_computation.3 | async-start | bytes 39321600 | tf_op jit(solution)/shard_map/all_gather | solution.py:121
  27.0 1192.9 %all-reduce.104.cloned.1.call-start = ((), (), s32[]{:S(2)}) async-start(), calls=%async_computation.4 | async-start | bytes 62914560
  39.1 18.5 %collective-permute-start = (bf16[1,512]{1,0:T(2,128)(2,1)S(1)}, bf16[1,512]{1,0:T(2,128)(2,1)S(1)}, u32[]{:S(2)}, u32[]{:S(2)}) collective-permute-start(bf16[1,512]{1,0:T(2,128)(2,1)S(1)} %get-tuple-element.489), channel_id=1, source_target_pairs={{0,1},{1,2},{2,3},{4,5},{5,6},{6,7},{8,9},{9,10},{10,11},{12,13},{... | collective-permute-start | bytes 3080 | tf_op jit(solution)/shard_map/ppermute | solution.py:137
  41.4 16.4 %collective-permute-start.1 = (bf16[1,512]{1,0:T(2,128)(2,1)S(1)}, bf16[1,512]{1,0:T(2,128)(2,1)S(1)}, u32[]{:S(2)}, u32[]{:S(2)}) collective-permute-start(bf16[1,512]{1,0:T(2,128)(2,1)S(1)} %get-tuple-element.488), channel_id=1, source_target_pairs={{1,0},{2,1},{3,2},{5,4},{6,5},{7,6},{9,8},{10,9},{11,10},{13,12},{... | collective-permute-start | bytes 3080 | tf_op jit(solution)/shard_map/ppermute | solution.py:138
  267.1 30.8 %collective-permute-start.2 = (bf16[2,512]{1,0:T(2,128)(2,1)}, bf16[2,512]{1,0:T(2,128)(2,1)S(1)}, u32[]{:S(2)}, u32[]{:S(2)}) collective-permute-start(bf16[2,512]{1,0:T(2,128)(2,1)} %get-tuple-element.485), channel_id=1, source_target_pairs={{0,1},{1,2},{2,3},{4,5},{5,6},{6,7},{8,9},{9,10},{10,11},{12,13},{... | collective-permute-start | bytes 6152 | tf_op jit(solution)/shard_map/ppermute | solution.py:137
  269.3 28.8 %collective-permute-start.3 = (bf16[2,512]{1,0:T(2,128)(2,1)}, bf16[2,512]{1,0:T(2,128)(2,1)S(1)}, u32[]{:S(2)}, u32[]{:S(2)}) collective-permute-start(bf16[2,512]{1,0:T(2,128)(2,1)} %get-tuple-element.484), channel_id=1, source_target_pairs={{1,0},{2,1},{3,2},{5,4},{6,5},{7,6},{9,8},{10,9},{11,10},{13,12},{... | collective-permute-start | bytes 6152 | tf_op jit(solution)/shard_map/ppermute | solution.py:138
  311.2 4.6 collective-permute-start.4
  314.4 4.0 collective-permute-start.5
  331.3 5.8 collective-permute-start.6
  351.8 5.5 collective-permute-start.8
  372.0 5.5 collective-permute-start.10
  392.2 5.6 collective-permute-start.12
  411.6 6.1 collective-permute-start.14
  416.0 3.2 collective-permute-start.15
  471.5 16.5 %collective-permute-start.17 = (bf16[128,512]{1,0:T(8,128)(2,1)S(1)}, bf16[128,512]{1,0:T(8,128)(2,1)S(1)}, u32[]{:S(2)}, u32[]{:S(2)}) collective-permute-start(bf16[128,512]{1,0:T(8,128)(2,1)S(1)} %get-tuple-element.337), channel_id=1, source_target_pairs={{0,1},{1,2},{2,3},{4,5},{5,6},{6,7},{8,9},{9,10},{10,11},{12,13},{... | collective-permute-start | bytes 393224 | tf_op jit(solution)/shard_map/ppermute | solution.py:219
  476.7 11.3 collective-permute-start.16
  498.8 14.1 collective-permute-start.19
  502.1 10.8 collective-permute-start.18
  527.0 15.4 %collective-permute-start.21 = (bf16[32,512]{1,0:T(8,128)(2,1)S(1)}, bf16[32,512]{1,0:T(8,128)(2,1)S(1)}, u32[]{:S(2)}, u32[]{:S(2)}) collective-permute-start(bf16[32,512]{1,0:T(8,128)(2,1)S(1)} %get-tuple-element.333), channel_id=1, source_target_pairs={{0,1},{1,2},{2,3},{4,5},{5,6},{6,7},{8,9},{9,10},{10,11},{12,13},{... | collective-permute-start | bytes 98312 | tf_op jit(solution)/shard_map/ppermute | solution.py:219
  531.1 11.2 collective-permute-start.20
  553.8 15.2 collective-permute-start.23
  558.4 10.7 collective-permute-start.22
  581.0 15.9 %collective-permute-start.25 = (bf16[8,512]{1,0:T(8,128)(2,1)S(1)}, bf16[8,512]{1,0:T(8,128)(2,1)S(1)}, u32[]{:S(2)}, u32[]{:S(2)}) collective-permute-start(bf16[8,512]{1,0:T(8,128)(2,1)S(1)} %get-tuple-element.329), channel_id=1, source_target_pairs={{0,1},{1,2},{2,3},{4,5},{5,6},{6,7},{8,9},{9,10},{10,11},{12,13},{... | collective-permute-start | bytes 24584 | tf_op jit(solution)/shard_map/ppermute | solution.py:219
  585.5 11.3 collective-permute-start.24
  608.4 16.0 %collective-permute-start.27 = (bf16[4,512]{1,0:T(4,128)(2,1)S(1)}, bf16[4,512]{1,0:T(4,128)(2,1)S(1)}, u32[]{:S(2)}, u32[]{:S(2)}) collective-permute-start(bf16[4,512]{1,0:T(4,128)(2,1)S(1)} %get-tuple-element.327), channel_id=1, source_target_pairs={{0,1},{1,2},{2,3},{4,5},{5,6},{6,7},{8,9},{9,10},{10,11},{12,13},{... | collective-permute-start | bytes 12296 | tf_op jit(solution)/shard_map/ppermute | solution.py:219
  612.9 11.5 collective-permute-start.26
  632.8 15.6 %collective-permute-start.29 = (bf16[2,512]{1,0:T(2,128)(2,1)S(1)}, bf16[2,512]{1,0:T(2,128)(2,1)S(1)}, u32[]{:S(2)}, u32[]{:S(2)}) collective-permute-start(bf16[2,512]{1,0:T(2,128)(2,1)S(1)} %get-tuple-element.325), channel_id=1, source_target_pairs={{0,1},{1,2},{2,3},{4,5},{5,6},{6,7},{8,9},{9,10},{10,11},{12,13},{... | collective-permute-start | bytes 6152 | tf_op jit(solution)/shard_map/ppermute | solution.py:219
  637.4 11.1 collective-permute-start.28
  691.8 792.8 %all-reduce.102.cloned.1.call-start = ((), (), s32[]{:S(2)}) async-start(), calls=%async_computation.1 | async-start | bytes 15728640 | tf_op jit(solution)/shard_map/psum | solution.py:229
  1227.8 281.7 %reduce-scatter.5.cloned.1.call-start = ((), (), s32[]{:S(2)}) async-start(), calls=%async_computation.2 | async-start | bytes 20480 | tf_op jit(solution)/shard_map/reduce_scatter | solution.py:265
  1250.9 11.9 collective-permute-start.31
  1252.2 10.6 collective-permute-start.30
  (421 other events, 2730.8 us)
Sparse Core Ops, SparseCore 0:
  27.1 193.0 all-gather.2
  691.9 527.9 all-reduce.103
  1227.9 256.6 all-reduce.101
  1487.6 18.3 reduce-scatter.4

commit v2 on v1

--- a/solution.py
+++ b/solution.py
@@ -1,6 +1,10 @@
+import functools
+
 import jax
 import jax.numpy as jnp
 from jax import lax
+from jax.experimental import pallas as pl
+from jax.experimental.pallas import tpu as pltpu
 from jax.sharding import PartitionSpec as P
 
 CH = 8
@@ -9,17 +13,659 @@
 LAYERS = 8
 HOP = 32
 FRAMES = 2048
+WIDTH = 512
 CONV = 1536
 EXT = 1664
 PACK = 1920
+SHARDS = 4
+ROWS = 128
+BLOCK = FRAMES // SHARDS
+PAD = 16
+EDGE = 128
 
 HIGH = lax.Precision.HIGHEST
 F32 = jnp.float32
 BF16 = jnp.bfloat16
+MESH = pl.DeviceIdType.MESH
+VMEM_LIMIT = 62 << 20
 
 
 def dot(a, b):
     return jnp.dot(a, b, preferred_element_type=F32)
+
+
+def dot_nt(a, b):
+    return lax.dot_general(a, b, (((1,), (1,)), ((), ())), preferred_element_type=F32)
+
+
+def dot_tn(a, b):
+    return lax.dot_general(a, b, (((0,), (0,)), ((), ())), preferred_element_type=F32)
+
+
+def when(cond):
+    if cond is True:
+        return lambda f: f()
+    return pl.when(cond)
+
+
+class Place:
+    def __init__(self):
+        self.dp = lax.axis_index("dp")
+        self.chan = lax.axis_index("chan")
+        self.core = self.chan % 2
+        self.side = self.chan // 2
+        self.bit = self.dp % 2
+
+    def chan_device(self, chan):
+        return (self.dp, chan)
+
+    @property
+    def core_shard(self):
+        return self.side * 2 + 1 - self.core
+
+    @property
+    def far_shard(self):
+        return (1 - self.side) * 2 + self.core
+
+    @property
+    def diag_shard(self):
+        return (1 - self.side) * 2 + 1 - self.core
+
+    def dp_bit(self, k):
+        return (self.dp // 2**k) % 2
+
+    def dp_device(self, k):
+        return (self.dp + 2**k * (1 - 2 * self.dp_bit(k)), self.chan)
+
+
+def greet(devices):
+    barrier = pltpu.get_barrier_semaphore()
+    for device in devices:
+        pl.semaphore_signal(barrier, inc=1, device_id=device, device_id_type=MESH)
+    pl.semaphore_wait(barrier, len(devices))
+
+
+def remote(src, dst, send, recv, device):
+    return pltpu.make_async_remote_copy(
+        src_ref=src, dst_ref=dst, send_sem=send, recv_sem=recv, device_id=device, device_id_type=MESH
+    )
+
+
+def forward_kernel(
+    packed, hidden0, mel, fold, res_bias,
+    weights_out, ext_out, acts_out, out,
+    weights, hid, ext, acts, top, bottom,
+    send, recv, own_sem, keep_sem, ext_sem, acts_sem, top_send, top_recv, bottom_send, bottom_recv,
+):
+    me = Place()
+    core_dev = me.chan_device(me.core_shard)
+    far_dev = me.chan_device(me.far_shard)
+    diag_dev = me.chan_device(me.diag_shard)
+    pair_dev = me.dp_device(0)
+    mine = pl.ds(pl.multiple_of(me.bit * ROWS, ROWS), ROWS)
+    other = pl.ds(pl.multiple_of((1 - me.bit) * ROWS, ROWS), ROWS)
+    has_prev = me.chan > 0
+    has_next = me.chan < SHARDS - 1
+    prev_dev = me.chan_device(jnp.maximum(me.chan - 1, 0))
+    next_dev = me.chan_device(jnp.minimum(me.chan + 1, SHARDS - 1))
+
+    @pl.when(jnp.logical_not(has_prev))
+    def _():
+        top[...] = jnp.zeros_like(top)
+
+    @pl.when(jnp.logical_not(has_next))
+    def _():
+        bottom[...] = jnp.zeros_like(bottom)
+
+    greet([core_dev, far_dev, diag_dev, pair_dev])
+
+    def own_copy(l):
+        return pltpu.make_async_copy(packed.at[l], weights.at[l, me.chan], own_sem.at[l])
+
+    def to_core(l):
+        return remote(packed.at[l], weights.at[l, me.chan], send.at[0, l], recv.at[0, l], core_dev)
+
+    def to_far(l):
+        return remote(
+            packed.at[l, mine], weights.at[l, me.chan, mine], send.at[1, l], recv.at[1, l], far_dev
+        )
+
+    def to_pair(l):
+        ref = weights.at[l, me.far_shard, mine]
+        return remote(ref, ref, send.at[2, l], recv.at[2, l], pair_dev)
+
+    def to_core_a(l):
+        ref = weights.at[l, me.far_shard, mine]
+        return remote(ref, ref, send.at[3, l], recv.at[3, l], core_dev)
+
+    def to_core_b(l):
+        ref = weights.at[l, me.far_shard, other]
+        return remote(ref, ref, send.at[4, l], recv.at[4, l], core_dev)
+
+    def issue(l):
+        to_far(l).start()
+        own_copy(l).start()
+        to_core(l).start()
+
+    def relay_far(l):
+        to_far(l).wait_recv()
+        to_pair(l).start()
+        to_core_a(l).start()
+
+    def relay_pair(l):
+        to_pair(l).wait_recv()
+        to_core_b(l).start()
+
+    def arrive(l):
+        own_copy(l).wait()
+        to_core(l).wait_recv()
+        to_core_a(l).wait_recv()
+        to_core_b(l).wait_recv()
+
+    issue(0)
+    issue(1)
+
+    hid[pl.ds(PAD, BLOCK), :] = hidden0[...]
+    out[...] = jnp.zeros_like(out)
+    for slot in range(2):
+        ext[slot, :, CONV:] = mel[...]
+
+    def ext_copy(l):
+        return pltpu.make_async_copy(ext.at[l % 2], ext_out.at[l], ext_sem.at[l % 2])
+
+    def acts_copy(l):
+        return pltpu.make_async_copy(acts.at[l % 2], acts_out.at[l], acts_sem.at[l % 2])
+
+    def keep_copy(l):
+        return pltpu.make_async_copy(weights.at[l], weights_out.at[l], keep_sem.at[l])
+
+    def to_next(l, rows):
+        p = l % 2
+        return remote(
+            ext.at[p, pl.ds(BLOCK - rows, rows), pl.ds(WIDTH, WIDTH)],
+            top.at[p, pl.ds(EDGE - rows, rows)],
+            top_send.at[p], top_recv.at[p], next_dev,
+        )
+
+    def to_prev(l, rows):
+        p = l % 2
+        return remote(
+            ext.at[p, pl.ds(0, rows), pl.ds(WIDTH, WIDTH)],
+            bottom.at[p, pl.ds(0, rows)],
+            bottom_send.at[p], bottom_recv.at[p], prev_dev,
+        )
+
+    def by_edge(l, f):
+        pl.when(l <= 4)(lambda: f(PAD))
+        pl.when(l > 4)(lambda: f(EDGE))
+
+    def compute(l):
+        p = l % 2
+
+        @pl.when(l >= 2)
+        def _():
+            ext_copy(l - 2).wait()
+            acts_copy(l - 2).wait()
+
+        ext[p, :, WIDTH : 2 * WIDTH] = hid[pl.ds(PAD, BLOCK), :].astype(BF16)
+
+        def start(rows):
+            pl.when(has_next)(lambda: to_next(l, rows).start())
+            pl.when(has_prev)(lambda: to_prev(l, rows).start())
+
+        def finish(rows):
+            @pl.when(has_next)
+            def _():
+                to_next(l, rows).wait_send()
+                to_prev(l, rows).wait_recv()
+
+            @pl.when(has_prev)
+            def _():
+                to_prev(l, rows).wait_send()
+                to_next(l, rows).wait_recv()
+
+        by_edge(l, start)
+        by_edge(l, finish)
+        hid[pl.ds(0, PAD), :] = top[p, pl.ds(EDGE - PAD, PAD), :].astype(F32)
+        hid[pl.ds(PAD + BLOCK, PAD), :] = bottom[p, pl.ds(0, PAD), :].astype(F32)
+        for layer in range(LAYERS):
+            d = 2**layer
+
+            @pl.when(l == layer)
+            def _():
+                if d < PAD:
+                    ext[p, :, :WIDTH] = hid[pl.ds(PAD - d, BLOCK), :].astype(BF16)
+                    ext[p, :, 2 * WIDTH : CONV] = hid[pl.ds(PAD + d, BLOCK), :].astype(BF16)
+                else:
+                    ext[p, :d, :WIDTH] = top[p, EDGE - d :, :]
+                    ext[p, d:, :WIDTH] = ext[p, : BLOCK - d, WIDTH : 2 * WIDTH]
+                    ext[p, BLOCK - d :, 2 * WIDTH : CONV] = bottom[p, :d, :]
+                    ext[p, : BLOCK - d, 2 * WIDTH : CONV] = ext[p, d:, WIDTH : 2 * WIDTH]
+
+        ext_copy(l).start()
+
+        def one(s, carry):
+            pre = dot_nt(ext[p], weights[l, s, :, :EXT])
+            t = jnp.tanh(pre[:, :ROWS])
+            g = 0.5 * jnp.tanh(0.5 * pre[:, ROWS:]) + 0.5
+            tg = t * g
+            acts[p, s, 0] = tg.astype(BF16)
+            acts[p, s, 1] = (g - t * tg).astype(BF16)
+            acts[p, s, 2] = (tg * (1.0 - g)).astype(BF16)
+            return carry
+
+        lax.fori_loop(0, SHARDS, one, 0)
+        acts_copy(l).start()
+        gated = jnp.concatenate([acts[p, s, 0] for s in range(SHARDS)], axis=1)
+        out[...] += dot_nt(gated, fold[l])
+
+        @pl.when(l < LAYERS - 1)
+        def _():
+            for h in range(2):
+                res = jnp.concatenate(
+                    [weights[l, s, :, EXT + h * ROWS : EXT + (h + 1) * ROWS] for s in range(SHARDS)], axis=1
+                )
+                cols = slice(h * 2 * ROWS, (h + 1) * 2 * ROWS)
+                hid[pl.ds(PAD, BLOCK), cols] += dot_nt(gated, res) + res_bias[pl.ds(l, 1), cols]
+
+    relay_far(0)
+
+    def step(l, carry):
+        pl.when(l + 2 < LAYERS)(lambda: issue(l + 2))
+        pl.when(l + 1 < LAYERS)(lambda: relay_far(l + 1))
+        relay_pair(l)
+        arrive(l)
+        keep_copy(l).start()
+        compute(l)
+        return carry
+
+    lax.fori_loop(0, LAYERS, step, 0)
+    for l in (LAYERS - 2, LAYERS - 1):
+        ext_copy(l).wait()
+        acts_copy(l).wait()
+
+    def drain(l, carry):
+        to_core(l).wait_send()
+        to_far(l).wait_send()
+        to_pair(l).wait_send()
+        to_core_a(l).wait_send()
+        to_core_b(l).wait_send()
+        keep_copy(l).wait()
+        return carry
+
+    lax.fori_loop(0, LAYERS, drain, 0)
+
+
+def run_forward(packed, hidden0, mel, fold, res_bias):
+    vmem = pl.BlockSpec(memory_space=pltpu.VMEM)
+    hbm = pl.BlockSpec(memory_space=pl.ANY)
+    dma = pltpu.SemaphoreType.DMA
+    return pl.pallas_call(
+        forward_kernel,
+        out_shape=(
+            jax.ShapeDtypeStruct((LAYERS, SHARDS, 2 * ROWS, PACK), BF16),
+            jax.ShapeDtypeStruct((LAYERS, BLOCK, EXT), BF16),
+            jax.ShapeDtypeStruct((LAYERS, SHARDS, 3, BLOCK, ROWS), BF16),
+            jax.ShapeDtypeStruct((BLOCK, 2 * CH), F32),
+        ),
+        in_specs=[hbm, vmem, vmem, vmem, vmem],
+        out_specs=(hbm, hbm, hbm, vmem),
+        scratch_shapes=[
+            pltpu.VMEM((LAYERS, SHARDS, 2 * ROWS, PACK), BF16),
+            pltpu.VMEM((PAD + BLOCK + PAD, WIDTH), F32),
+            pltpu.VMEM((2, BLOCK, EXT), BF16),
+            pltpu.VMEM((2, SHARDS, 3, BLOCK, ROWS), BF16),
+            pltpu.VMEM((2, EDGE, WIDTH), BF16),
+            pltpu.VMEM((2, EDGE, WIDTH), BF16),
+            dma((5, LAYERS)), dma((5, LAYERS)), dma((LAYERS,)), dma((LAYERS,)), dma((2,)), dma((2,)),
+            dma((2,)), dma((2,)), dma((2,)), dma((2,)),
+        ],
+        compiler_params=pltpu.CompilerParams(
+            collective_id=0, has_side_effects=True, vmem_limit_bytes=VMEM_LIMIT
+        ),
+    )(packed, hidden0, mel, fold, res_bias)
+
+
+def levels_of(dp_size):
+    levels, rows, bit = [], 2 * ROWS, 0
+    while 2**bit < dp_size:
+        after = rows // 2 if rows > PAD else rows
+        levels.append((bit, rows, after))
+        rows, bit = after, bit + 1
+    return levels
+
+
+def backward_kernel(
+    levels,
+    weights, ext_in, acts_in, og, fold,
+    total, grad_out, mel_out, bias_out,
+    wbuf, abuf, ext, low, tap0, tap2, sums, from_core, from_far, edge_out, edge_in, *rest,
+):
+    level_bufs = rest[: len(levels)]
+    (w_sem, a_sem, e_sem, core_send, core_recv, credit, far_send, far_recv,
+     rs_send, rs_recv, ag_send, ag_recv, edge_send, edge_recv, out_sem) = rest[len(levels) :]
+    me = Place()
+    core_dev = me.chan_device(me.core_shard)
+    far_dev = me.chan_device(me.far_shard)
+    diag_dev = me.chan_device(me.diag_shard)
+    has_prev = me.chan > 0
+    has_next = me.chan < SHARDS - 1
+    prev_dev = me.chan_device(jnp.maximum(me.chan - 1, 0))
+    next_dev = me.chan_device(jnp.minimum(me.chan + 1, SHARDS - 1))
+    edge_in[...] = jnp.zeros_like(edge_in)
+    greet([core_dev, far_dev, diag_dev] + [me.dp_device(bit) for bit, _, _ in levels])
+
+    def shard_of(j):
+        core = jnp.where(j < 2, 1 - me.core, me.core)
+        return (j % 2) * 2 + core
+
+    def w_copy(q):
+        l, s = LAYERS - 1 - q // SHARDS, shard_of(q % SHARDS)
+        return pltpu.make_async_copy(weights.at[l, s], wbuf.at[q % 2], w_sem.at[q % 2])
+
+    def a_copy(q):
+        l, s = LAYERS - 1 - q // SHARDS, shard_of(q % SHARDS)
+        return pltpu.make_async_copy(acts_in.at[l, s], abuf.at[q % 2], a_sem.at[q % 2])
+
+    def e_copy(i):
+        return pltpu.make_async_copy(ext_in.at[LAYERS - 1 - i], ext.at[i % 2], e_sem.at[i % 2])
+
+    def kept(i, ys):
+        return 4 + 2 * i + ys
+
+    def to_core(i, ys):
+        p = i % 2
+        return remote(
+            sums.at[2 * p + ys], from_core.at[2 * p + ys], core_send.at[p, ys], core_recv.at[p, ys], core_dev
+        )
+
+    def to_far(i):
+        return remote(
+            sums.at[kept(i, 1 - me.side)], from_far.at[i], far_send.at[i], far_recv.at[i], far_dev
+        )
+
+    def add_rows(i, base, rows, src, src_at):
+        own = kept(i, me.side)
+        chunk = min(rows, 32)
+
+        def body(k, carry):
+            at = pl.ds(pl.multiple_of(base + k * chunk, PAD), chunk)
+            sums[own, at, :] = sums[own, at, :] + src[src_at, pl.ds(pl.multiple_of(k * chunk, PAD), chunk), :]
+            return carry
+
+        lax.fori_loop(0, rows // chunk, body, 0)
+
+    def bases():
+        base, got = 0, []
+        for bit, rows, after in levels:
+            got.append(base)
+            if after < rows:
+                base = base + me.dp_bit(bit) * after
+        return got + [base]
+
+    base_at = bases()
+
+    def rs(k, i):
+        bit, rows, after = levels[k]
+        start = base_at[k]
+        if after < rows:
+            start = start + (1 - me.dp_bit(bit)) * after
+        at = pl.ds(pl.multiple_of(start, PAD), after)
+        return remote(
+            sums.at[kept(i, me.side), at], level_bufs[k].at[i], rs_send.at[k, i], rs_recv.at[k, i],
+            me.dp_device(bit),
+        )
+
+    def ag_out(k, i):
+        bit, rows, after = levels[k]
+        ref = total.at[LAYERS - 1 - i, pl.ds(pl.multiple_of(base_at[k + 1], PAD), after)]
+        return remote(ref, ref, ag_send.at[k, i], ag_recv.at[k, i], me.dp_device(bit))
+
+    def ag_in(k, i):
+        bit, rows, after = levels[k]
+        start = base_at[k] + (1 - me.dp_bit(bit)) * after
+        ref = total.at[LAYERS - 1 - i, pl.ds(pl.multiple_of(start, PAD), after)]
+        return remote(ref, ref, ag_send.at[k, i], ag_recv.at[k, i], me.dp_device(bit))
+
+    halving = [k for k, (bit, rows, after) in enumerate(levels) if after < rows]
+
+    def out_copy(i):
+        at = pl.ds(pl.multiple_of(base_at[-1], PAD), levels[-1][2] if levels else 2 * ROWS)
+        return pltpu.make_async_copy(
+            sums.at[kept(i, me.side), at], total.at[LAYERS - 1 - i, at], out_sem.at[i]
+        )
+
+    def stage_core(i):
+        p = i % 2
+        for ys in (1 - me.side, me.side):
+            to_core(i, ys).wait_recv()
+
+            def body(k, carry):
+                at = pl.ds(pl.multiple_of(k * 32, 32), 32)
+                slot = kept(i, ys)
+                sums[slot, at, :] = sums[slot, at, :] + from_core[2 * p + ys, at, :]
+                return carry
+
+            lax.fori_loop(0, 2 * ROWS // 32, body, 0)
+            pl.semaphore_signal(credit.at[ys], inc=1, device_id=core_dev, device_id_type=MESH)
+            if ys is not me.side:
+                to_far(i).start()
+
+    def stage_far(i):
+        to_far(i).wait_recv()
+        add_rows(i, 0, 2 * ROWS, from_far, i)
+        rs(0, i).start()
+
+    def ag_first(i):
+        out_copy(i).start()
+        out_copy(i).wait()
+        if halving:
+            ag_out(halving[-1], i).start()
+
+    def stage_rs(k, i):
+        bit, rows, after = levels[k]
+        rs(k, i).wait_recv()
+        if after == rows:
+            rs(k, i).wait_send()
+        add_rows(i, base_at[k + 1], after, level_bufs[k], i)
+        if k + 1 < len(levels):
+            rs(k + 1, i).start()
+        else:
+            ag_first(i)
+
+    def stage_ag(n, i):
+        k = halving[n]
+        ag_in(k, i).wait_recv()
+        if n > 0:
+            ag_out(halving[n - 1], i).start()
+
+    def to_prev(i, rows):
+        p = i % 2
+        return remote(
+            edge_out.at[0, pl.ds(0, rows)], edge_in.at[p, 0, pl.ds(0, rows)],
+            edge_send.at[0], edge_recv.at[p, 0], prev_dev,
+        )
+
+    def to_next(i, rows):
+        p = i % 2
+        return remote(
+            edge_out.at[1, pl.ds(EDGE - rows, rows)], edge_in.at[p, 1, pl.ds(EDGE - rows, rows)],
+            edge_send.at[1], edge_recv.at[p, 1], next_dev,
+        )
+
+    def by_edge(i, f):
+        pl.when(i < 3)(lambda: f(EDGE))
+        pl.when(i >= 3)(lambda: f(PAD))
+
+    def compute(i):
+        l = LAYERS - 1 - i
+        p = i % 2
+        pl.when(i + 1 < LAYERS)(lambda: e_copy(i + 1).start())
+        now = grad_out[...].astype(BF16)
+        low[:, :WIDTH] = now
+        bias_out[pl.ds(l, 1), :] = jnp.sum(now.astype(F32), axis=0, keepdims=True)
+        tap0[pl.ds(0, BLOCK), :] = jnp.zeros((BLOCK, WIDTH), F32)
+        tap2[pl.ds(EDGE, BLOCK), :] = jnp.zeros((BLOCK, WIDTH), F32)
+        e_copy(i).wait()
+
+        def one(j, carry):
+            q = i * SHARDS + j
+            b = q % 2
+            s = shard_of(j)
+            pl.when(q + 1 < LAYERS * SHARDS)(lambda: w_copy(q + 1).start())
+            pl.when(q + 1 < LAYERS * SHARDS)(lambda: a_copy(q + 1).start())
+
+            @pl.when((j < 2) & (i >= 2))
+            def _():
+                to_core(i - 2, j).wait_send()
+
+            w_copy(q).wait()
+            a_copy(q).wait()
+            slot = jnp.where(j < 2, 2 * p + j, kept(i, j - 2))
+            gated = abuf[b, 0]
+            res = jnp.concatenate([wbuf[b, :, EXT : EXT + ROWS], wbuf[b, :, EXT + ROWS :]], axis=0)
+            back = dot(low[:, :WIDTH], res) + dot(low[:, WIDTH:], fold[l, s])
+            pg = jnp.concatenate(
+                [(back * abuf[b, 1].astype(F32)).astype(BF16), (back * abuf[b, 2].astype(F32)).astype(BF16)],
+                axis=1,
+            )
+            tap0[pl.ds(0, BLOCK), :] += dot(pg, wbuf[b, :, :WIDTH])
+            grad_out[...] += dot(pg, wbuf[b, :, WIDTH : 2 * WIDTH])
+            tap2[pl.ds(EDGE, BLOCK), :] += dot(pg, wbuf[b, :, 2 * WIDTH : CONV])
+            mel_out[...] += dot(pg, wbuf[b, :, CONV:EXT])
+            for k in range(3):
+                cols = slice(k * WIDTH, (k + 1) * WIDTH)
+                sums[slot, :, cols] = dot_tn(pg, ext[p, :, cols]).astype(BF16)
+            side = dot_tn(gated, low[...])
+            extra = side[:, WIDTH:]
+            extra = extra + pltpu.roll(extra, ROWS - CH, 1)
+            lane = lax.broadcasted_iota(jnp.int32, (ROWS, ROWS), 1)
+            extra = jnp.where((lane >= 88) & (lane < 96), extra, 0.0)
+            top = dot_tn(pg, ext[p, :, CONV:])
+            sums[slot, :ROWS, CONV:EXT] = (top[:ROWS] + extra).astype(BF16)
+            sums[slot, ROWS:, CONV:EXT] = top[ROWS:].astype(BF16)
+            sums[slot, :ROWS, EXT:] = side[:, : 2 * ROWS].astype(BF16)
+            sums[slot, ROWS:, EXT:] = side[:, 2 * ROWS : WIDTH].astype(BF16)
+
+            @pl.when(j < 2)
+            def _():
+                pl.when(i >= 2)(lambda: pl.semaphore_wait(credit.at[j], 1))
+                to_core(i, j).start()
+
+            return carry
+
+        lax.fori_loop(0, SHARDS, one, 0)
+
+        edge_out[0] = tap0[pl.ds(0, EDGE), :].astype(BF16)
+        edge_out[1] = tap2[pl.ds(BLOCK, EDGE), :].astype(BF16)
+
+        def start(rows):
+            pl.when(has_next)(lambda: to_next(i, rows).start())
+            pl.when(has_prev)(lambda: to_prev(i, rows).start())
+
+        def finish(rows):
+            @pl.when(has_next)
+            def _():
+                to_next(i, rows).wait_send()
+                to_prev(i, rows).wait_recv()
+
+            @pl.when(has_prev)
+            def _():
+                to_prev(i, rows).wait_send()
+                to_next(i, rows).wait_recv()
+
+        by_edge(i, start)
+        by_edge(i, finish)
+        tap0[pl.ds(BLOCK, EDGE), :] = edge_in[p, 0].astype(F32)
+        tap2[pl.ds(0, EDGE), :] = edge_in[p, 1].astype(F32)
+        for layer in range(LAYERS):
+            d = 2**layer
+
+            @pl.when(l == layer)
+            def _():
+                grad_out[...] += tap0[pl.ds(d, BLOCK), :] + tap2[pl.ds(EDGE - d, BLOCK), :]
+
+    e_copy(0).start()
+    w_copy(0).start()
+    a_copy(0).start()
+    grad_out[...] = jnp.zeros_like(grad_out)
+    mel_out[...] = jnp.zeros_like(mel_out)
+    low[:, WIDTH:] = og[...]
+
+    stages = [stage_core, stage_far]
+    stages += [functools.partial(stage_rs, k) for k in range(len(levels))]
+    stages += [functools.partial(stage_ag, n) for n in range(len(halving) - 1, -1, -1)]
+
+    def step(i, carry):
+        for lag in range(len(stages) - 1, 0, -1):
+            pl.when((i >= lag) & (i < LAYERS + lag))(functools.partial(stages[lag], i - lag))
+
+        @pl.when(i < LAYERS)
+        def _():
+            compute(i)
+            stage_core(i)
+
+        return carry
+
+    lax.fori_loop(0, LAYERS + len(stages) - 1, step, 0)
+
+    for i in (LAYERS - 2, LAYERS - 1):
+        for ys in range(2):
+            to_core(i, ys).wait_send()
+            pl.semaphore_wait(credit.at[ys], 1)
+
+    def drain(i, carry):
+        to_far(i).wait_send()
+        for k, (bit, rows, after) in enumerate(levels):
+            if after < rows:
+                rs(k, i).wait_send()
+                ag_out(k, i).wait_send()
+        return carry
+
+    lax.fori_loop(0, LAYERS, drain, 0)
+
+
+def run_backward(dp_size, weights, ext, acts, og, fold):
+    levels = levels_of(dp_size)
+    vmem = pl.BlockSpec(memory_space=pltpu.VMEM)
+    hbm = pl.BlockSpec(memory_space=pl.ANY)
+    dma = pltpu.SemaphoreType.DMA
+    block = (2 * ROWS, PACK)
+    n = max(len(levels), 1)
+    return pl.pallas_call(
+        functools.partial(backward_kernel, levels),
+        out_shape=(
+            jax.ShapeDtypeStruct((LAYERS,) + block, BF16),
+            jax.ShapeDtypeStruct((BLOCK, WIDTH), F32),
+            jax.ShapeDtypeStruct((BLOCK, EXT - CONV), F32),
+            jax.ShapeDtypeStruct((LAYERS, WIDTH), F32),
+        ),
+        in_specs=[hbm, hbm, hbm, vmem, vmem],
+        out_specs=(hbm, vmem, vmem, vmem),
+        scratch_shapes=[
+            pltpu.VMEM((2,) + block, BF16),
+            pltpu.VMEM((2, 3, BLOCK, ROWS), BF16),
+            pltpu.VMEM((2, BLOCK, EXT), BF16),
+            pltpu.VMEM((BLOCK, WIDTH + ROWS), BF16),
+            pltpu.VMEM((BLOCK + EDGE, WIDTH), F32),
+            pltpu.VMEM((EDGE + BLOCK, WIDTH), F32),
+            pltpu.VMEM((4 + 2 * LAYERS,) + block, BF16),
+            pltpu.VMEM((4,) + block, BF16),
+            pltpu.VMEM((LAYERS,) + block, BF16),
+            pltpu.VMEM((2, EDGE, WIDTH), BF16),
+            pltpu.VMEM((2, 2, EDGE, WIDTH), BF16),
+        ]
+        + [pltpu.VMEM((LAYERS, after, PACK), BF16) for _, _, after in levels]
+        + [
+            dma((2,)), dma((2,)), dma((2,)), dma((2, 2)), dma((2, 2)), pltpu.SemaphoreType.REGULAR((2,)),
+            dma((LAYERS,)), dma((LAYERS,)),
+            dma((n, LAYERS)), dma((n, LAYERS)), dma((n, LAYERS)), dma((n, LAYERS)),
+            dma((2,)), dma((2, 2)), dma((LAYERS,)),
+        ],
+        compiler_params=pltpu.CompilerParams(
+            collective_id=1, has_side_effects=True, vmem_limit_bytes=VMEM_LIMIT
+        ),
+    )(weights, ext, acts, og, fold)
 
 
 def invert_small(matrix):
@@ -118,7 +764,6 @@
         ],
         axis=2,
     )
-    weights = lax.all_gather(packed, "chan", axis=0, tiled=False)
 
     mel_part = jnp.concatenate(
         [
@@ -129,43 +774,14 @@
         axis=1,
     )
     hidden = jnp.dot(first, start_weight, precision=HIGH) + start
-    kept = []
-    out = jnp.zeros((frames, CH), F32)
-    for layer in range(LAYERS):
-        d = 2**layer
-        low = hidden.astype(BF16)
-        before = lax.ppermute(low[frames - d :], "chan", up)
-        after = lax.ppermute(low[:d], "chan", down)
-        ext = jnp.concatenate(
-            [
-                jnp.concatenate([before, low[: frames - d]], axis=0),
-                low,
-                jnp.concatenate([low[d:], after], axis=0),
-                mel_part,
-            ],
-            axis=1,
-        )
-        gated, dt, ds = [], [], []
-        for s in range(shards):
-            pre = dot(ext, weights[s, layer, :, :EXT].T)
-            t = jnp.tanh(pre[:, :rows])
-            g = jax.nn.sigmoid(pre[:, rows:])
-            gated.append((t * g).astype(BF16))
-            dt.append((g * (1.0 - t * t)).astype(BF16))
-            ds.append((t * g * (1.0 - g)).astype(BF16))
-        full = jnp.concatenate(gated, axis=1)
-        kept.append((ext, gated, dt, ds))
-        out = out + dot(full, fold_high[layer].T) + dot(full, fold_low[layer].T)
-        if layer < LAYERS - 1:
-            residual = jnp.concatenate(
-                [
-                    weights[:, layer, :, EXT : EXT + rows],
-                    weights[:, layer, :, EXT + rows :],
-                ],
-                axis=1,
-            )
-            residual = jnp.moveaxis(residual, 0, 1).reshape(width, width)
-            hidden = hidden + dot(full, residual.T) + residual_bias[layer]
+    weights, ext, acts, out = run_forward(
+        packed,
+        hidden,
+        mel_part,
+        jnp.concatenate([fold_high, fold_low], axis=1),
+        jnp.pad(residual_bias, ((0, 1), (0, 0))),
+    )
+    out = out[:, :CH] + out[:, CH:]
     out = out + const
     log_scale, shift = out[:, :HALF], out[:, HALF:]
     scale = jnp.exp(log_scale)
@@ -177,56 +793,15 @@
     crop_loss = (0.5 * sums[1] - log_det) / (CH * FRAMES)
     out_grad = jnp.concatenate([second_out * scale * second - 1.0, second_out], axis=1)
     og_high, og_low = split(out_grad)
-    og_ext = jnp.concatenate([og_high, og_low, og_high], axis=1)
-    og_pad = jnp.concatenate(
-        [jnp.zeros((frames, 88), BF16), og_high, og_low, jnp.zeros((frames, 24), BF16)], axis=1
-    )
-
-    hidden_grad = jnp.zeros((frames, width), F32)
-    mel_grad = jnp.zeros((frames, EXT - CONV), F32)
-    grads = []
-    res_bias_grads = []
-    for layer in range(LAYERS - 1, -1, -1):
-        d = 2**layer
-        ext, gated, dt, ds = kept[layer]
-        low = hidden_grad.astype(BF16)
-        res_bias_grads.append(jnp.sum(low.astype(F32), axis=0))
-        fold_ext = jnp.concatenate([fold_high[layer], fold_high[layer], fold_low[layer]], axis=0)
-        back = jnp.zeros((frames, EXT), F32)
-        parts = []
-        for s in range(shards):
-            w = weights[s, layer]
-            residual = jnp.concatenate([w[:, EXT : EXT + rows], w[:, EXT + rows :]], axis=0)
-            gated_back = dot(og_ext, fold_ext[:, s * rows : (s + 1) * rows])
-            if layer < LAYERS - 1:
-                gated_back = gated_back + dot(low, residual)
-            pg = jnp.concatenate(
-                [gated_back * dt[s].astype(F32), gated_back * ds[s].astype(F32)], axis=1
-            ).astype(BF16)
-            back = back + dot(pg, w[:, :EXT])
-            top = dot(pg.T, ext)
-            side = dot(gated[s].T, jnp.concatenate([low, og_pad], axis=1))
-            extra = side[:, width:]
-            extra = extra[:, :96] + jnp.pad(extra[:, 96:104], ((0, 0), (88, 0)))
-            extra = jnp.pad(extra, ((0, rows), (0, 32)))
-            top = top + jnp.pad(extra, ((0, 0), (CONV, 0)))
-            res = jnp.concatenate([side[:, : width // 2], side[:, width // 2 : width]], axis=0)
-            parts.append(jnp.concatenate([top, res], axis=1).astype(BF16))
-        grads.append(jnp.stack(parts))
-        b0, b1, b2 = back[:, :width], back[:, width : 2 * width], back[:, 2 * width : 3 * width]
-        mel_grad = mel_grad + back[:, CONV:]
-        from_next = lax.ppermute(b0[:d].astype(BF16), "chan", down).astype(F32)
-        from_prev = lax.ppermute(b2[frames - d :].astype(BF16), "chan", up).astype(F32)
-        hidden_grad = (
-            hidden_grad
-            + b1
-            + jnp.concatenate([b0[d:], from_next], axis=0)
-            + jnp.concatenate([from_prev, b2[: frames - d]], axis=0)
-        )
-    total = lax.psum_scatter(
-        jnp.stack(grads[::-1], axis=1), "chan", scatter_dimension=0, tiled=False
-    )
-    total = lax.psum(total, "dp").astype(F32)
+    og = jnp.concatenate(
+        [jnp.zeros((frames, 88), BF16), og_high, og_low, og_high, jnp.zeros((frames, 16), BF16)], axis=1
+    )
+    fold_rows = jnp.pad(jnp.concatenate([fold_high, fold_high, fold_low], axis=1), ((0, 0), (88, 16), (0, 0)))
+    fold_rows = fold_rows.reshape(LAYERS, rows, shards, rows).swapaxes(1, 2)
+    total, hidden_grad, mel_grad, res_bias_grads = run_backward(
+        lax.axis_size("dp"), weights, ext, acts, og, fold_rows
+    )
+    total = total.astype(F32)
 
     first_back = first + jnp.dot(hidden_grad, start_weight.T, precision=HIGH)
     mixed_grad = jnp.concatenate([first_back, second_out * scale], axis=1)
@@ -235,7 +810,7 @@
         [
             jnp.dot(first.T, hidden_grad, precision=HIGH),
             jnp.sum(hidden_grad, axis=0)[None],
-            jnp.stack(res_bias_grads[:0:-1]),
+            res_bias_grads[: LAYERS - 1],
         ],
         axis=0,
     )

time: 1530 us -> 632 us (0.41)
  waiting for transfers between devices: 851 us -> 0.04 us
  Pallas kernels: 0 us -> 444 us
  matrix products: 234 us -> 12.8 us
  local copies, waits for them, and re-layouts: 149 us -> 60.1 us
  starting transfers between devices: 83.6 us -> 0.04 us
  other arithmetic: 92.1 us -> 17.1 us
    unnamed x5 -> x1, waiting for transfers between devices: 518 us -> 0.02 us
    pallas_call x0 -> x2, Pallas kernels: none -> 444 us  [the longest x1 323 us: run_backward(): pl.pallas_call(functools.partial(backward_kernel, levels), out_shape=(jax...]
    dot_general x211 -> x0, matrix products: 220 us -> none  [dot(): return jnp.dot(a, b, preferred_element_type=F32)]
    psum x1 -> x0, waiting for transfers between devices: 162 us -> none  [local(): total = lax.psum(total, 'dp').astype(F32)]
    all_gather x1 -> x0, waiting for transfers between devices: 160 us -> none  [local(): weights = lax.all_gather(packed, 'chan', axis=0, tiled=False)]
    ppermute x32 -> x0, starting transfers between devices: 83.4 us -> none  [the longest x8 32.1 us: local(): lax.ppermute(b2[frames - d:].astype(BF16), 'chan', up).astype(F32)]
    unnamed x7 -> x0, other arithmetic: 25.6 us -> none
    squeeze x4 -> x0, local copies, waits for them, and re-layouts: 24.9 us -> none  [the longest x2 21.2 us: local(): w = weights[s, layer]]
  transfers between devices with their start and end apart: 36 -> 1, of which waited for: 9 -> 0; matrix products, arithmetic and copies ran while one was open for 11% -> 8% of each run, Pallas kernels for 0% -> 0%
where the time goes in v2:
time: 632 us; the launch traced here: 630 us
  Pallas kernels  444 us (70%)
  blocking collectives  71.7 us (11%)
  local copies, waits for them, and re-layouts  60.1 us (10%)
  between operations  24 us (4%)
  other arithmetic  17.1 us (3%)
  matrix products  12.8 us (2%)
    pallas_call x1, Pallas kernels, run_backward(): pl.pallas_call(functools.partial(backward_kernel, levels), out_shape=(jax...  323 us
    pallas_call x1, Pallas kernels, run_forward(): pl.pallas_call(forward_kernel, out_shape=(jax.ShapeDtypeStruct((LAYERS, S...  121 us
    psum x1, blocking collectives, local(): rows_out, tiny = lax.psum((rows_out, tiny), ('dp', 'chan'))  42.9 us
  transfers between devices with their start and end apart: 1, of which 0 were waited for; matrix products, arithmetic and copies ran while one was open for 8% of the time, Pallas kernels for 0%

profile of v2, /device:TPU:0, one launch (start us, length us, event | category | flops | bytes accessed | tf_op | source)
XLA Modules:
  0.0 630.1 jit_solution(2858866396431067716)
XLA Ops:
  7.3 3.0 concatenate.69
  10.3 6.2 all_gather.12
  18.4 5.7 all_gather.13
  26.1 0.9 fusion.10
  27.1 2.0 convolution_add_fusion.hidden0
  29.2 2.1 copy.127
  32.7 2.0 copy.89
  37.9 12.6 %concatenate.68.packed = bf16[8,256,1920]{2,1,0:T(8,128)(2,1)} concatenate(bf16[8,256,1536]{2,1,0:T(8,128)(2,1)} %bitcast.131, bf16[8,256,80]{2,1,0:T(8,128)(2,1)} %bitcast.135, bf16[8,256,1]{2,1,0:T(8,128)(2,1)S(1)} %copy.93, bf16[8,256,1]{2,1,0:T(8,128)(2,1)S(1)} %copy.94, bf16[8,256,46]{2,1,0:T(8,128)(2,1)} %broadcast_in_dim.55, bf16[8,256,256]{2,1,0:T(8,128)(2,1)S(1)} %pad.28), dimensions={2} | concatenate | bytes 15728640 | tf_op jit(solution)/shard_map/concatenate | solution.py:746
  50.5 121.4 %shard_map.278 = (bf16[8,4,256,1920]{3,2,1,0:T(8,128)(2,1)}, bf16[8,512,1664]{2,1,0:T(8,128)(2,1)}, bf16[8,4,3,512,128]{4,3,2,1,0:T(8,128)(2,1)}, f32[512,16]{1,0:T(8,128)}) custom-call(bf16[8,256,1920]{2,1,0:T(8,128)(2,1)} %concatenate.68.packed, f32[512,512]{1,0:T(8,128)} %convolution_add_fusion.hidden0, bf16[512,128]{1,0:T(8,128)(2,1)} %maximum_maximum_fusion.mel, ...), custom_call_target="tpu_custom_call" | custom-call | tf_op jit(solution)/shard_map/pallas_call | solution.py:303
  171.9 1.2 add_add_fusion
  175.9 1.3 copy.103
  177.3 0.9 concatenate.73.og
  178.2 322.8 %shard_map.279 = (bf16[8,256,1920]{2,1,0:T(8,128)(2,1)}, f32[512,512]{1,0:T(8,128)}, f32[512,128]{1,0:T(8,128)}, f32[8,512]{1,0:T(8,128)}) custom-call(bf16[8,4,256,1920]{3,2,1,0:T(8,128)(2,1)} %get-tuple-element.122.weights, bf16[8,512,1664]{2,1,0:T(8,128)(2,1)} %get-tuple-element.123.ext_in, bf16[8,4,3,512,128]{4,3,2,1,0:T(8,128)(2,1)} %get-tuple-element.124.acts_in, ...), custom_call_target="tpu_custom_call" | custom-call | tf_op jit(solution)/shard_map/pallas_call | solution.py:635
  501.0 1.1 slice.340
  502.4 1.0 convolution_bitcast_fusion.2
  503.4 1.8 fusion.35
  505.2 1.3 reduce_sum.49
  506.6 2.2 convolution_add_fusion.1
  508.8 2.4 convolution_bitcast_fusion
  524.5 42.9 %all-reduce.3 = (f32[72]{0:T(128)S(1)}, f32[12,512]{1,0:T(8,128)S(1)}) all-reduce(f32[72]{0:T(128)S(1)} %pad_maximum_fusion.11, f32[12,512]{1,0:T(8,128)S(1)} %pad_maximum_fusion.3), channel_id=1, replica_groups=mesh['dp'=8,'chan'=4] {'dp','chan'}, use_global_device_ids=true, to_apply=%region_5.6 | all-reduce | flops 6216 | bytes 49728 | tf_op jit(solution)/shard_map/psum | solution.py:823
  569.0 1.4 pad_maximum_fusion.10
  570.4 5.8 psum.21
  576.7 5.8 all_gather.14
  585.1 9.3 %slice.381 = f32[8,256,1536]{2,1,0:T(8,128)} slice(bf16[8,256,1920]{2,1,0:T(8,128)(2,1)} %get-tuple-element.128), slice={[0:8], [0:256], [0:1536]} | slice | bytes 25165824 | tf_op jit(solution)/shard_map/slice | solution.py:855
  594.4 2.6 slice.383
  597.0 1.1 slice.379
  603.6 2.9 copy.112
  606.5 2.7 copy.110
  609.6 0.9 copy.115
  610.5 1.2 copy.114
  612.3 5.4 all_gather.15
  619.0 1.3 multiply_add_fusion.1
  (119 shorter events, 30.8 us)
Async XLA Ops:
  7.2 10.7 %copy-start = (bf16[8,512,128]{2,1,0:T(8,128)(2,1)S(1)}, bf16[8,512,128]{2,1,0:T(8,128)(2,1)}, u32[]{:S(2)}) copy-start(bf16[8,512,128]{2,1,0:T(8,128)(2,1)} %param.42) | copy-start | bytes 3145732
  7.2 27.5 %copy-start.8 = (f32[8]{0:T(128)S(1)}, f32[8]{0:T(128)}, u32[]{:S(2)}) copy-start(f32[8]{0:T(128)} %param.45) | copy-start | bytes 100
  7.2 611.8 %reduce-scatter.2.cloned.1.call-start = ((), (), s32[]{:S(2)}) async-start(), calls=%async_computation.1 | async-start | bytes 20480 | tf_op jit(solution)/shard_map/reduce_scatter | solution.py:840
  50.5 124.5 %copy-start.1 = (bf16[8,24,512]{2,1,0:T(8,128)(2,1)S(1)}, bf16[8,24,512]{2,1,0:T(8,128)(2,1)}, u32[]{:S(2)}) copy-start(bf16[8,24,512]{2,1,0:T(8,128)(2,1)} %pad_maximum_fusion) | copy-start | bytes 589828
  500.9 10.2 %copy-start.3 = (f32[8,8]{1,0:T(8,128)S(1)}, f32[8,8]{1,0:T(8,128)}, u32[]{:S(2)}) copy-start(f32[8,8]{1,0:T(8,128)} %param.34) | copy-start | bytes 772
  501.0 23.5 %copy-start.5 = (f32[8,512]{1,0:T(8,128)S(1)}, f32[8,512]{1,0:T(8,128)}, u32[]{:S(2)}) copy-start(f32[8,512]{1,0:T(8,128)} %get-tuple-element.127) | copy-start | bytes 49156
  501.0 67.4 %copy-start.4 = (f32[8,128]{1,0:T(8,128)S(1)}, f32[8,128]{1,0:T(8,128)}, u32[]{:S(2)}) copy-start(f32[8,128]{1,0:T(8,128)} %param.44) | copy-start | bytes 12292
  501.0 82.2 %copy-start.2 = (f32[512,128]{1,0:T(8,128)S(1)}, f32[512,128]{1,0:T(8,128)}, u32[]{:S(2)}) copy-start(f32[512,128]{1,0:T(8,128)} %get-tuple-element.126) | copy-start | bytes 786436
  567.5 51.5 %copy-start.7 = (f32[8]{0:T(128)}, f32[8]{0:T(128)S(1)}, u32[]{:S(2)}) copy-start(f32[8]{0:T(128)S(1)} %slice.342) | copy-start | bytes 100
  597.0 22.0 %copy-start.6 = (f32[128]{0:T(128)S(1)}, f32[128]{0:T(128)}, u32[]{:S(2)}) copy-start(f32[128]{0:T(128)} %param.43) | copy-start | bytes 1540
Sparse Core Ops, SparseCore 0:
  503.5 21.3 reduce-scatter.1

commit v3 on v2

v3 whole, which is shorter than its diff:
```python
import functools

import jax
import jax.numpy as jnp
from jax import lax
from jax.experimental import pallas as pl
from jax.experimental.pallas import tpu as pltpu
from jax.sharding import PartitionSpec as P

CH = 8
HALF = 4
MEL = 80
LAYERS = 8
HOP = 32
FRAMES = 2048
WIDTH = 512
CONV = 1536
EXT = 1664
PACK = 1920
SHARDS = 4
ROWS = 128
BLOCK = FRAMES // SHARDS
PAD = 16
EDGE = 128

HIGH = lax.Precision.HIGHEST
F32 = jnp.float32
BF16 = jnp.bfloat16
MESH = pl.DeviceIdType.MESH
VMEM_LIMIT = 62 << 20


def dot(a, b):
    return jnp.dot(a, b, preferred_element_type=F32)


def dot_nt(a, b):
    return lax.dot_general(a, b, (((1,), (1,)), ((), ())), preferred_element_type=F32)


def dot_tn(a, b):
    return lax.dot_general(a, b, (((0,), (0,)), ((), ())), preferred_element_type=F32)


def when(cond):
    if cond is True:
        return lambda f: f()
    return pl.when(cond)


class Place:
    def __init__(self):
        self.dp = lax.axis_index("dp")
        self.chan = lax.axis_index("chan")
        self.core = self.chan % 2
        self.side = self.chan // 2
        self.bit = self.dp % 2

    def chan_device(self, chan):
        return (self.dp, chan)

    @property
    def core_shard(self):
        return self.side * 2 + 1 - self.core

    @property
    def far_shard(self):
        return (1 - self.side) * 2 + self.core

    @property
    def diag_shard(self):
        return (1 - self.side) * 2 + 1 - self.core

    def dp_bit(self, k):
        return (self.dp // 2**k) % 2

    def dp_device(self, k):
        return (self.dp + 2**k * (1 - 2 * self.dp_bit(k)), self.chan)


def greet(devices):
    barrier = pltpu.get_barrier_semaphore()
    for device in devices:
        pl.semaphore_signal(barrier, inc=1, device_id=device, device_id_type=MESH)
    pl.semaphore_wait(barrier, len(devices))


def remote(src, dst, send, recv, device):
    return pltpu.make_async_remote_copy(
        src_ref=src, dst_ref=dst, send_sem=send, recv_sem=recv, device_id=device, device_id_type=MESH
    )


def levels_of(dp_size):
    levels, rows, bit = [], 2 * ROWS, 0
    while 2**bit < dp_size:
        after = rows // 2 if rows > PAD else rows
        levels.append((bit, rows, after))
        rows, bit = after, bit + 1
    return levels


ACROSS = pl.ds(0, 7 * ROWS)
ALONG = pl.ds(7 * ROWS, PACK - 7 * ROWS)
DEPTH = 4


def mesh_line(levels):
    return len(levels) == 3


def line_shapes():
    a, b = ACROSS.size, ALONG.size
    return [(2, ROWS, a), (ROWS, a), (ROWS // 2, a), (2 * ROWS, b), (ROWS, b), (ROWS // 2, b)]


class Lane:
    def __init__(self, buf, send, recv, credit, device):
        self.buf, self.send, self.recv, self.credit, self.device = buf, send, recv, credit, device

    def copy(self, i, src):
        d = i % DEPTH
        return remote(src, self.buf.at[d], self.send.at[d], self.recv.at[d], self.device)

    def start(self, i, src):
        @pl.when(i >= DEPTH)
        def _():
            self.copy(i, src).wait_send()
            pl.semaphore_wait(self.credit, 1)

        self.copy(i, src).start()

    def wait(self, i):
        d = i % DEPTH
        remote(self.buf.at[d], self.buf.at[d], self.send.at[d], self.recv.at[d], self.device).wait_recv()

    def free(self):
        pl.semaphore_signal(self.credit, inc=1, device_id=self.device, device_id_type=MESH)

    def finish(self):
        for d in range(DEPTH):
            ref = self.buf.at[d]
            remote(ref, ref, self.send.at[d], self.recv.at[d], self.device).wait_send()
            pl.semaphore_wait(self.credit, 1)


def split(values):
    high = values.astype(BF16).astype(F32)
    return high, values - high


def flow_kernel(
    levels,
    in_weight, cond_weight, res_weight, skip_weight, audio, mel, inv_weight, local_small, end_bias,
    total, weights_out, ext_out, acts_out, frames_out, mel_out, sums_out, inverse_out, log_out, small, end_out,
    mine_out, end_own_out,
    shared, hid, ext, acts, top, bottom, wbuf, low, low_t, tap0, tap2, grad, mel_sum, edge_out, edge_in,
    fold, keep, og_rows, out, small_in, end_in, *rest,
):
    line = mesh_line(levels)
    n_bufs = len(line_shapes()) if line else len(levels)
    level_bufs = rest[:n_bufs]
    (
        own_sem, send, recv, keep_sem, ext_sem, acts_sem,
        top_send, top_recv, bottom_send, bottom_recv,
        small_send, small_recv, fold_send, fold_recv,
        phase, w_sem, core_send, core_recv, credit, far_send, far_recv,
        rs_send, rs_recv, ag_send, ag_recv, out_sem, edge_send, edge_recv,
        sum_send, sum_recv, end_send, end_recv, frames_send, frames_recv, mel_send, mel_recv,
        lane_send, lane_recv, lane_credit, way_send, way_recv,
    ) = rest[n_bufs:]
    me = Place()
    core_dev = me.chan_device(me.core_shard)
    far_dev = me.chan_device(me.far_shard)
    diag_dev = me.chan_device(me.diag_shard)
    chan_devs = [core_dev, far_dev, diag_dev]
    has_prev = me.chan > 0
    has_next = me.chan < SHARDS - 1
    prev_dev = me.chan_device(jnp.maximum(me.chan - 1, 0))
    next_dev = me.chan_device(jnp.minimum(me.chan + 1, SHARDS - 1))

    quarter = ROWS // 2
    xb, zb = me.dp_bit(0), me.dp_bit(1)

    def quarter_at(x, z, first=0, rows=quarter):
        return pl.ds(pl.multiple_of((x * 2 + z) * quarter + first, 32), rows)

    half_quarter = quarter // 2

    def own_copies(l):
        dst = shared.at[l * SHARDS + me.chan]
        return [
            pltpu.make_async_copy(in_weight.at[l], dst.at[:, pl.ds(0, CONV)], own_sem.at[0, l]),
            pltpu.make_async_copy(cond_weight.at[l], dst.at[:, pl.ds(CONV, ROWS)], own_sem.at[1, l]),
        ]

    def res_copies(l):
        dst = shared.at[l * SHARDS + me.chan]
        return [
            pltpu.make_async_copy(
                res_weight.at[l, pl.ds(h * 2 * ROWS, 2 * ROWS)],
                dst.at[:, pl.ds(EXT + h * ROWS, ROWS)],
                own_sem.at[2 + h, l],
            )
            for h in range(2)
        ]

    def link(kind, l, shard, at, device):
        ref = shared.at[l * SHARDS + shard, at] if at is not None else shared.at[l * SHARDS + shard]
        return remote(ref, ref, send.at[kind, l], recv.at[kind, l], device)

    x_dev, z_dev = me.dp_device(0), me.dp_device(1)

    def far_a(l, shard):
        return link(0, l, shard, quarter_at(xb, zb), far_dev)

    def far_b(l, shard):
        return link(1, l, shard, quarter_at(1 - xb, 1 - zb, 0, half_quarter), far_dev)

    def x_a(l, x):
        return link(2, l, me.far_shard, quarter_at(x, zb), x_dev)

    def z_a(l, z):
        return link(3, l, me.far_shard, quarter_at(xb, z), z_dev)

    def x_b(l, x):
        return link(4, l, me.far_shard, quarter_at(x, 1 - zb, half_quarter, half_quarter), x_dev)

    def core_a(l, shard):
        return link(5, l, shard, None, core_dev)

    def core_b(l, shard):
        return link(6, l, shard, None, core_dev)

    def issue(l):
        for copy in own_copies(l):
            copy.wait()

        @pl.when(l < LAYERS - 1)
        def _():
            for copy in res_copies(l):
                copy.wait()

        far_a(l, me.chan).start()
        far_b(l, me.chan).start()
        core_a(l, me.chan).start()

    def relay_a(l):
        far_a(l, me.far_shard).wait_recv()
        x_a(l, xb).start()
        z_a(l, zb).start()
        pl.when(l + 1 < LAYERS)(lambda: issue(l + 1))

    def relay_b(l):
        z_a(l, 1 - zb).wait_recv()
        x_b(l, xb).start()

    def relay_c(l):
        far_b(l, me.far_shard).wait_recv()
        x_a(l, 1 - xb).wait_recv()
        x_b(l, 1 - xb).wait_recv()
        core_b(l, me.far_shard).start()

    def arrive(l):
        core_a(l, me.core_shard).wait_recv()
        core_b(l, me.diag_shard).wait_recv()

    shared[(LAYERS - 1) * SHARDS + me.chan, :, EXT:] = jnp.zeros((2 * ROWS, 2 * ROWS), BF16)

    def first_copies(l, carry):
        for copy in own_copies(l):
            copy.start()

        @pl.when(l < LAYERS - 1)
        def _():
            for copy in res_copies(l):
                copy.start()

        return carry

    lax.fori_loop(0, LAYERS, first_copies, 0)

    @pl.when(jnp.logical_not(has_prev))
    def _():
        top[...] = jnp.zeros_like(top)

    @pl.when(jnp.logical_not(has_next))
    def _():
        bottom[...] = jnp.zeros_like(bottom)

    edge_in[...] = jnp.zeros_like(edge_in)
    opp_dev = (6 + 2 * xb - me.dp, me.chan) if line else None
    greet(chan_devs + [me.dp_device(bit) for bit, _, _ in levels] + ([opp_dev] if line else []))

    def small_copy(k):
        return remote(local_small, small.at[me.chan], small_send.at[k], small_recv.at[k], chan_devs[k])

    def fold_copy(k):
        return remote(fold.at[me.chan], fold.at[me.chan], fold_send.at[k], fold_recv.at[k], chan_devs[k])

    issue(0)
    for k in range(3):
        small_copy(k).start()
    small[me.chan] = local_small[...]

    rows8 = lax.broadcasted_iota(jnp.int32, (CH, BLOCK), 0)
    mixed = jnp.zeros((CH, BLOCK), F32)
    for j in range(CH):
        mixed = mixed + inv_weight[:, j : j + 1] * audio[j : j + 1, :]
    first_ext = jnp.where(rows8 < HALF, mixed, jnp.where(rows8 == HALF, 1.0, 0.0))
    keep[0] = mixed
    keep[1] = first_ext
    for r in range(BLOCK // HOP):
        row = jnp.broadcast_to(mel[r : r + 1, :], (HOP, ROWS)).astype(BF16)
        for slot in range(2):
            ext[slot, pl.ds(r * HOP, HOP), CONV:] = row
    out[...] = jnp.zeros_like(out)
    for k in range(3):
        small_copy(k).wait_recv()

    def small_row(lo, hi):
        return jnp.concatenate([small[s, lo:hi, :] for s in range(SHARDS)], axis=1)

    start_ext = jnp.where(rows8 <= HALF, small_row(0, 8), 0.0)
    keep[2] = start_ext
    hid[pl.ds(PAD, BLOCK), :] = lax.dot_general(
        first_ext, start_ext, (((0,), (0,)), ((), ())), precision=HIGH, preferred_element_type=F32
    )
    final = small_row(16, 24)
    final_high, final_low = split(final)
    final_rows = jnp.concatenate([final_high, final_low], axis=0).astype(BF16)
    for l in range(LAYERS):
        both = dot(final_rows, skip_weight[l])
        high, rest_of = split(both[:CH] + both[CH:])
        fold[me.chan, l] = jnp.concatenate([high, rest_of, high, jnp.zeros_like(high)], axis=0).astype(BF16)
    for k in range(3):
        fold_copy(k).start()
    skip_bias = small_row(13, 14)
    const = jnp.sum(final * skip_bias, axis=1, keepdims=True) + end_bias[...]

    aug = jnp.concatenate(
        [
            inv_weight[...],
            jnp.where(
                lax.broadcasted_iota(jnp.int32, (CH, CH), 0) == lax.broadcasted_iota(jnp.int32, (CH, CH), 1), 1.0, 0.0
            ),
        ],
        axis=1,
    )
    aug_rows = lax.broadcasted_iota(jnp.int32, (CH, 2 * CH), 0)
    log_total = jnp.zeros((1, 1), F32)
    for c in range(CH):
        pivot = aug[c : c + 1, c : c + 1]
        log_total = log_total + jnp.log(pivot)
        pivot_row = aug[c : c + 1, :] / pivot
        aug = jnp.where(aug_rows == c, pivot_row, aug - aug[:, c : c + 1] * pivot_row)
    inverse_out[...] = aug
    log_out[...] = jnp.broadcast_to(log_total, log_out.shape)

    def ext_copy(l):
        return pltpu.make_async_copy(ext.at[l % 2], ext_out.at[l], ext_sem.at[l % 2])

    def acts_copy(l):
        return pltpu.make_async_copy(acts.at[l % 2], acts_out.at[l], acts_sem.at[l % 2])

    def keep_copy(l):
        return pltpu.make_async_copy(
            shared.at[pl.ds(l * SHARDS, SHARDS)], weights_out.at[l], keep_sem.at[l]
        )

    def to_next(l, rows):
        p = l % 2
        return remote(
            ext.at[p, pl.ds(BLOCK - rows, rows), pl.ds(WIDTH, WIDTH)],
            top.at[p, pl.ds(EDGE - rows, rows)],
            top_send.at[p], top_recv.at[p], next_dev,
        )

    def to_prev(l, rows):
        p = l % 2
        return remote(
            ext.at[p, pl.ds(0, rows), pl.ds(WIDTH, WIDTH)],
            bottom.at[p, pl.ds(0, rows)],
            bottom_send.at[p], bottom_recv.at[p], prev_dev,
        )

    def by_edge(l, f):
        pl.when(l <= 4)(lambda: f(PAD))
        pl.when(l > 4)(lambda: f(EDGE))

    def forward(l, carry):
        p = l % 2
        pl.when(l + 1 < LAYERS)(lambda: relay_a(l + 1))
        relay_c(l)
        arrive(l)
        keep_copy(l).start()

        @pl.when(l >= 2)
        def _():
            ext_copy(l - 2).wait()
            acts_copy(l - 2).wait()

        ext[p, :, WIDTH : 2 * WIDTH] = hid[pl.ds(PAD, BLOCK), :].astype(BF16)

        def start(rows):
            pl.when(has_next)(lambda: to_next(l, rows).start())
            pl.when(has_prev)(lambda: to_prev(l, rows).start())

        def finish(rows):
            @pl.when(has_next)
            def _():
                to_next(l, rows).wait_send()
                to_prev(l, rows).wait_recv()

            @pl.when(has_prev)
            def _():
                to_prev(l, rows).wait_send()
                to_next(l, rows).wait_recv()

        by_edge(l, start)
        by_edge(l, finish)
        hid[pl.ds(0, PAD), :] = top[p, pl.ds(EDGE - PAD, PAD), :].astype(F32)
        hid[pl.ds(PAD + BLOCK, PAD), :] = bottom[p, pl.ds(0, PAD), :].astype(F32)
        for layer in range(LAYERS):
            d = 2**layer

            @pl.when(l == layer)
            def _():
                if d < PAD:
                    ext[p, :, :WIDTH] = hid[pl.ds(PAD - d, BLOCK), :].astype(BF16)
                    ext[p, :, 2 * WIDTH : CONV] = hid[pl.ds(PAD + d, BLOCK), :].astype(BF16)
                else:
                    ext[p, :d, :WIDTH] = top[p, EDGE - d :, :]
                    ext[p, d:, :WIDTH] = ext[p, : BLOCK - d, WIDTH : 2 * WIDTH]
                    ext[p, BLOCK - d :, 2 * WIDTH : CONV] = bottom[p, :d, :]
                    ext[p, : BLOCK - d, 2 * WIDTH : CONV] = ext[p, d:, WIDTH : 2 * WIDTH]

        ext_copy(l).start()

        def one(s, carry):
            pre = dot_nt(ext[p], shared[l * SHARDS + s, :, :EXT])
            t = jnp.tanh(pre[:, :ROWS])
            g = 0.5 * jnp.tanh(0.5 * pre[:, ROWS:]) + 0.5
            tg = t * g
            acts[p, s, 0] = tg.astype(BF16)
            acts[p, s, 1] = (g - t * tg).astype(BF16)
            acts[p, s, 2] = (tg * (1.0 - g)).astype(BF16)
            pl.when((s == 1) & (l + 1 < LAYERS))(lambda: relay_b(l + 1))
            return carry

        lax.fori_loop(0, SHARDS, one, 0)
        acts_copy(l).start()

        @pl.when(l == 0)
        def _():
            for k in range(3):
                fold_copy(k).wait_recv()

        gated = jnp.concatenate([acts[p, s, 0] for s in range(SHARDS)], axis=1)
        out[...] += dot_nt(jnp.concatenate([fold[s, l, : 2 * CH, :] for s in range(SHARDS)], axis=1), gated)

        @pl.when(l < LAYERS - 1)
        def _():
            for h in range(2):
                res = jnp.concatenate(
                    [shared[l * SHARDS + s, :, EXT + h * ROWS : EXT + (h + 1) * ROWS] for s in range(SHARDS)], axis=1
                )
                bias = jnp.concatenate([small[s, pl.ds(5 + l, 1), :] for s in (2 * h, 2 * h + 1)], axis=1)
                cols = slice(h * 2 * ROWS, (h + 1) * 2 * ROWS)
                hid[pl.ds(PAD, BLOCK), cols] += dot_nt(gated, res) + bias

        return carry

    relay_a(0)
    relay_b(0)
    lax.fori_loop(0, LAYERS, forward, 0)

    both = out[...]
    output = both[:CH] + both[CH:] + const
    log_scale, shift = output[:HALF], output[HALF:]
    scale = jnp.exp(log_scale)
    mixed = keep[0]
    second = mixed[HALF:]
    second_out = scale * second + shift
    mine = pl.ds(pl.multiple_of(me.chan * BLOCK, BLOCK), BLOCK)
    frames_out[0:CH, mine] = jnp.concatenate([mixed[:HALF], second_out], axis=0)
    frames_out[2 * CH : 3 * CH, mine] = jnp.concatenate([log_scale, jnp.zeros_like(log_scale)], axis=0)
    out_grad = jnp.concatenate([second_out * scale * second - 1.0, second_out], axis=0)
    keep[3] = jnp.concatenate([jnp.zeros_like(scale), second_out * scale], axis=0)
    og_high, og_low = split(out_grad)
    og_rows[...] = jnp.concatenate([og_high, og_low], axis=0).astype(BF16)
    og_stack = jnp.concatenate([og_high, og_high, og_low, jnp.zeros((ROWS - 3 * CH, BLOCK), F32)], axis=0)
    low[:, WIDTH:] = og_stack.T.astype(BF16)
    end_sum = jnp.sum(out_grad, axis=1, keepdims=True)
    grad[...] = jnp.zeros_like(grad)
    mel_sum[...] = jnp.zeros_like(mel_sum)

    def drain_forward(l, carry):
        far_a(l, me.chan).wait_send()
        far_b(l, me.chan).wait_send()
        x_a(l, xb).wait_send()
        z_a(l, zb).wait_send()
        x_b(l, xb).wait_send()
        core_a(l, me.chan).wait_send()
        core_b(l, me.far_shard).wait_send()
        keep_copy(l).wait()
        return carry

    lax.fori_loop(0, LAYERS, drain_forward, 0)
    for l in (LAYERS - 2, LAYERS - 1):
        ext_copy(l).wait()
        acts_copy(l).wait()
    for k in range(3):
        small_copy(k).wait_send()
        fold_copy(k).wait_send()
    pl.semaphore_signal(phase.at[0], inc=1, device_id=core_dev, device_id_type=MESH)
    pl.semaphore_signal(phase.at[1], inc=1, device_id=far_dev, device_id_type=MESH)

    def shard_of(j):
        core = jnp.where(j < 2, 1 - me.core, me.core)
        return (j % 2) * 2 + core

    def w_copy(q):
        l, s = LAYERS - 1 - q // SHARDS, shard_of(q % SHARDS)
        return pltpu.make_async_copy(weights_out.at[l, s], wbuf.at[q % 2], w_sem.at[q % 2])

    def ext_back(l):
        return pltpu.make_async_copy(ext_out.at[l], ext.at[l % 2], ext_sem.at[l % 2])

    def acts_back(l):
        return pltpu.make_async_copy(acts_out.at[l], acts.at[l % 2], acts_sem.at[l % 2])

    def kept(i, ys):
        return 4 + 2 * i + ys

    def got_core(i, ys):
        return 20 + 2 * (i % 2) + ys

    def to_core(i, ys):
        p = i % 2
        return remote(
            shared.at[2 * p + ys], shared.at[got_core(i, ys)], core_send.at[p, ys], core_recv.at[p, ys], core_dev
        )

    def to_far(i):
        return remote(shared.at[kept(i, 1 - me.side)], shared.at[24 + i], far_send.at[i], far_recv.at[i], far_dev)

    def add_rows(block, base, rows, src, src_at):
        chunk = min(rows, 32)

        def body(k, carry):
            at = pl.ds(pl.multiple_of(base + k * chunk, PAD), chunk)
            shared[block, at, :] = shared[block, at, :] + src[src_at, pl.ds(pl.multiple_of(k * chunk, PAD), chunk), :]
            return carry

        lax.fori_loop(0, rows // chunk, body, 0)

    base_at = [0]
    for bit, rows, after in levels:
        base_at.append(base_at[-1] + (me.dp_bit(bit) * after if after < rows else 0))

    def rs(k, i):
        bit, rows, after = levels[k]
        first = base_at[k] + ((1 - me.dp_bit(bit)) * after if after < rows else 0)
        at = pl.ds(pl.multiple_of(first, PAD), after)
        return remote(
            shared.at[kept(i, me.side), at], level_bufs[k].at[i], rs_send.at[k, i], rs_recv.at[k, i], me.dp_device(bit)
        )

    def ag(k, i, arriving):
        bit, rows, after = levels[k]
        first = base_at[k] + (1 - me.dp_bit(bit)) * after if arriving else base_at[k + 1]
        ref = total.at[LAYERS - 1 - i, pl.ds(pl.multiple_of(first, PAD), after)]
        return remote(ref, ref, ag_send.at[k, i], ag_recv.at[k, i], me.dp_device(bit))

    halving = [k for k, (bit, rows, after) in enumerate(levels) if after < rows]

    def out_copy(i):
        at = pl.ds(pl.multiple_of(base_at[-1], PAD), levels[-1][2])
        return pltpu.make_async_copy(shared.at[kept(i, me.side), at], total.at[LAYERS - 1 - i, at], out_sem.at[0, i])

    def stage_core(i):
        for ys in (1 - me.side, me.side):
            to_core(i, ys).wait_recv()
            add_rows(kept(i, ys), 0, 2 * ROWS, shared, got_core(i, ys))
            pl.semaphore_signal(credit.at[ys], inc=1, device_id=core_dev, device_id_type=MESH)
            if ys is not me.side:
                pl.when(i == 0)(lambda: pl.semaphore_wait(phase.at[1], 1))
                if not line:
                    to_far(i).start()
        if line:
            start_ways(i)

    def stage_far(i):
        to_far(i).wait_recv()
        add_rows(kept(i, me.side), 0, 2 * ROWS, shared, 24 + i)
        rs(0, i).start()

    def stage_rs(k, i):
        bit, rows, after = levels[k]
        rs(k, i).wait_recv()
        if after == rows:
            rs(k, i).wait_send()
        add_rows(kept(i, me.side), base_at[k + 1], after, level_bufs[k], i)
        if k + 1 < len(levels):
            rs(k + 1, i).start()
        else:
            out_copy(i).start()
            out_copy(i).wait()
            ag(halving[-1], i, False).start()

    def stage_ag(n, i):
        ag(halving[n], i, True).wait_recv()
        if n > 0:
            ag(halving[n - 1], i, False).start()

    def add_block(block, base, rows, cols, src, src_base=0):
        chunk = min(rows, 64)

        def body(k, carry):
            at = pl.ds(pl.multiple_of(base + k * chunk, 64), chunk)
            got = src[pl.ds(pl.multiple_of(src_base + k * chunk, 64), chunk), :]
            shared[block, at, cols] = shared[block, at, cols] + got
            return carry

        lax.fori_loop(0, rows // chunk, body, 0)

    def rows_at(first, rows):
        return pl.ds(pl.multiple_of(first, 64), rows)

    if line:
        zc = me.dp // 2
        inner = (zc == 1) | (zc == 2)
        edge = jnp.logical_not(inner)
        hb = jnp.where(zc == 2, 1, 0)
        lane_devs = [x_dev, z_dev, opp_dev, z_dev, opp_dev, x_dev]
        lanes = [
            Lane(level_bufs[k], lane_send.at[k], lane_recv.at[k], lane_credit.at[k], lane_devs[k]) for k in range(6)
        ]
        qx, q1, q2, r1, r2, rx = lanes
        half = ROWS
        mine_x, mine_x2 = xb * half, xb * half + hb * (half // 2)
        r_base, r_base2 = hb * half, hb * half + xb * (half // 2)

        def far_way(k, i, rows, cols):
            return remote(
                shared.at[kept(i, 1 - me.side), rows, cols], shared.at[24 + i, rows, cols],
                way_send.at[k, i], way_recv.at[k, i], far_dev,
            )

        def far_q(i):
            return far_way(0, i, rows_at(mine_x, half), ACROSS)

        def far_r(i):
            return far_way(1, i, pl.ds(0, 2 * ROWS), ALONG)

        def total_way(k, i, rows, cols, device, src=None):
            ref = total.at[LAYERS - 1 - i, rows, cols]
            return remote(ref if src is None else src, ref, way_send.at[k, i], way_recv.at[k, i], device)

        def own_part(k, i, rows, cols):
            return pltpu.make_async_copy(
                shared.at[kept(i, me.side), rows, cols], total.at[LAYERS - 1 - i, rows, cols], out_sem.at[k, i]
            )

        def q_inner(i, b):
            rows = rows_at(mine_x + b * (half // 2), half // 2)
            return total_way(2, i, rows, ACROSS, opp_dev, shared.at[kept(i, me.side), rows, ACROSS])

        def q_edge(i):
            return total_way(3, i, rows_at(mine_x, half), ACROSS, z_dev)

        def q_x(i, x):
            return total_way(4, i, rows_at(x * half, half), ACROSS, x_dev)

        def r_x(i, x):
            rows = rows_at(r_base + x * (half // 2), half // 2)
            return total_way(5, i, rows, ALONG, x_dev, shared.at[kept(i, me.side), rows, ALONG])

        def r_inner(i, b):
            return total_way(6, i, rows_at(b * half, half), ALONG, opp_dev)

        def r_edge(i):
            return total_way(7, i, pl.ds(0, 2 * ROWS), ALONG, z_dev)

        def q_out(i):
            return own_part(0, i, rows_at(mine_x2, half // 2), ACROSS)

        def r_out(i):
            return own_part(1, i, rows_at(r_base2, half // 2), ALONG)

        def own_ref(i, first, rows, cols):
            return shared.at[kept(i, me.side), rows_at(first, rows), cols]

        def start_ways(i):
            far_r(i).start()
            qx.start(i, shared.at[pl.ds(kept(i, 0), 2), rows_at((1 - xb) * half, half), ACROSS])

        def q_stage1(i):
            qx.wait(i)
            for ys in (1 - me.side, me.side):
                add_block(kept(i, ys), mine_x, half, ACROSS, qx.buf.at[i % DEPTH, ys])
                if ys is not me.side:
                    far_q(i).start()
            qx.free()

        def r_stage1(i):
            far_r(i).wait_recv()
            add_block(kept(i, me.side), 0, 2 * ROWS, ALONG, shared.at[24 + i, :, ALONG])
            pl.when(edge)(lambda: r1.start(i, own_ref(i, 0, 2 * ROWS, ALONG)))

        def q_stage2(i):
            far_q(i).wait_recv()
            add_block(kept(i, me.side), mine_x, half, ACROSS, shared.at[24 + i, :, ACROSS], mine_x)
            pl.when(edge)(lambda: q1.start(i, own_ref(i, mine_x, half, ACROSS)))

        def r_stage2(i):
            @pl.when(inner)
            def _():
                r1.wait(i)
                add_block(kept(i, me.side), 0, 2 * ROWS, ALONG, r1.buf.at[i % DEPTH])
                r1.free()
                r2.start(i, own_ref(i, (1 - hb) * half, half, ALONG))

        def q_stage3(i):
            @pl.when(inner)
            def _():
                q1.wait(i)
                add_block(kept(i, me.side), mine_x, half, ACROSS, q1.buf.at[i % DEPTH])
                q1.free()
                q2.start(i, own_ref(i, mine_x + (1 - hb) * (half // 2), half // 2, ACROSS))

        def r_stage3(i):
            @pl.when(inner)
            def _():
                r2.wait(i)
                add_block(kept(i, me.side), r_base, half, ALONG, r2.buf.at[i % DEPTH])
                r2.free()
                rx.start(i, own_ref(i, r_base + (1 - xb) * (half // 2), half // 2, ALONG))

        def q_stage4(i):
            @pl.when(inner)
            def _():
                q2.wait(i)
                add_block(kept(i, me.side), mine_x2, half // 2, ACROSS, q2.buf.at[i % DEPTH])
                q2.free()
                q_inner(i, hb).start()
                q_out(i).start()

        def r_stage4(i):
            @pl.when(inner)
            def _():
                rx.wait(i)
                add_block(kept(i, me.side), r_base2, half // 2, ALONG, rx.buf.at[i % DEPTH])
                rx.free()
                r_x(i, xb).start()
                r_out(i).start()

        def q_stage5(i):
            @pl.when(inner)
            def _():
                q_out(i).wait()
                q_inner(i, 1 - hb).wait_recv()
                q_edge(i).start()
                q_x(i, xb).start()

        def r_stage5(i):
            @pl.when(inner)
            def _():
                r_out(i).wait()
                r_x(i, 1 - xb).wait_recv()
                r_inner(i, hb).start()

        def q_stage6(i):
            @pl.when(edge)
            def _():
                q_edge(i).wait_recv()
                q_x(i, xb).start()

        def r_stage6(i):
            @pl.when(inner)
            def _():
                r_inner(i, 1 - hb).wait_recv()
                r_edge(i).start()

        def q_stage7(i):
            q_x(i, 1 - xb).wait_recv()

        def r_stage7(i):
            pl.when(edge)(lambda: r_edge(i).wait_recv())

        def drain_ways(i, carry):
            far_q(i).wait_send()
            far_r(i).wait_send()
            q_x(i, xb).wait_send()

            @pl.when(inner)
            def _():
                q_inner(i, hb).wait_send()
                q_edge(i).wait_send()
                r_x(i, xb).wait_send()
                r_inner(i, hb).wait_send()
                r_edge(i).wait_send()

            return carry

        def finish_lanes():
            qx.finish()

            @pl.when(edge)
            def _():
                q1.finish()
                r1.finish()

            @pl.when(inner)
            def _():
                q2.finish()
                r2.finish()
                rx.finish()

        line_stages = [
            [q_stage1, r_stage1], [q_stage2, r_stage2], [q_stage3, r_stage3], [q_stage4, r_stage4],
            [q_stage5, r_stage5], [q_stage6, r_stage6], [q_stage7, r_stage7],
        ]

    def back_prev(i, rows):
        return remote(
            edge_out.at[0, pl.ds(0, rows)], edge_in.at[i % 2, 0, pl.ds(0, rows)],
            edge_send.at[0], edge_recv.at[i % 2, 0], prev_dev,
        )

    def back_next(i, rows):
        return remote(
            edge_out.at[1, pl.ds(EDGE - rows, rows)], edge_in.at[i % 2, 1, pl.ds(EDGE - rows, rows)],
            edge_send.at[1], edge_recv.at[i % 2, 1], next_dev,
        )

    def backward(i):
        l = LAYERS - 1 - i
        p = l % 2
        now = grad[...].astype(BF16)
        low[:, :WIDTH] = now
        low_t[...] = now.T
        sums_out[pl.ds(72 + l, 1), :] = jnp.sum(now.astype(F32), axis=0, keepdims=True)
        tap0[pl.ds(0, BLOCK), :] = jnp.zeros((BLOCK, WIDTH), F32)
        tap2[pl.ds(EDGE, BLOCK), :] = jnp.zeros((BLOCK, WIDTH), F32)

        @pl.when(i >= 2)
        def _():
            ext_back(l).wait()
            acts_back(l).wait()

        def one(j, carry):
            q = i * SHARDS + j
            b = q % 2
            s = shard_of(j)
            pl.when(q + 1 < LAYERS * SHARDS)(lambda: w_copy(q + 1).start())

            @pl.when((j < 2) & (i >= 2))
            def _():
                to_core(i - 2, j).wait_send()

            w_copy(q).wait()
            slot = jnp.where(j < 2, 2 * (i % 2) + j, kept(i, j - 2))
            gated = acts[p, s, 0]
            res = jnp.concatenate([wbuf[b, :, EXT : EXT + ROWS], wbuf[b, :, EXT + ROWS :]], axis=0)
            back = dot(low[:, :WIDTH], res) + dot(low[:, WIDTH : WIDTH + 4 * CH], fold[s, l])
            pg = jnp.concatenate(
                [(back * acts[p, s, 1].astype(F32)).astype(BF16), (back * acts[p, s, 2].astype(F32)).astype(BF16)],
                axis=1,
            )
            tap0[pl.ds(0, BLOCK), :] += dot(pg, wbuf[b, :, :WIDTH])
            grad[...] += dot(pg, wbuf[b, :, WIDTH : 2 * WIDTH])
            tap2[pl.ds(EDGE, BLOCK), :] += dot(pg, wbuf[b, :, 2 * WIDTH : CONV])
            mel_sum[...] += dot(pg, wbuf[b, :, CONV:EXT])
            for k in range(3):
                cols = slice(k * WIDTH, (k + 1) * WIDTH)
                shared[slot, :, cols] = dot_tn(pg, ext[p, :, cols]).astype(BF16)
            shared[slot, :, CONV:EXT] = dot_tn(pg, ext[p, :, CONV:]).astype(BF16)
            side = dot(low_t[...], gated).astype(BF16)
            shared[slot, :, EXT : EXT + ROWS] = side[: 2 * ROWS]
            shared[slot, :, EXT + ROWS :] = side[2 * ROWS :]
            e = dot(og_rows[...], gated)
            sums_out[pl.ds(pl.multiple_of(l * CH, CH), CH), pl.ds(pl.multiple_of(s * ROWS, ROWS), ROWS)] = e[:CH] + e[CH:]

            @pl.when(j < 2)
            def _():
                pl.when(q == 0)(lambda: pl.semaphore_wait(phase.at[0], 1))
                pl.when(i >= 2)(lambda: pl.semaphore_wait(credit.at[j], 1))
                to_core(i, j).start()

            return carry

        lax.fori_loop(0, SHARDS, one, 0)

        @pl.when(l >= 2)
        def _():
            ext_back(l - 2).start()
            acts_back(l - 2).start()

        edge_out[0] = tap0[pl.ds(0, EDGE), :].astype(BF16)
        edge_out[1] = tap2[pl.ds(BLOCK, EDGE), :].astype(BF16)

        def start(rows):
            pl.when(has_next)(lambda: back_next(i, rows).start())
            pl.when(has_prev)(lambda: back_prev(i, rows).start())

        def finish(rows):
            @pl.when(has_next)
            def _():
                back_next(i, rows).wait_send()
                back_prev(i, rows).wait_recv()

            @pl.when(has_prev)
            def _():
                back_prev(i, rows).wait_send()
                back_next(i, rows).wait_recv()

        by_edge(l, start)
        by_edge(l, finish)
        tap0[pl.ds(BLOCK, EDGE), :] = edge_in[i % 2, 0].astype(F32)
        tap2[pl.ds(0, EDGE), :] = edge_in[i % 2, 1].astype(F32)
        for layer in range(LAYERS):
            d = 2**layer

            @pl.when(l == layer)
            def _():
                grad[...] += tap0[pl.ds(d, BLOCK), :] + tap2[pl.ds(EDGE - d, BLOCK), :]

    sum_devs = [core_dev, far_dev] + [me.dp_device(bit) for bit, _, _ in levels]

    def sum_copy(k):
        return remote(sums_out, small_in.at[k], sum_send.at[k], sum_recv.at[k], sum_devs[k])

    def end_copy(k):
        return remote(end_out, end_in.at[k], end_send.at[k], end_recv.at[k], sum_devs[k])

    def frames_copy(k):
        ref = frames_out.at[:, mine]
        return remote(ref, ref, frames_send.at[k], frames_recv.at[k], chan_devs[k])

    mel_rows = BLOCK // HOP

    def mel_copy(k):
        ref = mel_out.at[pl.ds(pl.multiple_of(me.chan * mel_rows, mel_rows), mel_rows)]
        return remote(ref, ref, mel_send.at[k], mel_recv.at[k], chan_devs[k])

    def last(values, other, dims):
        return lax.dot_general(values, other, (dims, ((), ())), precision=HIGH, preferred_element_type=F32)

    def finish_frames():
        hidden_grad = grad[...]
        sums_out[64:72, :] = last(keep[1], hidden_grad, ((1,), (0,)))
        mixed = keep[0]
        first_back = last(keep[2], hidden_grad, ((1,), (1,)))
        rows = lax.broadcasted_iota(jnp.int32, (CH, BLOCK), 0)
        mixed_grad = jnp.where(rows < HALF, mixed + first_back, keep[3])
        frames_out[CH : 2 * CH, mine] = last(inv_weight[...], mixed_grad, ((0,), (0,)))
        inv_part = last(mixed_grad, audio[...], ((1,), (1,)))
        sums_out[80:88, :] = jnp.concatenate([inv_part, end_sum, jnp.zeros((CH, WIDTH - CH - 1), F32)], axis=1)
        mel_out[pl.ds(pl.multiple_of(me.chan * mel_rows, mel_rows), mel_rows), :] = jnp.sum(
            mel_sum[...].reshape(mel_rows, HOP, ROWS), axis=1
        )
        for k in range(3):
            frames_copy(k).start()
            mel_copy(k).start()
        sum_copy(0).start()

    def sum_stage(k):
        sum_copy(k).wait_recv()
        sum_copy(k).wait_send()
        sums_out[...] = sums_out[...] + small_in[k]
        if k + 1 < len(sum_devs):
            sum_copy(k + 1).start()
            return
        e = sums_out[0:64, pl.ds(pl.multiple_of(me.chan * ROWS, ROWS), ROWS)]
        e_high, e_low = split(e)
        end = jnp.zeros((2 * CH, WIDTH), F32)
        for l in range(LAYERS):
            part = slice(l * CH, (l + 1) * CH)
            end = end + dot_nt(jnp.concatenate([e_high[part], e_low[part]], axis=0).astype(BF16), skip_weight[l])
        end_out[...] = end[:CH] + end[CH:]
        end_copy(0).start()

    def end_stage(k):
        end_copy(k).wait_recv()
        end_copy(k).wait_send()
        end_out[...] = end_out[...] + end_in[k]
        if k == 0:
            end_copy(1).start()

    small_stages = [finish_frames]
    small_stages += [functools.partial(sum_stage, k) for k in range(len(sum_devs))]
    small_stages += [functools.partial(end_stage, k) for k in range(2)]

    if line:
        stages = [[stage_core]] + line_stages
    else:
        stages = [[stage_core], [stage_far]]
        stages += [[functools.partial(stage_rs, k)] for k in range(len(levels))]
        stages += [[functools.partial(stage_ag, n)] for n in range(len(halving) - 1, -1, -1)]
    steps = LAYERS - 1 + max(len(stages), len(small_stages))

    w_copy(0).start()

    def step(i, carry):
        @pl.when(i < LAYERS)
        def _():
            backward(i)
            stage_core(i)

        for k, stage in enumerate(small_stages):
            pl.when(i == LAYERS - 1 + k)(stage)
        for lag in range(len(stages) - 1, 0, -1):

            @pl.when((i >= lag) & (i < LAYERS + lag))
            def _():
                for stage in stages[lag]:
                    stage(i - lag)

        return carry

    lax.fori_loop(0, steps, step, 0)

    for i in (LAYERS - 2, LAYERS - 1):
        for ys in range(2):
            to_core(i, ys).wait_send()
            pl.semaphore_wait(credit.at[ys], 1)

    def drain(i, carry):
        to_far(i).wait_send()
        for k, (bit, rows, after) in enumerate(levels):
            if after < rows:
                rs(k, i).wait_send()
                ag(k, i, False).wait_send()
        return carry

    if line:
        lax.fori_loop(0, LAYERS, drain_ways, 0)
        finish_lanes()
    else:
        lax.fori_loop(0, LAYERS, drain, 0)
    for k, shard in enumerate([me.core_shard, me.far_shard, me.diag_shard]):
        frames_copy(k).wait_send()
        mel_copy(k).wait_send()
        frames_copy(k).wait_recv()
        mel_copy(k).wait_recv()
    own_lanes = pl.ds(pl.multiple_of(me.chan * ROWS, ROWS), ROWS)
    mine_out[...] = sums_out[:, own_lanes]
    end_own_out[...] = end_out[:, own_lanes]


def run_flow(dp_size, *args):
    levels = levels_of(dp_size)
    vmem = pl.BlockSpec(memory_space=pltpu.VMEM)
    hbm = pl.BlockSpec(memory_space=pl.ANY)
    dma = pltpu.SemaphoreType.DMA
    regular = pltpu.SemaphoreType.REGULAR
    block = (2 * ROWS, PACK)
    n = len(levels)
    return pl.pallas_call(
        functools.partial(flow_kernel, levels),
        out_shape=(
            jax.ShapeDtypeStruct((LAYERS,) + block, BF16),
            jax.ShapeDtypeStruct((LAYERS, SHARDS) + block, BF16),
            jax.ShapeDtypeStruct((LAYERS, BLOCK, EXT), BF16),
            jax.ShapeDtypeStruct((LAYERS, SHARDS, 3, BLOCK, ROWS), BF16),
            jax.ShapeDtypeStruct((3 * CH, FRAMES), F32),
            jax.ShapeDtypeStruct((FRAMES // HOP, ROWS), F32),
            jax.ShapeDtypeStruct((88, WIDTH), F32),
            jax.ShapeDtypeStruct((CH, 2 * CH), F32),
            jax.ShapeDtypeStruct((CH, ROWS), F32),
            jax.ShapeDtypeStruct((SHARDS, 24, ROWS), F32),
            jax.ShapeDtypeStruct((CH, WIDTH), F32),
            jax.ShapeDtypeStruct((88, ROWS), F32),
            jax.ShapeDtypeStruct((CH, ROWS), F32),
        ),
        in_specs=[hbm] * 3 + [vmem] * 6,
        out_specs=tuple([hbm] * 4 + [vmem] * 9),
        scratch_shapes=[
            pltpu.VMEM((LAYERS * SHARDS,) + block, BF16),
            pltpu.VMEM((PAD + BLOCK + PAD, WIDTH), F32),
            pltpu.VMEM((2, BLOCK, EXT), BF16),
            pltpu.VMEM((2, SHARDS, 3, BLOCK, ROWS), BF16),
            pltpu.VMEM((2, EDGE, WIDTH), BF16),
            pltpu.VMEM((2, EDGE, WIDTH), BF16),
            pltpu.VMEM((2,) + block, BF16),
            pltpu.VMEM((BLOCK, WIDTH + ROWS), BF16),
            pltpu.VMEM((WIDTH, BLOCK), BF16),
            pltpu.VMEM((BLOCK + EDGE, WIDTH), F32),
            pltpu.VMEM((EDGE + BLOCK, WIDTH), F32),
            pltpu.VMEM((BLOCK, WIDTH), F32),
            pltpu.VMEM((BLOCK, ROWS), F32),
            pltpu.VMEM((2, EDGE, WIDTH), BF16),
            pltpu.VMEM((2, 2, EDGE, WIDTH), BF16),
            pltpu.VMEM((SHARDS, LAYERS, 4 * CH, ROWS), BF16),
            pltpu.VMEM((4, CH, BLOCK), F32),
            pltpu.VMEM((2 * CH, BLOCK), BF16),
            pltpu.VMEM((2 * CH, BLOCK), F32),
            pltpu.VMEM((n + 2, 88, WIDTH), F32),
            pltpu.VMEM((2, CH, WIDTH), F32),
        ]
        + (
            [pltpu.VMEM((DEPTH,) + shape, BF16) for shape in line_shapes()]
            if mesh_line(levels)
            else [pltpu.VMEM((LAYERS, after, PACK), BF16) for _, _, after in levels]
        )
        + [
            dma((4, LAYERS)), dma((7, LAYERS)), dma((7, LAYERS)), dma((LAYERS,)), dma((2,)), dma((2,)),
            dma((2,)), dma((2,)), dma((2,)), dma((2,)),
            dma((3,)), dma((3,)), dma((3,)), dma((3,)),
            regular((2,)), dma((2,)), dma((2, 2)), dma((2, 2)), regular((2,)), dma((LAYERS,)), dma((LAYERS,)),
            dma((n, LAYERS)), dma((n, LAYERS)), dma((n, LAYERS)), dma((n, LAYERS)), dma((2, LAYERS)),
            dma((2,)), dma((2, 2)),
            dma((n + 2,)), dma((n + 2,)), dma((2,)), dma((2,)), dma((3,)), dma((3,)), dma((3,)), dma((3,)),
            dma((6, DEPTH)), dma((6, DEPTH)), regular((6,)), dma((8, LAYERS)), dma((8, LAYERS)),
        ],
        compiler_params=pltpu.CompilerParams(
            collective_id=0, has_side_effects=True, vmem_limit_bytes=VMEM_LIMIT
        ),
    )(*args)


def prepare_kernel(
    offset, clip, mel_frames, cond_weight, in_bias, start_weight, start_bias, res_bias, skip_bias, final, end_bias,
    audio, mel, cond_ext, local_small, end_column,
):
    chan = lax.axis_index("chan")
    first = offset[0] * HOP + chan * BLOCK
    length = clip.shape[2]
    audio[...] = pltpu.roll(clip[0], lax.rem(length - first, length), 1)[:, :BLOCK]
    mel_rows = BLOCK // HOP
    clip_rows = mel_frames.shape[1]
    frames = jnp.concatenate([mel_frames[0].astype(F32), jnp.ones((clip_rows, ROWS - MEL), F32)], axis=1)
    frames = pltpu.roll(frames, lax.rem(clip_rows - offset[0] - chan * mel_rows, clip_rows), 0)[:mel_rows]
    lane = lax.broadcasted_iota(jnp.int32, (mel_rows, ROWS), 1)
    mel[...] = jnp.where(lane < MEL + 2, frames, 0.0)
    for l in range(LAYERS):
        high, rest = split(in_bias[l])
        for g in range(2):
            part = jnp.concatenate(
                [
                    cond_weight[l, g].astype(F32),
                    high[g : g + 1],
                    rest[g : g + 1],
                    jnp.zeros((ROWS - MEL - 2, ROWS), F32),
                ],
                axis=0,
            )
            cond_ext[l, g * ROWS : (g + 1) * ROWS, :] = part.T.astype(BF16)
    local_small[...] = jnp.concatenate(
        [
            start_weight[...],
            start_bias[...],
            res_bias[...],
            jnp.zeros((1, ROWS), F32),
            skip_bias[...],
            jnp.zeros((2, ROWS), F32),
            final[...],
        ],
        axis=0,
    )
    row = jnp.concatenate([end_bias[...], jnp.zeros((1, ROWS - CH), F32)], axis=1)
    end_column[...] = jnp.broadcast_to(row, (ROWS, ROWS)).T[:CH, :1]


def run_prepare(*args):
    vmem = pl.BlockSpec(memory_space=pltpu.VMEM)
    return pl.pallas_call(
        prepare_kernel,
        out_shape=(
            jax.ShapeDtypeStruct((CH, BLOCK), F32),
            jax.ShapeDtypeStruct((BLOCK // HOP, ROWS), F32),
            jax.ShapeDtypeStruct((LAYERS, 2 * ROWS, ROWS), BF16),
            jax.ShapeDtypeStruct((24, ROWS), F32),
            jax.ShapeDtypeStruct((CH, 1), F32),
        ),
        in_specs=[pl.BlockSpec(memory_space=pltpu.SMEM)] + [vmem] * 10,
        out_specs=tuple([vmem] * 5),
    )(*args)


def finish_kernel(
    crops, total, sums, mine, small, frames, mel_in, inverse, log_abs, end_in, final_own, skip_bias,
    latent, log_det, loss, audio_grad, mel_grad, inv_grad, start_grad, start_bias_grad, cond_grad, in_grad,
    bias_grad, res_grad, res_bias_grad, skip_grad, skip_bias_grad, end_grad, end_bias_grad,
):
    l = pl.program_id(0)
    for g in range(2):
        rows = slice(g * ROWS, (g + 1) * ROWS)
        in_grad[0, g] = total[0, rows, :CONV].astype(F32)
        cond = total[0, rows, CONV:EXT].astype(F32)
        cond = cond.T
        cond_grad[0, g] = cond[:MEL]
        bias_grad[0, g : g + 1, :] = cond[MEL : MEL + 1]

    @pl.when(l < LAYERS - 1)
    def _():
        res_grad[0, : 2 * ROWS] = total[0, :, EXT : EXT + ROWS].astype(F32)
        res_grad[0, 2 * ROWS :] = total[0, :, EXT + ROWS :].astype(F32)

    final = jnp.concatenate([small[s, 16:24, :] for s in range(SHARDS)], axis=1)
    skip_grad[0] = lax.dot_general(
        final, mine[pl.ds(pl.multiple_of(l * CH, CH), CH), :], (((0,), (0,)), ((), ())),
        precision=HIGH, preferred_element_type=F32,
    )

    @pl.when(l == 0)
    def _():
        z = frames[:CH]
        latent[0] = z
        audio_grad[0] = frames[CH : 2 * CH]
        mel_grad[0] = mel_in[:, :MEL]
        log_scale = frames[2 * CH : 2 * CH + HALF]
        det = jnp.sum(jnp.sum(log_scale, axis=1, keepdims=True), axis=0, keepdims=True) + FRAMES * log_abs[:1, :1]
        squares = jnp.sum(jnp.sum(z * z, axis=1, keepdims=True), axis=0, keepdims=True)
        log_det[...] = det
        loss[...] = (0.5 * squares - det) / (CH * FRAMES)
        tiny = sums[80:88, :ROWS]
        inv_grad[...] = tiny[:, :CH] - crops * FRAMES * inverse[:, CH:].T
        end_column = tiny[:, CH : CH + 1]
        end_bias_grad[...] = jnp.broadcast_to(end_column, (CH, ROWS)).T[:1, :]
        start_grad[...] = mine[64:68, :]
        start_bias_grad[...] = mine[68:69, :]
        res_bias_grad[...] = mine[72:79, :]
        skip_bias_grad[...] = jnp.sum(end_column * final_own[...], axis=0, keepdims=True)
        end_grad[...] = end_in[...] + end_column * skip_bias[...]


def run_finish(crops, total, *args):
    def whole(shape):
        return pl.BlockSpec(shape, lambda l: (0,) * len(shape))

    outs = [
        ((1, CH, FRAMES), None),
        ((1, 1), None),
        ((1, 1), None),
        ((1, CH, FRAMES), None),
        ((1, FRAMES // HOP, MEL), None),
        ((CH, CH), None),
        ((HALF, ROWS), None),
        ((1, ROWS), None),
        ((LAYERS, 2, MEL, ROWS), pl.BlockSpec((1, 2, MEL, ROWS), lambda l: (l, 0, 0, 0))),
        ((LAYERS, 2, ROWS, CONV), pl.BlockSpec((1, 2, ROWS, CONV), lambda l: (l, 0, 0, 0))),
        ((LAYERS, 2, ROWS), pl.BlockSpec((1, 2, ROWS), lambda l: (l, 0, 0))),
        (
            (LAYERS - 1, WIDTH, ROWS),
            pl.BlockSpec((1, WIDTH, ROWS), lambda l: (jnp.minimum(l, LAYERS - 2), 0, 0)),
        ),
        ((LAYERS - 1, ROWS), None),
        ((LAYERS, WIDTH, ROWS), pl.BlockSpec((1, WIDTH, ROWS), lambda l: (l, 0, 0))),
        ((1, ROWS), None),
        ((CH, ROWS), None),
        ((1, CH), None),
    ]
    return pl.pallas_call(
        functools.partial(finish_kernel, crops),
        grid=(LAYERS,),
        out_shape=tuple(jax.ShapeDtypeStruct(shape, F32) for shape, _ in outs),
        in_specs=[pl.BlockSpec((1, 2 * ROWS, PACK), lambda l: (l, 0, 0))] + [whole(a.shape) for a in args],
        out_specs=tuple(spec or whole(shape) for shape, spec in outs),
    )(total, *args)


def local(
    audio_clips,
    mel_frames,
    crop_offsets,
    inv_weight,
    initial_projection_weight,
    start_bias,
    cond_weight,
    in_weight,
    in_bias,
    res_weight,
    res_bias,
    skip_projection_weight,
    skip_output_bias,
    final_projection_weight,
    end_bias,
):
    skip_bias = skip_output_bias[None]
    audio, mel, cond_ext, local_small, end_column = run_prepare(
        crop_offsets,
        audio_clips,
        jnp.swapaxes(mel_frames, 1, 2),
        jnp.swapaxes(cond_weight, 2, 3),
        in_bias,
        initial_projection_weight.T,
        start_bias[None],
        res_bias,
        skip_bias,
        final_projection_weight,
        end_bias[None],
    )
    total, _, _, _, frames, mel_grad, sums, inverse, log_abs, small, _, mine, end_own = run_flow(
        lax.axis_size("dp"),
        in_weight.reshape(LAYERS, 2 * ROWS, CONV),
        cond_ext,
        res_weight,
        skip_projection_weight,
        audio,
        mel,
        inv_weight,
        local_small,
        end_column,
    )
    crops = lax.axis_size("dp") * audio_clips.shape[0]
    outs = list(
        run_finish(
            crops, total, sums, mine, small, frames, mel_grad, inverse, log_abs, end_own,
            final_projection_weight, skip_bias,
        )
    )
    for k, shape in ((1, (1,)), (2, (1,)), (7, (ROWS,)), (14, (ROWS,)), (16, (CH,))):
        outs[k] = outs[k].reshape(shape)
    outs[4] = jnp.swapaxes(outs[4], 1, 2)
    outs[6] = outs[6].T
    outs[8] = jnp.swapaxes(outs[8], 2, 3)
    return tuple(outs)


def solution(mesh):
    in_specs = (
        P("dp", None, None),
        P("dp", None, None),
        P("dp"),
        P(),
        P("chan", None),
        P("chan"),
        P(None, None, "chan", None),
        P(None, None, "chan", None),
        P(None, None, "chan"),
        P(None, None, "chan"),
        P(None, "chan"),
        P(None, None, "chan"),
        P("chan"),
        P(None, "chan"),
        P(),
    )
    out_specs = (
        P("dp", None, None),
        P("dp"),
        P("dp"),
        P("dp", None, None),
        P("dp", None, None),
        P(),
        P("chan", None),
        P("chan"),
        P(None, None, "chan", None),
        P(None, None, "chan", None),
        P(None, None, "chan"),
        P(None, None, "chan"),
        P(None, "chan"),
        P(None, None, "chan"),
        P("chan"),
        P(None, "chan"),
        P(),
    )
    return jax.shard_map(local, mesh=mesh, in_specs=in_specs, out_specs=out_specs, check_vma=False)
```

time: 632 us -> 386 us (0.61)
  blocking collectives: 71.7 us -> 0 us
  Pallas kernels: 444 us -> 382 us
  local copies, waits for them, and re-layouts: 60.1 us -> 0 us
  between operations: 24 us -> 1.31 us
  other arithmetic: 17.1 us -> 0 us
  matrix products: 12.8 us -> 0 us
    pallas_call x2 -> x3, Pallas kernels: 444 us -> 382 us  [the longest x1 367 us: run_flow(): pl.pallas_call(functools.partial(flow_kernel, levels), out_shape=(jax.Sha...]
    psum x2 -> x0, blocking collectives: 48.7 us -> none  [the longest x1 42.9 us: local(): rows_out, tiny = lax.psum((rows_out, tiny), ('dp', 'chan'))]
    all_gather x4 -> x0, blocking collectives: 23 us -> none  [the longest x1 6.22 us: local(): small = lax.all_gather(small, 'chan', axis=1, tiled=True)]
    slice x21 -> x0, local copies, waits for them, and re-layouts: 20.8 us -> none  [the longest x1 9.33 us: local(): total[:, :, :CONV].reshape(LAYERS, 2, rows, CONV)]
    concatenate x7 -> x0, local copies, waits for them, and re-layouts: 17.3 us -> none  [the longest x1 12.6 us: local(): jnp.concatenate([in_weight.reshape(LAYERS, 2 * rows, CONV), jnp.concatena...]
    dot_general x11 -> x0, matrix products: 12.8 us -> none  [the longest x1 2.39 us: local(): skip_grad = jnp.einsum('ko,lki->loi', final_weight, e, precision=HIGH)]
    unnamed x28 -> x0, local copies, waits for them, and re-layouts: 9.13 us -> none
    div x8 -> x0, other arithmetic: 6.49 us -> none  [invert_small(): pivot_row = augmented[column] / pivot]
  transfers between devices with their start and end apart: 1 -> 0, of which waited for: 0 -> 0; matrix products, arithmetic and copies ran while one was open for 8% -> 0% of each run, Pallas kernels for 0% -> 0%
where the time goes in v3:
time: 386 us; the launch traced here: 383 us
  Pallas kernels  382 us (99%)
    pallas_call x1, Pallas kernels, run_flow(): pl.pallas_call(functools.partial(flow_kernel, levels), out_shape=(jax.Sha...  367 us
    pallas_call x1, Pallas kernels, run_finish(): pl.pallas_call(functools.partial(finish_kernel, crops), grid=(LAYERS,), o...  12.7 us

profile of v3, /device:TPU:0, one launch (start us, length us, event | category | flops | bytes accessed | tf_op | source)
XLA Modules:
  0.0 382.9 jit_solution(15819983599540197042)
XLA Ops:
  1.3 2.1 shard_map.278
  3.5 366.7 %shard_map.279 = (bf16[8,256,1920]{2,1,0:T(8,128)(2,1)}, bf16[8,4,256,1920]{3,2,1,0:T(8,128)(2,1)}, bf16[8,512,1664]{2,1,0:T(8,128)(2,1)}, bf16[8,4,3,512,128]{4...) custom-call(bf16[8,256,1536]{2,1,0:T(8,128)(2,1)} %bitcast.15, ...), custom_call_target="tpu_custom_call" | custom-call | tf_op jit(solution)/shard_map/pallas_call | solution.py:1061
  370.2 12.7 %shard_map.280 = (f32[1,8,2048]{2,1,0:T(8,128)}, f32[1,1]{1,0:T(1,128)}, f32[1,1]{1,0:T(1,128)}, f32[1,8,2048]{2,1,0:T(8,128)}, f32[1,64,80]{2,1,0:T(8,128)}, /*...) custom-call(bf16[8,256,1920]{2,1,0:T(8,128)(2,1)} %get-tuple-element, ...), custom_call_target="tpu_custom_call" | custom-call | tf_op jit(solution)/shard_map/pallas_call | solution.py:1256

commit v4 on v3

--- a/solution.py
+++ b/solution.py
@@ -100,8 +100,8 @@
     return levels
 
 
-ACROSS = pl.ds(0, 7 * ROWS)
-ALONG = pl.ds(7 * ROWS, PACK - 7 * ROWS)
+ACROSS = pl.ds(0, 6 * ROWS)
+ALONG = pl.ds(6 * ROWS, PACK - 6 * ROWS)
 DEPTH = 4
 
 
@@ -111,7 +111,7 @@
 
 def line_shapes():
     a, b = ACROSS.size, ALONG.size
-    return [(2, ROWS, a), (ROWS, a), (ROWS // 2, a), (2 * ROWS, b), (ROWS, b), (ROWS // 2, b)]
+    return [(2, ROWS // 2, a), (ROWS // 2, a), (ROWS // 4, a), (ROWS, b), (ROWS // 2, b), (ROWS // 4, b)]
 
 
 class Lane:
@@ -249,7 +249,6 @@
         far_a(l, me.far_shard).wait_recv()
         x_a(l, xb).start()
         z_a(l, zb).start()
-        pl.when(l + 1 < LAYERS)(lambda: issue(l + 1))
 
     def relay_b(l):
         z_a(l, 1 - zb).wait_recv()
@@ -326,6 +325,8 @@
     hid[pl.ds(PAD, BLOCK), :] = lax.dot_general(
         first_ext, start_ext, (((0,), (0,)), ((), ())), precision=HIGH, preferred_element_type=F32
     )
+    relay_a(0)
+    issue(1)
     final = small_row(16, 24)
     final_high, final_low = split(final)
     final_rows = jnp.concatenate([final_high, final_low], axis=0).astype(BF16)
@@ -338,6 +339,7 @@
     skip_bias = small_row(13, 14)
     const = jnp.sum(final * skip_bias, axis=1, keepdims=True) + end_bias[...]
 
+    relay_b(0)
     aug = jnp.concatenate(
         [
             inv_weight[...],
@@ -356,6 +358,10 @@
         aug = jnp.where(aug_rows == c, pivot_row, aug - aug[:, c : c + 1] * pivot_row)
     inverse_out[...] = aug
     log_out[...] = jnp.broadcast_to(log_total, log_out.shape)
+    relay_a(1)
+    issue(2)
+    relay_c(0)
+    relay_b(1)
 
     def ext_copy(l):
         return pltpu.make_async_copy(ext.at[l % 2], ext_out.at[l], ext_sem.at[l % 2])
@@ -390,10 +396,9 @@
 
     def forward(l, carry):
         p = l % 2
-        pl.when(l + 1 < LAYERS)(lambda: relay_a(l + 1))
-        relay_c(l)
+        pl.when(l + 2 < LAYERS)(lambda: relay_a(l + 2))
         arrive(l)
-        keep_copy(l).start()
+        pl.when(l < LAYERS - 1)(lambda: keep_copy(l).start())
 
         @pl.when(l >= 2)
         def _():
@@ -418,6 +423,7 @@
                 to_next(l, rows).wait_recv()
 
         by_edge(l, start)
+        pl.when(l + 3 < LAYERS)(lambda: issue(l + 3))
         by_edge(l, finish)
         hid[pl.ds(0, PAD), :] = top[p, pl.ds(EDGE - PAD, PAD), :].astype(F32)
         hid[pl.ds(PAD + BLOCK, PAD), :] = bottom[p, pl.ds(0, PAD), :].astype(F32)
@@ -445,7 +451,6 @@
             acts[p, s, 0] = tg.astype(BF16)
             acts[p, s, 1] = (g - t * tg).astype(BF16)
             acts[p, s, 2] = (tg * (1.0 - g)).astype(BF16)
-            pl.when((s == 1) & (l + 1 < LAYERS))(lambda: relay_b(l + 1))
             return carry
 
         lax.fori_loop(0, SHARDS, one, 0)
@@ -469,10 +474,10 @@
                 cols = slice(h * 2 * ROWS, (h + 1) * 2 * ROWS)
                 hid[pl.ds(PAD, BLOCK), cols] += dot_nt(gated, res) + bias
 
+        pl.when(l + 1 < LAYERS)(lambda: relay_c(l + 1))
+        pl.when(l + 2 < LAYERS)(lambda: relay_b(l + 2))
         return carry
 
-    relay_a(0)
-    relay_b(0)
     lax.fori_loop(0, LAYERS, forward, 0)
 
     both = out[...]
@@ -503,7 +508,7 @@
         x_b(l, xb).wait_send()
         core_a(l, me.chan).wait_send()
         core_b(l, me.far_shard).wait_send()
-        keep_copy(l).wait()
+        pl.when(l < LAYERS - 1)(lambda: keep_copy(l).wait())
         return carry
 
     lax.fori_loop(0, LAYERS, drain_forward, 0)
@@ -524,6 +529,12 @@
         l, s = LAYERS - 1 - q // SHARDS, shard_of(q % SHARDS)
         return pltpu.make_async_copy(weights_out.at[l, s], wbuf.at[q % 2], w_sem.at[q % 2])
 
+    def w_start(q):
+        s = shard_of(q % SHARDS)
+        here = pltpu.make_async_copy(shared.at[(LAYERS - 1) * SHARDS + s], wbuf.at[q % 2], w_sem.at[q % 2])
+        pl.when(q < SHARDS)(lambda: here.start())
+        pl.when(q >= SHARDS)(lambda: w_copy(q).start())
+
     def ext_back(l):
         return pltpu.make_async_copy(ext_out.at[l], ext.at[l % 2], ext_sem.at[l % 2])
 
@@ -588,8 +599,6 @@
                 pl.when(i == 0)(lambda: pl.semaphore_wait(phase.at[1], 1))
                 if not line:
                     to_far(i).start()
-        if line:
-            start_ways(i)
 
     def stage_far(i):
         to_far(i).wait_recv()
@@ -618,15 +627,15 @@
         chunk = min(rows, 64)
 
         def body(k, carry):
-            at = pl.ds(pl.multiple_of(base + k * chunk, 64), chunk)
-            got = src[pl.ds(pl.multiple_of(src_base + k * chunk, 64), chunk), :]
+            at = pl.ds(pl.multiple_of(base + k * chunk, 32), chunk)
+            got = src[pl.ds(pl.multiple_of(src_base + k * chunk, 32), chunk), :]
             shared[block, at, cols] = shared[block, at, cols] + got
             return carry
 
         lax.fori_loop(0, rows // chunk, body, 0)
 
     def rows_at(first, rows):
-        return pl.ds(pl.multiple_of(first, 64), rows)
+        return pl.ds(pl.multiple_of(first, 32), rows)
 
     if line:
         zc = me.dp // 2
@@ -638,169 +647,182 @@
             Lane(level_bufs[k], lane_send.at[k], lane_recv.at[k], lane_credit.at[k], lane_devs[k]) for k in range(6)
         ]
         qx, q1, q2, r1, r2, rx = lanes
-        half = ROWS
-        mine_x, mine_x2 = xb * half, xb * half + hb * (half // 2)
-        r_base, r_base2 = hb * half, hb * half + xb * (half // 2)
-
-        def far_way(k, i, rows, cols):
+        wide, half, small_half = ROWS, ROWS // 2, ROWS // 4
+
+        def q_rows(u, x):
+            return x * wide + u % 2 * half
+
+        def r_rows(u):
+            return u % 2 * wide
+
+        def far_way(k, u, rows, cols):
+            i = u // 2
             return remote(
                 shared.at[kept(i, 1 - me.side), rows, cols], shared.at[24 + i, rows, cols],
-                way_send.at[k, i], way_recv.at[k, i], far_dev,
+                way_send.at[k, u], way_recv.at[k, u], far_dev,
             )
 
-        def far_q(i):
-            return far_way(0, i, rows_at(mine_x, half), ACROSS)
-
-        def far_r(i):
-            return far_way(1, i, pl.ds(0, 2 * ROWS), ALONG)
-
-        def total_way(k, i, rows, cols, device, src=None):
-            ref = total.at[LAYERS - 1 - i, rows, cols]
-            return remote(ref if src is None else src, ref, way_send.at[k, i], way_recv.at[k, i], device)
-
-        def own_part(k, i, rows, cols):
-            return pltpu.make_async_copy(
-                shared.at[kept(i, me.side), rows, cols], total.at[LAYERS - 1 - i, rows, cols], out_sem.at[k, i]
-            )
-
-        def q_inner(i, b):
-            rows = rows_at(mine_x + b * (half // 2), half // 2)
-            return total_way(2, i, rows, ACROSS, opp_dev, shared.at[kept(i, me.side), rows, ACROSS])
-
-        def q_edge(i):
-            return total_way(3, i, rows_at(mine_x, half), ACROSS, z_dev)
-
-        def q_x(i, x):
-            return total_way(4, i, rows_at(x * half, half), ACROSS, x_dev)
-
-        def r_x(i, x):
-            rows = rows_at(r_base + x * (half // 2), half // 2)
-            return total_way(5, i, rows, ALONG, x_dev, shared.at[kept(i, me.side), rows, ALONG])
-
-        def r_inner(i, b):
-            return total_way(6, i, rows_at(b * half, half), ALONG, opp_dev)
-
-        def r_edge(i):
-            return total_way(7, i, pl.ds(0, 2 * ROWS), ALONG, z_dev)
-
-        def q_out(i):
-            return own_part(0, i, rows_at(mine_x2, half // 2), ACROSS)
-
-        def r_out(i):
-            return own_part(1, i, rows_at(r_base2, half // 2), ALONG)
-
-        def own_ref(i, first, rows, cols):
-            return shared.at[kept(i, me.side), rows_at(first, rows), cols]
-
-        def start_ways(i):
-            far_r(i).start()
-            qx.start(i, shared.at[pl.ds(kept(i, 0), 2), rows_at((1 - xb) * half, half), ACROSS])
-
-        def q_stage1(i):
-            qx.wait(i)
+        def far_q(u):
+            return far_way(0, u, rows_at(q_rows(u, xb), half), ACROSS)
+
+        def far_r(u):
+            return far_way(1, u, rows_at(r_rows(u), wide), ALONG)
+
+        def own_ref(u, first, rows, cols):
+            return shared.at[kept(u // 2, me.side), rows_at(first, rows), cols]
+
+        def total_ref(u, first, rows, cols):
+            return total.at[LAYERS - 1 - u // 2, rows_at(first, rows), cols]
+
+        def way(k, u, src, dst, device):
+            return remote(src, dst, way_send.at[k, u], way_recv.at[k, u], device)
+
+        def q_inner(u, b):
+            at = (u, q_rows(u, xb) + b * small_half, small_half, ACROSS)
+            return way(2, u, own_ref(*at), total_ref(*at), opp_dev)
+
+        def q_edge(u):
+            ref = total_ref(u, q_rows(u, xb), half, ACROSS)
+            return way(3, u, ref, ref, z_dev)
+
+        def q_x(u, x):
+            ref = total_ref(u, q_rows(u, x), half, ACROSS)
+            return way(4, u, ref, ref, x_dev)
+
+        def r_x(u, x):
+            at = (u, r_rows(u) + hb * half + x * small_half, small_half, ALONG)
+            return way(5, u, own_ref(*at), total_ref(*at), x_dev)
+
+        def r_inner(u, b):
+            ref = total_ref(u, r_rows(u) + b * half, half, ALONG)
+            return way(6, u, ref, ref, opp_dev)
+
+        def r_edge(u):
+            ref = total_ref(u, r_rows(u), wide, ALONG)
+            return way(7, u, ref, ref, z_dev)
+
+        def q_out(u):
+            at = (u, q_rows(u, xb) + hb * small_half, small_half, ACROSS)
+            return pltpu.make_async_copy(own_ref(*at), total_ref(*at), out_sem.at[0, u])
+
+        def r_out(u):
+            at = (u, r_rows(u) + hb * half + xb * small_half, small_half, ALONG)
+            return pltpu.make_async_copy(own_ref(*at), total_ref(*at), out_sem.at[1, u])
+
+        def start_ways(u):
+            far_r(u).start()
+            qx.start(u, shared.at[pl.ds(kept(u // 2, 0), 2), rows_at(q_rows(u, 1 - xb), half), ACROSS])
+
+        def q_stage1(u):
+            qx.wait(u)
             for ys in (1 - me.side, me.side):
-                add_block(kept(i, ys), mine_x, half, ACROSS, qx.buf.at[i % DEPTH, ys])
+                add_block(kept(u // 2, ys), q_rows(u, xb), half, ACROSS, qx.buf.at[u % DEPTH, ys])
                 if ys is not me.side:
-                    far_q(i).start()
+                    far_q(u).start()
             qx.free()
 
-        def r_stage1(i):
-            far_r(i).wait_recv()
-            add_block(kept(i, me.side), 0, 2 * ROWS, ALONG, shared.at[24 + i, :, ALONG])
-            pl.when(edge)(lambda: r1.start(i, own_ref(i, 0, 2 * ROWS, ALONG)))
-
-        def q_stage2(i):
-            far_q(i).wait_recv()
-            add_block(kept(i, me.side), mine_x, half, ACROSS, shared.at[24 + i, :, ACROSS], mine_x)
-            pl.when(edge)(lambda: q1.start(i, own_ref(i, mine_x, half, ACROSS)))
-
-        def r_stage2(i):
+        def r_stage1(u):
+            far_r(u).wait_recv()
+            add_block(kept(u // 2, me.side), r_rows(u), wide, ALONG, shared.at[24 + u // 2, :, ALONG], r_rows(u))
+            pl.when(edge)(lambda: r1.start(u, own_ref(u, r_rows(u), wide, ALONG)))
+
+        def q_stage2(u):
+            far_q(u).wait_recv()
+            first = q_rows(u, xb)
+            add_block(kept(u // 2, me.side), first, half, ACROSS, shared.at[24 + u // 2, :, ACROSS], first)
+            pl.when(edge)(lambda: q1.start(u, own_ref(u, first, half, ACROSS)))
+
+        def r_stage2(u):
             @pl.when(inner)
             def _():
-                r1.wait(i)
-                add_block(kept(i, me.side), 0, 2 * ROWS, ALONG, r1.buf.at[i % DEPTH])
+                r1.wait(u)
+                add_block(kept(u // 2, me.side), r_rows(u), wide, ALONG, r1.buf.at[u % DEPTH])
                 r1.free()
-                r2.start(i, own_ref(i, (1 - hb) * half, half, ALONG))
-
-        def q_stage3(i):
+                r2.start(u, own_ref(u, r_rows(u) + (1 - hb) * half, half, ALONG))
+
+        def q_stage3(u):
             @pl.when(inner)
             def _():
-                q1.wait(i)
-                add_block(kept(i, me.side), mine_x, half, ACROSS, q1.buf.at[i % DEPTH])
+                first = q_rows(u, xb)
+                q1.wait(u)
+                add_block(kept(u // 2, me.side), first, half, ACROSS, q1.buf.at[u % DEPTH])
                 q1.free()
-                q2.start(i, own_ref(i, mine_x + (1 - hb) * (half // 2), half // 2, ACROSS))
-
-        def r_stage3(i):
+                q2.start(u, own_ref(u, first + (1 - hb) * small_half, small_half, ACROSS))
+
+        def r_stage3(u):
             @pl.when(inner)
             def _():
-                r2.wait(i)
-                add_block(kept(i, me.side), r_base, half, ALONG, r2.buf.at[i % DEPTH])
+                first = r_rows(u) + hb * half
+                r2.wait(u)
+                add_block(kept(u // 2, me.side), first, half, ALONG, r2.buf.at[u % DEPTH])
                 r2.free()
-                rx.start(i, own_ref(i, r_base + (1 - xb) * (half // 2), half // 2, ALONG))
-
-        def q_stage4(i):
+                rx.start(u, own_ref(u, first + (1 - xb) * small_half, small_half, ALONG))
+
+        def q_stage4(u):
             @pl.when(inner)
             def _():
-                q2.wait(i)
-                add_block(kept(i, me.side), mine_x2, half // 2, ACROSS, q2.buf.at[i % DEPTH])
+                q2.wait(u)
+                first = q_rows(u, xb) + hb * small_half
+                add_block(kept(u // 2, me.side), first, small_half, ACROSS, q2.buf.at[u % DEPTH])
                 q2.free()
-                q_inner(i, hb).start()
-                q_out(i).start()
-
-        def r_stage4(i):
+                q_inner(u, hb).start()
+                q_out(u).start()
+
+        def r_stage4(u):
             @pl.when(inner)
             def _():
-                rx.wait(i)
-                add_block(kept(i, me.side), r_base2, half // 2, ALONG, rx.buf.at[i % DEPTH])
+                rx.wait(u)
+                first = r_rows(u) + hb * half + xb * small_half
+                add_block(kept(u // 2, me.side), first, small_half, ALONG, rx.buf.at[u % DEPTH])
                 rx.free()
-                r_x(i, xb).start()
-                r_out(i).start()
-
-        def q_stage5(i):
+                r_x(u, xb).start()
+                r_out(u).start()
+
+        def q_stage5(u):
             @pl.when(inner)
             def _():
-                q_out(i).wait()
-                q_inner(i, 1 - hb).wait_recv()
-                q_edge(i).start()
-                q_x(i, xb).start()
-
-        def r_stage5(i):
+                q_out(u).wait()
+                q_inner(u, 1 - hb).wait_recv()
+                q_edge(u).start()
+                q_x(u, xb).start()
+
+        def r_stage5(u):
             @pl.when(inner)
             def _():
-                r_out(i).wait()
-                r_x(i, 1 - xb).wait_recv()
-                r_inner(i, hb).start()
-
-        def q_stage6(i):
+                r_out(u).wait()
+                r_x(u, 1 - xb).wait_recv()
+                r_inner(u, hb).start()
+
+        def q_stage6(u):
             @pl.when(edge)
             def _():
-                q_edge(i).wait_recv()
-                q_x(i, xb).start()
-
-        def r_stage6(i):
+                q_edge(u).wait_recv()
+                q_x(u, xb).start()
+
+        def r_stage6(u):
             @pl.when(inner)
             def _():
-                r_inner(i, 1 - hb).wait_recv()
-                r_edge(i).start()
-
-        def q_stage7(i):
-            q_x(i, 1 - xb).wait_recv()
-
-        def r_stage7(i):
-            pl.when(edge)(lambda: r_edge(i).wait_recv())
-
-        def drain_ways(i, carry):
-            far_q(i).wait_send()
-            far_r(i).wait_send()
-            q_x(i, xb).wait_send()
+                r_inner(u, 1 - hb).wait_recv()
+                r_edge(u).start()
+
+        def q_stage7(u):
+            q_x(u, 1 - xb).wait_recv()
+
+        def r_stage7(u):
+            pl.when(edge)(lambda: r_edge(u).wait_recv())
+
+        def drain_ways(u, carry):
+            far_q(u).wait_send()
+            far_r(u).wait_send()
+            q_x(u, xb).wait_send()
 
             @pl.when(inner)
             def _():
-                q_inner(i, hb).wait_send()
-                q_edge(i).wait_send()
-                r_x(i, xb).wait_send()
-                r_inner(i, hb).wait_send()
-                r_edge(i).wait_send()
+                q_inner(u, hb).wait_send()
+                q_edge(u).wait_send()
+                r_x(u, xb).wait_send()
+                r_inner(u, hb).wait_send()
+                r_edge(u).wait_send()
 
             return carry
 
@@ -835,9 +857,34 @@
             edge_send.at[1], edge_recv.at[i % 2, 1], next_dev,
         )
 
-    def backward(i):
+    def back_edge(i, f):
+        by_edge(LAYERS - 1 - i, f)
+
+    def apply_edges(i):
+        def finish(rows):
+            @pl.when(has_next)
+            def _():
+                back_next(i, rows).wait_send()
+                back_prev(i, rows).wait_recv()
+
+            @pl.when(has_prev)
+            def _():
+                back_prev(i, rows).wait_send()
+                back_next(i, rows).wait_recv()
+
+        back_edge(i, finish)
+        tap0[pl.ds(BLOCK, EDGE), :] = edge_in[i % 2, 0].astype(F32)
+        tap2[pl.ds(0, EDGE), :] = edge_in[i % 2, 1].astype(F32)
+        for layer in range(LAYERS):
+            d = 2**layer
+
+            @pl.when(LAYERS - 1 - i == layer)
+            def _():
+                grad[...] += tap0[pl.ds(d, BLOCK), :] + tap2[pl.ds(EDGE - d, BLOCK), :]
+
+    def backward_open(i):
         l = LAYERS - 1 - i
-        p = l % 2
+        pl.when(i > 0)(lambda: apply_edges(i - 1))
         now = grad[...].astype(BF16)
         low[:, :WIDTH] = now
         low_t[...] = now.T
@@ -850,11 +897,16 @@
             ext_back(l).wait()
             acts_back(l).wait()
 
-        def one(j, carry):
+    def backward_shards(i, h):
+        l = LAYERS - 1 - i
+        p = l % 2
+
+        def one(k, carry):
+            j = 2 * h + k
             q = i * SHARDS + j
             b = q % 2
             s = shard_of(j)
-            pl.when(q + 1 < LAYERS * SHARDS)(lambda: w_copy(q + 1).start())
+            pl.when(q + 1 < LAYERS * SHARDS)(lambda: w_start(q + 1))
 
             @pl.when((j < 2) & (i >= 2))
             def _():
@@ -891,7 +943,10 @@
 
             return carry
 
-        lax.fori_loop(0, SHARDS, one, 0)
+        lax.fori_loop(0, 2, one, 0)
+
+    def backward_close(i):
+        l = LAYERS - 1 - i
 
         @pl.when(l >= 2)
         def _():
@@ -905,27 +960,7 @@
             pl.when(has_next)(lambda: back_next(i, rows).start())
             pl.when(has_prev)(lambda: back_prev(i, rows).start())
 
-        def finish(rows):
-            @pl.when(has_next)
-            def _():
-                back_next(i, rows).wait_send()
-                back_prev(i, rows).wait_recv()
-
-            @pl.when(has_prev)
-            def _():
-                back_prev(i, rows).wait_send()
-                back_next(i, rows).wait_recv()
-
-        by_edge(l, start)
-        by_edge(l, finish)
-        tap0[pl.ds(BLOCK, EDGE), :] = edge_in[i % 2, 0].astype(F32)
-        tap2[pl.ds(0, EDGE), :] = edge_in[i % 2, 1].astype(F32)
-        for layer in range(LAYERS):
-            d = 2**layer
-
-            @pl.when(l == layer)
-            def _():
-                grad[...] += tap0[pl.ds(d, BLOCK), :] + tap2[pl.ds(EDGE - d, BLOCK), :]
+        back_edge(i, start)
 
     sum_devs = [core_dev, far_dev] + [me.dp_device(bit) for bit, _, _ in levels]
 
@@ -949,6 +984,7 @@
         return lax.dot_general(values, other, (dims, ((), ())), precision=HIGH, preferred_element_type=F32)
 
     def finish_frames():
+        apply_edges(LAYERS - 1)
         hidden_grad = grad[...]
         sums_out[64:72, :] = last(keep[1], hidden_grad, ((1,), (0,)))
         mixed = keep[0]
@@ -999,24 +1035,39 @@
         stages = [[stage_core], [stage_far]]
         stages += [[functools.partial(stage_rs, k)] for k in range(len(levels))]
         stages += [[functools.partial(stage_ag, n)] for n in range(len(halving) - 1, -1, -1)]
-    steps = LAYERS - 1 + max(len(stages), len(small_stages))
-
-    w_copy(0).start()
-
-    def step(i, carry):
-        @pl.when(i < LAYERS)
+    if line:
+        steps = 2 * LAYERS + max(len(stages), len(small_stages))
+    else:
+        steps = 2 * LAYERS + max(2 * len(stages) - 2, len(small_stages))
+
+    w_start(0)
+
+    def step(v, carry):
+        i, h = v // 2, v % 2
+
+        @pl.when(v < 2 * LAYERS)
         def _():
-            backward(i)
-            stage_core(i)
+            pl.when(h == 0)(lambda: backward_open(i))
+            backward_shards(i, h)
+
+            @pl.when(h == 1)
+            def _():
+                backward_close(i)
+                stage_core(i)
 
         for k, stage in enumerate(small_stages):
-            pl.when(i == LAYERS - 1 + k)(stage)
+            pl.when(v == 2 * LAYERS + k)(stage)
+        if line:
+            pl.when((v >= 1) & (v <= 2 * LAYERS))(lambda: start_ways(v - 1))
         for lag in range(len(stages) - 1, 0, -1):
-
-            @pl.when((i >= lag) & (i < LAYERS + lag))
+            at = v - 1 - lag if line else i - lag
+            count = 2 * LAYERS if line else LAYERS
+            now = (at >= 0) & (at < count)
+
+            @pl.when(now if line else now & (h == 1))
             def _():
                 for stage in stages[lag]:
-                    stage(i - lag)
+                    stage(at)
 
         return carry
 
@@ -1036,7 +1087,7 @@
         return carry
 
     if line:
-        lax.fori_loop(0, LAYERS, drain_ways, 0)
+        lax.fori_loop(0, 2 * LAYERS, drain_ways, 0)
         finish_lanes()
     else:
         lax.fori_loop(0, LAYERS, drain, 0)
@@ -1110,10 +1161,10 @@
             dma((2,)), dma((2,)), dma((2,)), dma((2,)),
             dma((3,)), dma((3,)), dma((3,)), dma((3,)),
             regular((2,)), dma((2,)), dma((2, 2)), dma((2, 2)), regular((2,)), dma((LAYERS,)), dma((LAYERS,)),
-            dma((n, LAYERS)), dma((n, LAYERS)), dma((n, LAYERS)), dma((n, LAYERS)), dma((2, LAYERS)),
+            dma((n, LAYERS)), dma((n, LAYERS)), dma((n, LAYERS)), dma((n, LAYERS)), dma((2, 2 * LAYERS)),
             dma((2,)), dma((2, 2)),
             dma((n + 2,)), dma((n + 2,)), dma((2,)), dma((2,)), dma((3,)), dma((3,)), dma((3,)), dma((3,)),
-            dma((6, DEPTH)), dma((6, DEPTH)), regular((6,)), dma((8, LAYERS)), dma((8, LAYERS)),
+            dma((6, DEPTH)), dma((6, DEPTH)), regular((6,)), dma((8, 2 * LAYERS)), dma((8, 2 * LAYERS)),
         ],
         compiler_params=pltpu.CompilerParams(
             collective_id=0, has_side_effects=True, vmem_limit_bytes=VMEM_LIMIT

time: 386 us -> 334 us (0.87)
  Pallas kernels: 382 us -> 333 us
    pallas_call x1, Pallas kernels: 367 us -> 318 us  [run_flow(): pl.pallas_call(functools.partial(flow_kernel, levels), out_shape=(jax.Sha...]
where the time goes in v4:
time: 334 us
  Pallas kernels  333 us (100%)
    pallas_call x1, Pallas kernels, run_flow(): pl.pallas_call(functools.partial(flow_kernel, levels), out_shape=(jax.Sha...  318 us
    pallas_call x1, Pallas kernels, run_finish(): pl.pallas_call(functools.partial(finish_kernel, crops), grid=(LAYERS,), o...  12.7 us

profile of v4, /device:TPU:0, one launch (start us, length us, event | category | flops | bytes accessed | tf_op | source)
XLA Modules:
  0.0 334.0 jit_solution(15154209838283185653)
XLA Ops:
  1.3 2.1 shard_map.278
  3.5 317.9 %shard_map.279 = (bf16[8,256,1920]{2,1,0:T(8,128)(2,1)}, bf16[8,4,256,1920]{3,2,1,0:T(8,128)(2,1)}, bf16[8,512,1664]{2,1,0:T(8,128)(2,1)}, bf16[8,4,3,512,128]{4...) custom-call(bf16[8,256,1536]{2,1,0:T(8,128)(2,1)} %bitcast.15, ...), custom_call_target="tpu_custom_call" | custom-call | tf_op jit(solution)/shard_map/pallas_call | solution.py:1112
  321.3 12.7 %shard_map.280 = (f32[1,8,2048]{2,1,0:T(8,128)}, f32[1,1]{1,0:T(1,128)}, f32[1,1]{1,0:T(1,128)}, f32[1,8,2048]{2,1,0:T(8,128)}, f32[1,64,80]{2,1,0:T(8,128)}, /*...) custom-call(bf16[8,256,1920]{2,1,0:T(8,128)(2,1)} %get-tuple-element, ...), custom_call_target="tpu_custom_call" | custom-call | tf_op jit(solution)/shard_map/pallas_call | solution.py:1307

commit v5 on v4

--- a/solution.py
+++ b/solution.py
@@ -102,7 +102,10 @@
 
 ACROSS = pl.ds(0, 6 * ROWS)
 ALONG = pl.ds(6 * ROWS, PACK - 6 * ROWS)
-DEPTH = 4
+DEPTH = 8
+ACROSS_LAGS = (0, 1, 3, 3, 4, 5, 7, 20)
+ALONG_LAGS = (0, 1, 2, 3, 4, 5, 6, 21)
+ORDER = 'q5 r6 q4 r5 q2 q1 r1 r4 r7 q7 q6 r3 q3 r2'
 
 
 def mesh_line(levels):
@@ -405,6 +408,7 @@
             ext_copy(l - 2).wait()
             acts_copy(l - 2).wait()
 
+        spilled = l < LAYERS - 2
         ext[p, :, WIDTH : 2 * WIDTH] = hid[pl.ds(PAD, BLOCK), :].astype(BF16)
 
         def start(rows):
@@ -441,7 +445,7 @@
                     ext[p, BLOCK - d :, 2 * WIDTH : CONV] = bottom[p, :d, :]
                     ext[p, : BLOCK - d, 2 * WIDTH : CONV] = ext[p, d:, WIDTH : 2 * WIDTH]
 
-        ext_copy(l).start()
+        pl.when(spilled)(lambda: ext_copy(l).start())
 
         def one(s, carry):
             pre = dot_nt(ext[p], shared[l * SHARDS + s, :, :EXT])
@@ -454,7 +458,7 @@
             return carry
 
         lax.fori_loop(0, SHARDS, one, 0)
-        acts_copy(l).start()
+        pl.when(spilled)(lambda: acts_copy(l).start())
 
         @pl.when(l == 0)
         def _():
@@ -512,18 +516,17 @@
         return carry
 
     lax.fori_loop(0, LAYERS, drain_forward, 0)
-    for l in (LAYERS - 2, LAYERS - 1):
-        ext_copy(l).wait()
-        acts_copy(l).wait()
     for k in range(3):
         small_copy(k).wait_send()
         fold_copy(k).wait_send()
     pl.semaphore_signal(phase.at[0], inc=1, device_id=core_dev, device_id_type=MESH)
     pl.semaphore_signal(phase.at[1], inc=1, device_id=far_dev, device_id_type=MESH)
 
+    def side_of(j):
+        return jnp.where(j < 2, 1 - me.side, me.side)
+
     def shard_of(j):
-        core = jnp.where(j < 2, 1 - me.core, me.core)
-        return (j % 2) * 2 + core
+        return side_of(j) * 2 + jnp.where(j % 2 == 0, 1 - me.core, me.core)
 
     def w_copy(q):
         l, s = LAYERS - 1 - q // SHARDS, shard_of(q % SHARDS)
@@ -590,15 +593,16 @@
         at = pl.ds(pl.multiple_of(base_at[-1], PAD), levels[-1][2])
         return pltpu.make_async_copy(shared.at[kept(i, me.side), at], total.at[LAYERS - 1 - i, at], out_sem.at[0, i])
 
-    def stage_core(i):
-        for ys in (1 - me.side, me.side):
-            to_core(i, ys).wait_recv()
-            add_rows(kept(i, ys), 0, 2 * ROWS, shared, got_core(i, ys))
-            pl.semaphore_signal(credit.at[ys], inc=1, device_id=core_dev, device_id_type=MESH)
-            if ys is not me.side:
-                pl.when(i == 0)(lambda: pl.semaphore_wait(phase.at[1], 1))
-                if not line:
-                    to_far(i).start()
+    def core_block(i, ys):
+        to_core(i, ys).wait_recv()
+        add_rows(kept(i, ys), 0, 2 * ROWS, shared, got_core(i, ys))
+        pl.semaphore_signal(credit.at[ys], inc=1, device_id=core_dev, device_id_type=MESH)
+
+    def far_block(i):
+        core_block(i, 1 - me.side)
+        pl.when(i == 0)(lambda: pl.semaphore_wait(phase.at[1], 1))
+        if not line:
+            to_far(i).start()
 
     def stage_far(i):
         to_far(i).wait_recv()
@@ -709,8 +713,7 @@
             at = (u, r_rows(u) + hb * half + xb * small_half, small_half, ALONG)
             return pltpu.make_async_copy(own_ref(*at), total_ref(*at), out_sem.at[1, u])
 
-        def start_ways(u):
-            far_r(u).start()
+        def start_q(u):
             qx.start(u, shared.at[pl.ds(kept(u // 2, 0), 2), rows_at(q_rows(u, 1 - xb), half), ACROSS])
 
         def q_stage1(u):
@@ -908,38 +911,46 @@
             s = shard_of(j)
             pl.when(q + 1 < LAYERS * SHARDS)(lambda: w_start(q + 1))
 
-            @pl.when((j < 2) & (i >= 2))
-            def _():
-                to_core(i - 2, j).wait_send()
+            @pl.when((j % 2 == 0) & (i >= 2))
+            def _():
+                to_core(i - 2, side_of(j)).wait_send()
 
             w_copy(q).wait()
-            slot = jnp.where(j < 2, 2 * (i % 2) + j, kept(i, j - 2))
+            slot = jnp.where(j % 2 == 0, 2 * (i % 2) + side_of(j), kept(i, side_of(j)))
             gated = acts[p, s, 0]
-            res = jnp.concatenate([wbuf[b, :, EXT : EXT + ROWS], wbuf[b, :, EXT + ROWS :]], axis=0)
-            back = dot(low[:, :WIDTH], res) + dot(low[:, WIDTH : WIDTH + 4 * CH], fold[s, l])
+            res = jnp.concatenate(
+                [
+                    wbuf[b, :, EXT : EXT + ROWS],
+                    wbuf[b, :, EXT + ROWS :],
+                    fold[s, l],
+                    jnp.zeros((ROWS - 4 * CH, ROWS), BF16),
+                ],
+                axis=0,
+            )
+            back = dot(low[...], res)
             pg = jnp.concatenate(
                 [(back * acts[p, s, 1].astype(F32)).astype(BF16), (back * acts[p, s, 2].astype(F32)).astype(BF16)],
                 axis=1,
             )
+            pg_t = pg.T
             tap0[pl.ds(0, BLOCK), :] += dot(pg, wbuf[b, :, :WIDTH])
             grad[...] += dot(pg, wbuf[b, :, WIDTH : 2 * WIDTH])
-            tap2[pl.ds(EDGE, BLOCK), :] += dot(pg, wbuf[b, :, 2 * WIDTH : CONV])
-            mel_sum[...] += dot(pg, wbuf[b, :, CONV:EXT])
-            for k in range(3):
-                cols = slice(k * WIDTH, (k + 1) * WIDTH)
-                shared[slot, :, cols] = dot_tn(pg, ext[p, :, cols]).astype(BF16)
-            shared[slot, :, CONV:EXT] = dot_tn(pg, ext[p, :, CONV:]).astype(BF16)
+            last_tap = dot(pg, wbuf[b, :, 2 * WIDTH : EXT])
+            tap2[pl.ds(EDGE, BLOCK), :] += last_tap[:, :WIDTH]
+            mel_sum[...] += last_tap[:, WIDTH:]
+            for cols in (slice(0, 6 * ROWS), slice(6 * ROWS, EXT)):
+                shared[slot, :, cols] = dot(pg_t, ext[p, :, cols]).astype(BF16)
             side = dot(low_t[...], gated).astype(BF16)
             shared[slot, :, EXT : EXT + ROWS] = side[: 2 * ROWS]
             shared[slot, :, EXT + ROWS :] = side[2 * ROWS :]
             e = dot(og_rows[...], gated)
             sums_out[pl.ds(pl.multiple_of(l * CH, CH), CH), pl.ds(pl.multiple_of(s * ROWS, ROWS), ROWS)] = e[:CH] + e[CH:]
 
-            @pl.when(j < 2)
+            @pl.when(j % 2 == 0)
             def _():
                 pl.when(q == 0)(lambda: pl.semaphore_wait(phase.at[0], 1))
-                pl.when(i >= 2)(lambda: pl.semaphore_wait(credit.at[j], 1))
-                to_core(i, j).start()
+                pl.when(i >= 2)(lambda: pl.semaphore_wait(credit.at[side_of(j)], 1))
+                to_core(i, side_of(j)).start()
 
             return carry
 
@@ -1030,15 +1041,15 @@
     small_stages += [functools.partial(end_stage, k) for k in range(2)]
 
     if line:
-        stages = [[stage_core]] + line_stages
+        stages = [[]] + line_stages
     else:
-        stages = [[stage_core], [stage_far]]
+        stages = [[], [stage_far]]
         stages += [[functools.partial(stage_rs, k)] for k in range(len(levels))]
         stages += [[functools.partial(stage_ag, n)] for n in range(len(halving) - 1, -1, -1)]
     if line:
-        steps = 2 * LAYERS + max(len(stages), len(small_stages))
+        steps = 2 * LAYERS + max(ACROSS_LAGS[-1] + 2, ALONG_LAGS[-1] + 1, len(small_stages))
     else:
-        steps = 2 * LAYERS + max(2 * len(stages) - 2, len(small_stages))
+        steps = 2 * LAYERS + max(2 * len(stages), len(small_stages))
 
     w_start(0)
 
@@ -1053,22 +1064,30 @@
             @pl.when(h == 1)
             def _():
                 backward_close(i)
-                stage_core(i)
+
+        core_from = v - 1
+        pl.when((core_from >= 0) & (core_from < 2 * LAYERS) & (h == 1))(lambda: far_block(core_from // 2))
+        pl.when((core_from >= 0) & (core_from < 2 * LAYERS) & (h == 0))(lambda: core_block(core_from // 2, me.side))
+
+        if line:
+            pl.when((v >= 1) & (v <= 2 * LAYERS))(lambda: far_r(v - 1).start())
+            pl.when((v >= 2) & (v <= 2 * LAYERS + 1))(lambda: start_q(v - 2))
+        def at_lag(at, count, stage, now=True):
+            pl.when((at >= 0) & (at < count) & now)(lambda: stage(at))
+
+        if line:
+            for name in ORDER.split():
+                k = int(name[1])
+                if name[0] == "q":
+                    at_lag(v - 2 - ACROSS_LAGS[k], 2 * LAYERS, stages[k][0])
+                else:
+                    at_lag(v - 1 - ALONG_LAGS[k], 2 * LAYERS, stages[k][1])
+        else:
+            for lag in range(len(stages) - 1, 0, -1):
+                at_lag((v - 2) // 2 - lag + 1, LAYERS, stages[lag][0], (h == 0) & (v >= 2))
 
         for k, stage in enumerate(small_stages):
             pl.when(v == 2 * LAYERS + k)(stage)
-        if line:
-            pl.when((v >= 1) & (v <= 2 * LAYERS))(lambda: start_ways(v - 1))
-        for lag in range(len(stages) - 1, 0, -1):
-            at = v - 1 - lag if line else i - lag
-            count = 2 * LAYERS if line else LAYERS
-            now = (at >= 0) & (at < count)
-
-            @pl.when(now if line else now & (h == 1))
-            def _():
-                for stage in stages[lag]:
-                    stage(at)
-
         return carry
 
     lax.fori_loop(0, steps, step, 0)
@@ -1250,10 +1269,11 @@
         res_grad[0, : 2 * ROWS] = total[0, :, EXT : EXT + ROWS].astype(F32)
         res_grad[0, 2 * ROWS :] = total[0, :, EXT + ROWS :].astype(F32)
 
-    final = jnp.concatenate([small[s, 16:24, :] for s in range(SHARDS)], axis=1)
-    skip_grad[0] = lax.dot_general(
-        final, mine[pl.ds(pl.multiple_of(l * CH, CH), CH), :], (((0,), (0,)), ((), ())),
-        precision=HIGH, preferred_element_type=F32,
+    final_high, final_low = split(jnp.concatenate([small[s, 16:24, :] for s in range(SHARDS)], axis=1))
+    e_high, e_low = split(mine[pl.ds(pl.multiple_of(l * CH, CH), CH), :])
+    skip_grad[0] = dot_tn(
+        jnp.concatenate([final_high, final_high, final_low, jnp.zeros_like(final_low)], axis=0).astype(BF16),
+        jnp.concatenate([e_high, e_low, e_high, jnp.zeros_like(e_low)], axis=0).astype(BF16),
     )
 
     @pl.when(l == 0)

time: 334 us -> 331 us (level)
  Pallas kernels: 333 us -> 329 us
where the time goes in v5:
time: 331 us; the launch traced here: 330 us
  Pallas kernels  329 us (99%)
    pallas_call x1, Pallas kernels, run_flow(): pl.pallas_call(functools.partial(flow_kernel, levels), out_shape=(jax.Sha...  315 us
    pallas_call x1, Pallas kernels, run_finish(): pl.pallas_call(functools.partial(finish_kernel, crops), grid=(LAYERS,), o...  11.8 us

profile of v5, /device:TPU:0, one launch (start us, length us, event | category | flops | bytes accessed | tf_op | source)
XLA Modules:
  0.0 330.1 jit_solution(8180490807657717499)
XLA Ops:
  1.3 2.1 shard_map.278
  3.5 314.9 %shard_map.279 = (bf16[8,256,1920]{2,1,0:T(8,128)(2,1)}, bf16[8,4,256,1920]{3,2,1,0:T(8,128)(2,1)}, bf16[8,512,1664]{2,1,0:T(8,128)(2,1)}, bf16[8,4,3,512,128]{4...) custom-call(bf16[8,256,1536]{2,1,0:T(8,128)(2,1)} %bitcast.15, ...), custom_call_target="tpu_custom_call" | custom-call | tf_op jit(solution)/shard_map/pallas_call | solution.py:1131
  318.3 11.8 %shard_map.280 = (f32[1,8,2048]{2,1,0:T(8,128)}, f32[1,1]{1,0:T(1,128)}, f32[1,1]{1,0:T(1,128)}, f32[1,8,2048]{2,1,0:T(8,128)}, f32[1,64,80]{2,1,0:T(8,128)}, /*...) custom-call(bf16[8,256,1920]{2,1,0:T(8,128)(2,1)} %get-tuple-element, ...), custom_call_target="tpu_custom_call" | custom-call | tf_op jit(solution)/shard_map/pallas_call | solution.py:1327

commit v6 on v5

--- a/solution.py
+++ b/solution.py
@@ -103,7 +103,7 @@
 ACROSS = pl.ds(0, 6 * ROWS)
 ALONG = pl.ds(6 * ROWS, PACK - 6 * ROWS)
 DEPTH = 8
-ACROSS_LAGS = (0, 1, 3, 3, 4, 5, 7, 20)
+ACROSS_LAGS = (0, 1, 2, 3, 4, 5, 6, 20)
 ALONG_LAGS = (0, 1, 2, 3, 4, 5, 6, 21)
 ORDER = 'q5 r6 q4 r5 q2 q1 r1 r4 r7 q7 q6 r3 q3 r2'
 

time: 331 us -> 330 us (level)
  no operation moved by 1% of the time
where the time goes in v6:
time: 330 us
  Pallas kernels  329 us (100%)
    pallas_call x1, Pallas kernels, run_flow(): pl.pallas_call(functools.partial(flow_kernel, levels), out_shape=(jax.Sha...  315 us
    pallas_call x1, Pallas kernels, run_finish(): pl.pallas_call(functools.partial(finish_kernel, crops), grid=(LAYERS,), o...  11.8 us

profile of v6, /device:TPU:0, one launch (start us, length us, event | category | flops | bytes accessed | tf_op | source)
XLA Modules:
  0.0 329.8 jit_solution(3049530475232265914)
XLA Ops:
  1.3 2.1 shard_map.278
  3.5 314.6 %shard_map.279 = (bf16[8,256,1920]{2,1,0:T(8,128)(2,1)}, bf16[8,4,256,1920]{3,2,1,0:T(8,128)(2,1)}, bf16[8,512,1664]{2,1,0:T(8,128)(2,1)}, bf16[8,4,3,512,128]{4...) custom-call(bf16[8,256,1536]{2,1,0:T(8,128)(2,1)} %bitcast.15, ...), custom_call_target="tpu_custom_call" | custom-call | tf_op jit(solution)/shard_map/pallas_call | solution.py:1131
  318.0 11.8 %shard_map.280 = (f32[1,8,2048]{2,1,0:T(8,128)}, f32[1,1]{1,0:T(1,128)}, f32[1,1]{1,0:T(1,128)}, f32[1,8,2048]{2,1,0:T(8,128)}, f32[1,64,80]{2,1,0:T(8,128)}, /*...) custom-call(bf16[8,256,1920]{2,1,0:T(8,128)(2,1)} %get-tuple-element, ...), custom_call_target="tpu_custom_call" | custom-call | tf_op jit(solution)/shard_map/pallas_call | solution.py:1327
